TPU v7x, 32 devices: a whole 2x2x4 slice. The times are simulated.
32 devices in a mesh: seq: 4 (over z), tp: 8 (over y, x, core).
Axes of the slice: x: 2, y: 2, z: 4, core: 2. Of those that a mesh axis runs over, the one named last changes fastest.
Arguments:
- sequence_in: bfloat16 [1536, 2048], P('tp', 'seq')
- conv_weight: bfloat16 [3, 1536, 3, 1536], P(None, 'tp')
- norm_gain: float32 [3, 1536], P(None, 'tp'), may hold values from 0.1 to 1.9
- tissue_scale: float32 [367, 1536], replicated, may hold values from 0.3 to 3
- donor_offset: int32 [1024], P('seq'), may hold values from 0 to 511
- acceptor_owner: int32 [1024, 1], P('seq'), may hold values from 0 to 3; in each aligned block of 256 rows (0 to 255, 256 to 511, ...) at most 128 rows name the same one
- acceptor_offset: int32 [1024], P('seq'), may hold values from 0 to 511
- tissue: int32 [1024], P('seq'), may hold values from 0 to 366
- tower_grad: float32 [1536, 2048], P('tp', 'seq'), may hold values from -6 to 6
- score_grad: float32 [1024], P('seq'), may hold values from -24 to 24
Outputs:
- scores: float32 [1024], P('seq')
- input_grad: float32 [1536, 2048], P('tp', 'seq')
- weight_grad: float32 [3, 1536, 3, 1536], P(None, 'tp')
- gain_grad: float32 [3, 1536], P(None, 'tp')
Inputs may be any that keep to these rules, and one draw needn't show every extreme that they name: `acceptor_owner`: among the 256 junctions of one index of seq, at most 128 have their acceptor on one index of seq.
All inputs are finite; a program needn't handle non-finite values.
Results may differ from a plain program's by a relative error of at most 0.025.
Values may be sent and summed in bfloat16 or wider, within the bound.
No kernel may reach another device: no remote copies, remote signals or barrier semaphores. Data moves between devices by JAX's collectives and lax.ppermute only.
A program may use at most 128 MiB of HBM per device.

v0:
```python
import math

import jax
import jax.numpy as jnp
from jax import lax
from jax.sharding import PartitionSpec as P

CHANNELS = 1536
LAYERS = 3
CAP = 128


EPSILON = 1e-06


def with_halo(x, sides, width):
    for axis, dim in sides:
        count, length = (lax.axis_size(axis), x.shape[dim])
        up = [(i, (i + 1) % count) for i in range(count - 1)]
        down = [(j, i) for i, j in up]
        last = lax.slice_in_dim(x, length - width, length, axis=dim)
        initial = lax.slice_in_dim(x, 0, width, axis=dim)
        before = lax.ppermute(last, axis, up)
        after = lax.ppermute(initial, axis, down)
        x = jnp.concatenate([before, x, after], axis=dim)
    return x


def gelu_fn(value):
    return jax.nn.gelu(value, approximate=True)


def widen(block, width):
    return with_halo(block, (("seq", 1),), width)


def forward_taps(weights, padded, reach, length):
    total = jnp.zeros((weights.shape[0], length), jnp.float32)
    for tap in range(3):
        total = total + jnp.dot(
            weights[:, tap, :],
            padded[:, tap * reach : tap * reach + length],
            preferred_element_type=jnp.float32,
        )
    return total


def backward_taps(weights, grad_pad, reach, length):
    total = jnp.zeros((weights.shape[2], length), jnp.float32)
    for tap in range(3):
        total = total + lax.dot_general(
            weights[:, tap, :],
            grad_pad[:, (2 - tap) * reach : (2 - tap) * reach + length],
            (((0,), (0,)), ((), ())),
            preferred_element_type=jnp.float32,
        )
    return total


def weight_taps(padded, grad_bf, reach, length):
    blocks = []
    for tap in range(3):
        blocks.append(
            lax.dot_general(
                grad_bf,
                padded[:, tap * reach : tap * reach + length],
                (((1,), (1,)), ((), ())),
                preferred_element_type=jnp.float32,
            )
        )
    return jnp.stack(blocks, axis=1)


def local(
    sequence_in,
    conv_weight,
    norm_gain,
    tissue_scale,
    donor_offset,
    acceptor_owner,
    acceptor_offset,
    tissue,
    tower_grad,
    score_grad,
):
    local_ch = sequence_in.shape[0]
    length = sequence_in.shape[1]
    seq_count = lax.axis_size("seq")
    state = sequence_in
    stored = []
    for layer in range(LAYERS):
        reach = 2 ** (layer + 3)
        stream = state.astype(jnp.float32)
        power = lax.psum(jnp.sum(stream * stream, axis=0), "tp") / CHANNELS
        inverse = 1.0 / jnp.sqrt(power + EPSILON)
        pre_act = stream * inverse[None, :] * norm_gain[layer][:, None]
        hidden = gelu_fn(pre_act).astype(jnp.bfloat16)
        padded = widen(hidden, reach)
        weights = conv_weight[layer]
        gathered = padded

        def fold_inputs(total, piece, start, weights=weights, reach=reach):
            return forward_taps(weights, piece, reach, length)

        mixed = fold_inputs(
            jnp.zeros((local_ch, length), jnp.float32),
            lax.all_gather(padded, "tp", axis=0, tiled=True),
            jnp.int32(0),
        )
        stored.append((state, inverse, pre_act, gathered))
        state = (stream + mixed).astype(jnp.bfloat16)
    owner = acceptor_owner[:, 0]
    member = (owner[:, None] == jnp.arange(seq_count, dtype=jnp.int32)[None, :]).astype(jnp.int32)
    slot = jnp.sum(jnp.cumsum(member, axis=0) * member, axis=1) - 1
    requests = jnp.zeros((seq_count, CAP), jnp.int32).at[owner, slot].set(acceptor_offset)
    rows_view = state.T
    offsets = lax.all_to_all(requests, "seq", split_axis=0, concat_axis=0, tiled=True)
    picked = rows_view[offsets]
    returned = lax.all_to_all(picked, "seq", split_axis=0, concat_axis=0, tiled=True)
    accept_cols = returned[owner, slot].astype(jnp.float32)
    donor_cols = rows_view[donor_offset].astype(jnp.float32)
    chan_start = lax.axis_index("tp") * local_ch
    local_table = lax.dynamic_slice_in_dim(tissue_scale, chan_start, local_ch, 1)
    tissue_hit = (
        tissue[:, None] == jnp.arange(tissue_scale.shape[0], dtype=jnp.int32)[None, :]
    ).astype(jnp.float32)
    tissue_rows = jnp.dot(tissue_hit, local_table, precision=lax.Precision.HIGHEST)
    root = math.sqrt(CHANNELS)
    partial_scores = jnp.sum(donor_cols * accept_cols * tissue_rows, axis=1) / root
    scores = lax.psum(partial_scores, "tp")
    weight_j = score_grad / root
    donor_back = weight_j[:, None] * accept_cols * tissue_rows
    accept_back = weight_j[:, None] * donor_cols * tissue_rows
    outgoing = jnp.zeros((seq_count, CAP, local_ch), jnp.float32).at[owner, slot].set(accept_back)
    incoming = lax.all_to_all(
        outgoing.astype(jnp.bfloat16), "seq", split_axis=0, concat_axis=0, tiled=True
    ).astype(outgoing.dtype)
    upstream = tower_grad.at[:, donor_offset].add(donor_back.T)
    upstream = upstream.at[:, offsets.reshape(-1)].add(incoming.reshape(-1, local_ch).T)
    weight_list = [None] * LAYERS
    gain_list = [None] * LAYERS
    for layer in reversed(range(LAYERS)):
        reach = 2 ** (layer + 3)
        old_state, inverse, pre_act, gathered = stored[layer]
        stream = old_state.astype(jnp.float32)
        grad_bf = upstream.astype(jnp.bfloat16)
        grad_pad = widen(grad_bf, reach)
        weights = conv_weight[layer]

        def term_rows(start, count, weights=weights, grad_pad=grad_pad, reach=reach):
            return backward_taps(weights, grad_pad, reach, length)

        back_hidden = lax.psum_scatter(
            term_rows(jnp.int32(0), local_ch * lax.axis_size("tp")).astype(jnp.bfloat16),
            "tp",
            scatter_dimension=0,
            tiled=True,
        ).astype(jnp.float32)

        def fold_weights(total, piece, start, grad_bf=grad_bf, reach=reach):
            return weight_taps(piece, grad_bf, reach, length)

        weight_term = fold_weights(
            jnp.zeros((local_ch, 3, CHANNELS), jnp.float32),
            lax.all_gather(gathered, "tp", axis=0, tiled=True),
            jnp.int32(0),
        )
        weight_list[layer] = lax.psum(weight_term.astype(jnp.bfloat16), "seq").astype(jnp.float32)
        _, gelu_back = jax.vjp(gelu_fn, pre_act)
        back_pre = gelu_back(back_hidden)[0]
        gain_list[layer] = jnp.sum(back_pre * stream * inverse[None, :], axis=1)
        back_norm = back_pre * norm_gain[layer][:, None]
        inner = lax.psum(jnp.sum(back_norm * stream, axis=0), "tp")
        upstream = (
            upstream
            + inverse[None, :] * back_norm
            - stream * (inverse**3)[None, :] * inner[None, :] / CHANNELS
        )
    gain_grad = lax.psum(jnp.stack(gain_list), "seq")
    return (scores, upstream, jnp.stack(weight_list), gain_grad)


def solution(mesh):
    return jax.shard_map(
        local,
        mesh=mesh,
        in_specs=(
            P("tp", "seq"),
            P(None, "tp", None, None),
            P(None, "tp"),
            P(),
            P("seq"),
            P("seq", None),
            P("seq"),
            P("seq"),
            P("tp", "seq"),
            P("seq"),
        ),
        out_specs=(P("seq"), P("tp", "seq"), P(None, "tp", None, None), P(None, "tp")),
        check_vma=False,
    )
```

profile of v0, /device:TPU:0, one launch (start us, length us, event | category | flops | bytes accessed | tf_op | source)
XLA Modules:
  0.0 647.3 jit_solution(17721434171829143058)
XLA Ops:
  8.4 15.1 %psum.77 = f32[512]{0:T(512)S(1)} all-reduce(f32[512]{0:T(512)S(1)} %fusion.132), channel_id=1, replica_groups=mesh['seq'=4,'tp'=8] {'tp'}, use_global_device_ids=true, to_apply=%region_1.0 | all-reduce | flops 512 | bytes 4096 | tf_op jit(solution)/shard_map/psum | solution.py:94
  25.5 3.5 collective-permute-start
  30.8 4.3 collective-permute-done.1
  35.9 5.1 slice_bitcast_fusion
  41.0 20.7 %all-gather.4.cloned.1.call-done = bf16[1536,528]{1,0:T(8,128)(2,1)} async-done(((bf16[192,528]{1,0:T(8,128)(2,1)}), bf16[1536,528]{1,0:T(8,128)(2,1)}) %all-gather.4.cloned.1.call-update) | async-done | bytes 1622032 | tf_op jit(solution)/shard_map/all_gather | solution.py:107
  61.7 2.6 fusion.37
  64.3 2.4 fusion.40
  67.3 13.1 %psum.78 = f32[512]{0:T(512)S(1)} all-reduce(f32[512]{0:T(512)S(1)} %get-tuple-element.50), channel_id=1, replica_groups=mesh['seq'=4,'tp'=8] {'tp'}, use_global_device_ids=true, to_apply=%region_3.0 | all-reduce | flops 512 | bytes 4096 | tf_op jit(solution)/shard_map/psum | solution.py:94
  81.3 3.4 collective-permute-start.2
  86.5 4.3 collective-permute-done.3
  91.6 26.5 %all-gather.6.cloned.1.call-done = bf16[1536,544]{1,0:T(8,128)(2,1)} async-done(((bf16[192,544]{1,0:T(8,128)(2,1)}), bf16[1536,544]{1,0:T(8,128)(2,1)}) %all-gather.6.cloned.1.call-update) | async-done | bytes 1671184 | tf_op jit(solution)/shard_map/all_gather | solution.py:107
  118.2 2.6 fusion.28
  120.8 2.4 fusion.31
  123.7 13.1 %psum.79 = f32[512]{0:T(512)S(1)} all-reduce(f32[512]{0:T(512)S(1)} %get-tuple-element.52), channel_id=1, replica_groups=mesh['seq'=4,'tp'=8] {'tp'}, use_global_device_ids=true, to_apply=%region_5.0 | all-reduce | flops 512 | bytes 4096 | tf_op jit(solution)/shard_map/psum | solution.py:94
  137.8 3.4 collective-permute-start.4
  142.9 4.3 collective-permute-done.5
  150.3 38.6 %scatter_fusion = s32[4,128]{1,0:T(4,128)} fusion(s32[4,128]{1,0:T(4,128)} %broadcast.150, s32[256]{0:T(256)S(1)} %bitcast.154, s32[256]{0:T(256)S(1)} %copy-done.18), kind=kCustom, calls=%fused_computation.3 | custom fusion | bytes 5120 | tf_op jit(solution)/shard_map/scatter | solution.py:115
  188.9 3.7 all-to-all-start
  192.6 5.4 all-to-all-done
  198.0 2.6 fusion.19
  200.6 2.4 fusion.22
  205.2 2.6 gather_fusion.1
  207.8 1.8 copy.105
  209.6 4.2 all-to-all-start.1
  215.0 1.8 gather_fusion
  216.8 1.7 copy.100
  221.0 2.3 gather_fusion.2
  224.3 2.3 fusion.146
  227.8 13.2 %scatter_fusion.2 = f32[4,128,192]{2,1,0:T(8,128)S(1)} fusion(f32[4,128,192]{2,1,0:T(8,128)S(1)} %broadcast_in_dim.5, s32[256]{0:T(256)S(1)} %bitcast.155, f32[256,192]{1,0:T(8,128)S(1)} %copy.110), kind=kCustom, calls=%fused_computation.5 | custom fusion | bytes 591872 | tf_op jit(solution)/shard_map/scatter | solution.py:134
  241.8 3.5 all-to-all-start.2
  245.7 2.2 scatter_fusion.1
  247.9 3.7 all-to-all-done.2
  251.7 4.0 scatter_fusion.3
  255.8 3.3 collective-permute-start.7
  259.1 1.7 fusion.103
  262.9 3.6 collective-permute-done.6
  266.5 1.8 fusion.8
  268.6 36.3 %reduce-scatter.4.cloned.1.call-done = bf16[192,512]{1,0:T(8,128)(2,1)} async-done(((bf16[1536,512]{1,0:T(8,128)(2,1)}), bf16[192,512]{1,0:T(8,128)(2,1)}) %reduce-scatter.4.cloned.1.call-update) | async-done | bytes 196624 | tf_op jit(solution)/shard_map/reduce_scatter | solution.py:153
  306.4 12.7 %psum.81 = f32[512]{0:T(512)S(1)} all-reduce(f32[512]{0:T(512)S(1)} %get-tuple-element.7), channel_id=1, replica_groups=mesh['seq'=4,'tp'=8] {'tp'}, use_global_device_ids=true, to_apply=%region_17.18 | all-reduce | flops 512 | bytes 4096 | tf_op jit(solution)/shard_map/psum | solution.py:173
  319.1 2.1 fusion.167
  321.3 3.5 collective-permute-start.9
  324.8 1.7 fusion.101
  326.5 1.5 collective-permute-start.8
  328.8 3.7 collective-permute-done.8
  332.5 1.9 fusion.7
  334.5 3.5 fusion.16
  338.0 3.1 fusion.15
  341.1 31.1 %reduce-scatter.6.cloned.1.call-done = bf16[192,512]{1,0:T(8,128)(2,1)} async-done(((bf16[1536,512]{1,0:T(8,128)(2,1)}), bf16[192,512]{1,0:T(8,128)(2,1)}) %reduce-scatter.6.cloned.1.call-update) | async-done | bytes 196624 | tf_op jit(solution)/shard_map/reduce_scatter | solution.py:153
  372.2 1.5 multiply_reduce_fusion.1
  373.7 12.7 %psum.82 = f32[512]{0:T(512)S(1)} all-reduce(f32[512]{0:T(512)S(1)} %get-tuple-element.5), channel_id=1, replica_groups=mesh['seq'=4,'tp'=8] {'tp'}, use_global_device_ids=true, to_apply=%region_20.21 | all-reduce | flops 512 | bytes 4096 | tf_op jit(solution)/shard_map/psum | solution.py:173
  386.4 1.5 fusion.166
  388.0 3.4 collective-permute-start.11
  394.1 3.9 collective-permute-done.10
  398.0 1.9 fusion.6
  400.1 2.6 fusion.17
  402.7 2.8 maximum_bitcast_fusion.2
  412.5 1.5 maximum_bitcast_fusion
  414.0 23.7 %reduce-scatter.8.cloned.1.call-done = bf16[192,512]{1,0:T(8,128)(2,1)} async-done(((bf16[1536,512]{1,0:T(8,128)(2,1)}), bf16[192,512]{1,0:T(8,128)(2,1)}) %reduce-scatter.8.cloned.1.call-update) | async-done | bytes 196624 | tf_op jit(solution)/shard_map/reduce_scatter | solution.py:153
  437.7 1.5 fusion.141
  439.1 13.2 %all-reduce = (f32[256]{0:T(256)}, f32[512]{0:T(512)S(1)}) all-reduce(f32[256]{0:T(256)S(1)} %broadcast_multiply_fusion.1, f32[512]{0:T(512)S(1)} %get-tuple-element.9), channel_id=1, replica_groups=mesh['seq'=4,'tp'=8] {'tp'}, use_global_device_ids=true, to_apply=%region_11.12 | all-reduce | flops 768 | bytes 6144 | tf_op jit(solution)/shard_map/psum | solution.py:130
  452.4 13.0 %psum.87 = f32[3,192]{1,0:T(4,128)} all-reduce(f32[3,192]{1,0:T(4,128)S(1)} %pad_maximum_fusion.15), channel_id=1, replica_groups=mesh['seq'=4,'tp'=8] {'seq'}, use_global_device_ids=true, to_apply=%region_30.31 | all-reduce | flops 576 | bytes 4608 | tf_op jit(solution)/shard_map/psum | solution.py:179
  465.4 2.1 fusion.138
  467.6 165.2 %all-reduce.4.cloned.1.call-done = (bf16[1,192,3,1536]{3,1,2,0:T(8,128)(2,1)}, bf16[1,192,3,1536]{3,1,2,0:T(8,128)(2,1)}, bf16[1,192,3,1536]{3,1,2,0:T(8,128)(2,1)}) async-done(((bf16[1,192,3,1536]{3,1,2,0:T(8,128)(2,1)}, bf16[1,192,3,1536]{3,1,2,0:T(8,128)(2,1)}, bf16[1,192,3,1536]{3,1,2,0:T(8,128)(2,1)}), (bf16[1,192,3,1536]{3,1,2,0:T(8,128)(2,1)}, bf16[1,192,3,1536]{3,1,2,0:T(8,128)(2,1)}, ...) | async-done | bytes 5308432 | tf_op jit(solution)/shard_map/psum | solution.py:168
  632.8 7.6 %maximum_convert_fusion = f32[3,192,3,1536]{3,1,2,0:T(8,128)} fusion(bf16[1,192,3,1536]{3,1,2,0:T(8,128)(2,1)} %get-tuple-element.12, bf16[1,192,3,1536]{3,1,2,0:T(8,128)(2,1)} %get-tuple-element.13, bf16[1,192,3,1536]{3,1,2,0:T(8,128)(2,1)} %get-tuple-element.14), kind=kLoop, calls=%fused_computation.7 | loop fusion | flops 7962624 | bytes 15925248 | tf_op jit(solution)/shard_map/stack | solution.py:180
  (134 shorter events, 40.0 us)
Async XLA Ops:
  7.2 217.1 %copy-start = (f32[367,1536]{1,0:T(8,128)S(1)}, f32[367,1536]{1,0:T(8,128)}, u32[]{:S(2)}) copy-start(f32[367,1536]{1,0:T(8,128)} %param.13) | copy-start | bytes 6764548
  7.2 54.6 %all-gather.4.cloned.1.call-start = ((), (), s32[]{:S(2)}) async-start(), calls=%async_computation.6 | async-start | bytes 2211840 | tf_op jit(solution)/shard_map/all_gather | solution.py:107
  25.5 5.2 collective-permute-start
  29.0 6.0 collective-permute-start.1
  35.9 82.3 %all-gather.6.cloned.1.call-start = ((), (), s32[]{:S(2)}) async-start(), calls=%async_computation.7 | async-start | bytes 2211840 | tf_op jit(solution)/shard_map/all_gather | solution.py:107
  61.7 2.6 copy-start.6
  64.3 2.4 copy-start.8
  64.3 2.4 copy-start.20
  81.3 5.1 collective-permute-start.2
  84.7 6.0 collective-permute-start.3
  91.6 106.4 %all-gather.8.cloned.1.call-start = ((), (), s32[]{:S(2)}) async-start(), calls=%async_computation.8 | async-start | bytes 2211840 | tf_op jit(solution)/shard_map/all_gather | solution.py:107
  118.2 2.6 copy-start.2
  120.8 2.4 copy-start.10
  123.2 24.8 %copy-start.14 = (s32[256,1]{0,1:T(1,128)S(1)}, s32[256,1]{0,1:T(1,128)}, u32[]{:S(2)}) copy-start(s32[256,1]{0,1:T(1,128)} %param.15) | copy-start | bytes 3076
  123.2 27.1 %copy-start.18 = (s32[256]{0:T(256)S(1)}, s32[256]{0:T(256)}, u32[]{:S(2)}) copy-start(s32[256]{0:T(256)} %param.16) | copy-start | bytes 3076
  137.7 54.9 %copy-start.19 = (s32[256]{0:T(256)S(1)}, s32[256]{0:T(256)}, u32[]{:S(2)}) copy-start(s32[256]{0:T(256)} %param.14) | copy-start | bytes 3076
  137.8 5.1 collective-permute-start.4
  141.2 6.0 collective-permute-start.5
  188.9 9.1 %all-to-all-start = ((s32[4,1,128]{2,1,0:T(1,128)}), s32[4,1,128]{2,1,0:T(1,128)S(1)}, u32[]{:S(2)}, u32[]{:S(2)}) async-start(s32[4,1,128]{2,1,0:T(1,128)} %bitcast.27), calls=%async_computation | async-start | bytes 4096 | tf_op jit(solution)/shard_map/all_to_all | solution.py:117
  198.0 2.6 copy-start.4
  200.6 2.4 copy-start.9
  209.6 10.3 %all-to-all-start.1 = ((bf16[4,128,192]{1,2,0:T(8,128)(2,1)}), bf16[4,128,192]{1,2,0:T(8,128)(2,1)}, u32[]{:S(2)}, u32[]{:S(2)}) async-start(bf16[4,128,192]{1,2,0:T(8,128)(2,1)} %copy.105), calls=%async_computation.1 | async-start | bytes 393216 | tf_op jit(solution)/shard_map/all_to_all | solution.py:119
  216.8 7.5 %copy-start.17 = (f32[256]{0:T(256)S(1)}, f32[256]{0:T(256)}, u32[]{:S(2)}) copy-start(f32[256]{0:T(256)} %broadcast_multiply_fusion) | copy-start | bytes 3076
  227.8 17.5 %copy-start.13 = (f32[192,512]{1,0:T(8,128)S(1)}, f32[192,512]{1,0:T(8,128)}, u32[]{:S(2)}) copy-start(f32[192,512]{1,0:T(8,128)} %param.18) | copy-start | bytes 1179652
  241.0 4.5 copy-start.12
  241.8 9.7 %all-to-all-start.2 = ((bf16[4,128,192]{1,2,0:T(8,128)(2,1)}), bf16[4,128,192]{1,2,0:T(8,128)(2,1)S(1)}, u32[]{:S(2)}, u32[]{:S(2)}) async-start(bf16[4,128,192]{1,2,0:T(8,128)(2,1)} %copy.111), calls=%async_computation.2 | async-start | bytes 393216 | tf_op jit(solution)/shard_map/all_to_all | solution.py:135
  245.3 59.6 %reduce-scatter.4.cloned.1.call-start = ((), (), s32[]{:S(2)}) async-start(), calls=%async_computation.9 | async-start | bytes 1769472 | tf_op jit(solution)/shard_map/reduce_scatter | solution.py:153
  255.8 6.4 copy-start.5
  255.8 6.4 collective-permute-start.7
  260.9 5.6 collective-permute-start.6
  268.3 50.7 %copy-start.16 = (f32[512]{0:T(512)S(1)}, f32[512]{0:T(512)}, u32[]{:S(2)}) copy-start(f32[512]{0:T(512)} %get-tuple-element.46) | copy-start | bytes 6148
  268.3 103.9 %reduce-scatter.6.cloned.1.call-start = ((), (), s32[]{:S(2)}) async-start(), calls=%async_computation.10 | async-start | bytes 1769472 | tf_op jit(solution)/shard_map/reduce_scatter | solution.py:153
  321.3 6.8 %copy-start.3 = (bf16[192,3,1536]{2,0,1:T(8,128)(2,1)S(1)}, bf16[192,3,1536]{2,0,1:T(8,128)(2,1)}, u32[]{:S(2)}) copy-start(bf16[192,3,1536]{2,0,1:T(8,128)(2,1)} %get-tuple-element.23) | copy-start | bytes 5308420
  321.3 6.8 %collective-permute-start.9 = (bf16[192,16]{1,0:T(8,128)(2,1)S(1)}, bf16[192,16]{1,0:T(8,128)(2,1)S(1)}, u32[]{:S(2)}, u32[]{:S(2)}) collective-permute-start(bf16[192,16]{1,0:T(8,128)(2,1)S(1)} %get-tuple-element.32), channel_id=1, source_target_pairs={{0,8},{8,16},{16,24},{1,9},{9,17},{17,25},{2,10},{10,18},{18,26},{... | collective-permute-start | bytes 18440 | tf_op jit(solution)/shard_map/ppermute | solution.py:23
  326.5 6.0 collective-permute-start.8
  334.5 103.2 %reduce-scatter.8.cloned.1.call-start = ((), (), s32[]{:S(2)}) async-start(), calls=%async_computation.11 | async-start | bytes 1769472 | tf_op jit(solution)/shard_map/reduce_scatter | solution.py:153
  338.0 48.4 %copy-start.15 = (f32[512]{0:T(512)S(1)}, f32[512]{0:T(512)}, u32[]{:S(2)}) copy-start(f32[512]{0:T(512)} %get-tuple-element.44) | copy-start | bytes 6148
  341.1 50.3 %copy-start.7 = (bf16[192,3,1536]{2,0,1:T(8,128)(2,1)S(1)}, bf16[192,3,1536]{2,0,1:T(8,128)(2,1)}, u32[]{:S(2)}) copy-start(bf16[192,3,1536]{2,0,1:T(8,128)(2,1)} %get-tuple-element.22) | copy-start | bytes 5308420
  388.0 5.4 collective-permute-start.11
  392.0 6.0 collective-permute-start.10
  400.0 232.8 %all-reduce.4.cloned.1.call-start = ((), (), s32[]{:S(2)}) async-start(), calls=%async_computation.12 | async-start | bytes 10616832 | tf_op jit(solution)/shard_map/psum | solution.py:168
  402.7 2.8 copy-start.11
  407.8 2.3 copy-start.21
  632.8 7.6 %copy-start.1 = (f32[367,1536]{1,0:T(8,128)S(1)}, f32[367,1536]{1,0:T(8,128)}, u32[]{:S(2)}) copy-start(f32[367,1536]{1,0:T(8,128)} %param.13) | copy-start | bytes 6764548
Sparse Core Ops, SparseCore 0:
  36.0 25.6 all-gather.3
  91.7 26.4 all-gather.5
  148.1 26.4 all-gather.7
  268.5 36.4 reduce-scatter.3
  334.6 37.5 reduce-scatter.5
  400.1 37.4 reduce-scatter.7
  440.8 191.9 all-reduce.3
where the time goes:
time: 649 us; the launch traced here: 647 us
  waiting for transfers between devices  339 us (52%)
  blocking collectives  93 us (14%)
  local copies, waits for them, and re-layouts  75.8 us (12%)
  matrix products  45.3 us (7%)
  starting transfers between devices  40.1 us (6%)
  other arithmetic  38.8 us (6%)
  between operations  14.8 us (2%)
    psum x1, waiting for transfers between devices, local(): lax.psum(weight_term.astype(jnp.bfloat16), 'seq').astype(jnp.float32)  165 us
    reduce_scatter x3, waiting for transfers between devices, local(): lax.psum_scatter(term_rows(jnp.int32(0), local_ch * lax.axis_size('tp'))....  91.1 us
    all_gather x3, waiting for transfers between devices, local(): lax.all_gather(padded, 'tp', axis=0, tiled=True)  47.3 us
    psum x3, blocking collectives, local(): power = lax.psum(jnp.sum(stream * stream, axis=0), 'tp') / CHANNELS  41.3 us
    scatter x1, local copies, waits for them, and re-layouts, local(): jnp.zeros((seq_count, CAP), jnp.int32).at[owner, slot].set(acceptor_offset)  38.6 us
    psum x2, blocking collectives, local(): inner = lax.psum(jnp.sum(back_norm * stream, axis=0), 'tp')  25.4 us
    ppermute x6, waiting for transfers between devices, with_halo(): after = lax.ppermute(initial, axis, down)  24 us
    ppermute x6, starting transfers between devices, with_halo(): before = lax.ppermute(last, axis, up)  20.5 us
  transfers between devices with their start and end apart: 22, of which 18 were waited for; matrix products, arithmetic and copies ran while one was open for 13% of the time, Pallas kernels for 0%

commit v1 on v0

v1 whole, which is shorter than its diff:
```python
import functools
import math

import jax
import jax.numpy as jnp
from jax import lax
from jax.experimental import pallas as pl
from jax.experimental.pallas import tpu as pltpu
from jax.sharding import PartitionSpec as P

LAYERS = 3
EPSILON = 1e-06
EDGE = 64
CHUNK = 384
ROWS = 16
K0 = math.sqrt(2.0 / math.pi)
K1 = K0 * 0.044715
F32 = jnp.float32
BF16 = jnp.bfloat16

VMEM = pl.BlockSpec(memory_space=pltpu.VMEM)
SMEM = pl.BlockSpec(memory_space=pltpu.SMEM)
HBM = pl.BlockSpec(memory_space=pl.ANY)


def params(**kw):
    return pltpu.CompilerParams(vmem_limit_bytes=40 * 1024 * 1024, **kw)


def reach_of(layer):
    return 2 ** (layer + 3)


def swap(x, axis, mask):
    count = lax.axis_size(axis)
    return lax.ppermute(x, axis, [(i, i ^ mask) for i in range(count)])


def gather_tp(x):
    if lax.axis_size("tp") == 8:
        far = [x] + [swap(x, "tp", m) for m in (2, 4, 6)]
        near = [swap(v, "tp", 1) for v in far]
        return [v for pair in zip(far, near) for v in pair]
    whole = lax.all_gather(x, "tp", axis=0)
    return [whole[i] for i in range(whole.shape[0])]


def tp_order(me):
    count = lax.axis_size("tp")
    steps = jnp.arange(count, dtype=jnp.int32)
    return me ^ steps if count == 8 else steps


def gather_seq(x):
    if lax.axis_size("seq") == 4:
        one = swap(x, "seq", 1)
        two = swap(x, "seq", 2)
        return [x, one, two, swap(x, "seq", 3)]
    whole = lax.all_gather(x, "seq", axis=0)
    return [whole[i] for i in range(whole.shape[0])]


def seq_order(me):
    count = lax.axis_size("seq")
    steps = jnp.arange(count, dtype=jnp.int32)
    return me ^ steps if count == 4 else steps


def roll(x, shift):
    width = x.shape[1]
    shift = shift % width
    return x if shift == 0 else pltpu.roll(x, shift, 1)


def own_part(x, length):
    return roll(x, -EDGE)[:, :length]


def in_sequence(seq_at, width, length, total):
    at = lax.broadcasted_iota(jnp.int32, (1, width), 1) + (seq_at * length - EDGE)
    return (at >= 0) & (at < total)


def prep_kernel(meta, seq_ref, tower_ref, first_ref, second_ref, gain_ref, state_ref, window_ref, *, n_tp, n_seq):
    ch, length = seq_ref.shape
    seq_at = meta[n_tp + n_seq + 1]
    even = lax.rem(seq_at, 2) == 0
    first = first_ref[...].astype(F32)
    second = second_ref[...].astype(F32)
    right = jnp.where(even, first, second)
    left = jnp.where(even, second, first)
    lane = lax.broadcasted_iota(jnp.int32, (ch, 128), 1)
    low = lane < EDGE
    rt, lt = right[:, :128], left[:, :128]
    edge = jnp.where(low, rt, roll(lt, EDGE))
    state = jnp.concatenate([seq_ref[...].astype(F32), edge], axis=1)
    state = roll(state, EDGE)
    gains = gain_ref[...]
    high = gains.astype(BF16).astype(F32)
    rest = gains - high
    middle = rest.astype(BF16).astype(F32)
    last = (rest - middle).astype(BF16).astype(F32)
    width = length + 2 * EDGE
    wide = lax.broadcasted_iota(jnp.int32, (ch, width), 1)
    for layer in range(LAYERS):
        state = jnp.where(wide == layer, high[:, layer : layer + 1], state)
        state = jnp.where(wide == LAYERS + layer, middle[:, layer : layer + 1], state)
        state = jnp.where(wide == width - 8 + layer, last[:, layer : layer + 1], state)
    state_ref[...] = state.astype(BF16)
    th = jnp.where(low, roll(rt, EDGE), lt)
    tl = jnp.where(low, right[:, 128:], roll(left[:, 128:], EDGE))
    window_ref[...] = roll(jnp.concatenate([tower_ref[...], th + tl], axis=1), EDGE)


def lookup_kernel(meta, table_ref, *refs, n_tp, n_seq):
    pieces = refs[:n_seq]
    rec_ref, rows_ref = refs[n_seq:]
    count = pieces[0].shape[1]
    for m in range(n_seq):
        at = meta[n_tp + m]
        rec_ref[:, pl.ds(pl.multiple_of(at * count, 128), count)] = pieces[m][...]
    table = table_ref[...]
    ch, tissues = table.shape
    high = table.astype(BF16)
    rest = table - high.astype(F32)
    middle = rest.astype(BF16)
    last = (rest - middle.astype(F32)).astype(BF16)
    stack = jnp.concatenate([high, middle, last], axis=0)
    which = rec_ref[2:3, :].astype(jnp.int32)
    hit = lax.broadcasted_iota(jnp.int32, (tissues, which.shape[1]), 0) == which
    got = jnp.dot(stack, jnp.where(hit, 1.0, 0.0).astype(BF16), preferred_element_type=F32)
    rows_ref[...] = got[:ch] + (got[ch : 2 * ch] + got[2 * ch :])


def forward_kernel(meta, w_ref, own_ref, *refs, layer, n_tp, n_seq, length):
    pieces, refs = refs[:n_tp], refs[n_tp:]
    if layer == 0:
        state_ref, hidden_ref, slope_ref, inverse_ref, gain_ref, held, weights, sem = refs
    else:
        gain_ref, state_ref, hidden_ref, slope_ref, inverse_ref, held, weights, sem = refs
    ch, width = pieces[0].shape
    channels = ch * n_tp
    reach = reach_of(layer)
    me, seq_at = meta[n_tp + n_seq], meta[n_tp + n_seq + 1]
    copy = pltpu.make_async_copy(w_ref.at[layer], weights, sem)
    copy.start()

    def add_power(j, acc):
        rows = pl.ds(pl.multiple_of(j * ROWS, ROWS), ROWS)
        for piece in pieces:
            x = piece[rows, :].astype(F32)
            sq = x * x
            for i in range(0, ROWS, 8):
                acc = acc + sq[i : i + 8]
        return acc

    acc = lax.fori_loop(0, ch // ROWS, add_power, jnp.zeros((8, width), F32))
    power = jnp.sum(acc, axis=0, keepdims=True) / channels
    inverse = 1.0 / jnp.sqrt(power + EPSILON)
    inverse_ref[...] = jnp.broadcast_to(inverse, (8, width))

    def activate(j, carry):
        rows = pl.ds(pl.multiple_of(j * ROWS, ROWS), ROWS)
        for m, piece in enumerate(pieces):
            at = meta[m]
            x = piece[rows, :].astype(F32)
            if layer == 0:
                front, back = x[:, :128], x[:, width - 128 :]
                cols = [
                    front[:, l : l + 1] + (front[:, LAYERS + l : LAYERS + l + 1] + back[:, 120 + l : 121 + l])
                    for l in range(LAYERS)
                ]
                lane = lax.broadcasted_iota(jnp.int32, (ROWS, 128), 1)
                gain_ref[at, rows, :] = jnp.where(lane == 0, cols[0], jnp.where(lane == 1, cols[1], cols[2]))
                gain = cols[0]
            else:
                gain = gain_ref[at, rows, layer : layer + 1]
            scaled = x * gain
            pre = scaled * inverse
            sq = pre * pre
            th = jnp.tanh(pre * (K0 + K1 * sq))
            half = 0.5 + 0.5 * th
            hidden = pre * half
            held[at, rows, :] = hidden.astype(BF16)
            slope = half + (hidden - hidden * th) * (K0 + (3.0 * K1) * sq)
            slope_ref[at, rows, :] = (slope * scaled).astype(BF16)
        return carry

    lax.fori_loop(0, ch // ROWS, activate, 0)
    hidden_ref[...] = own_part(held[me].astype(F32), length).astype(BF16)
    copy.wait()
    every = held[...].reshape(channels, width)
    total = own_ref[...].astype(F32)
    for tap in range(3):
        part = jnp.dot(weights[tap * ch : (tap + 1) * ch, :], every, preferred_element_type=F32)
        total = total + roll(part, (1 - tap) * reach)
    total = jnp.where(in_sequence(seq_at, width, length, n_seq * length), total, 0.0).astype(BF16)
    if layer == LAYERS - 1:
        state_ref[...] = own_part(total.astype(F32), length).astype(BF16)
    else:
        state_ref[...] = total


def send_back(layer, upstream, meta, weights, slope_ref, taps, grad_ref, out_refs, score, n_tp, n_seq, length):
    ch, width = upstream.shape
    reach = reach_of(layer)
    me, seq_at = meta[n_tp + n_seq], meta[n_tp + n_seq + 1]
    grad = jnp.where(in_sequence(seq_at, width, length, n_seq * length), upstream, 0.0)
    grad = grad.astype(BF16).astype(F32)
    grad_ref[...] = own_part(grad, length).astype(BF16)
    for tap in range(3):
        taps[tap * ch : (tap + 1) * ch, :] = roll(grad, (tap - 1) * reach).astype(BF16)
    inner = jnp.zeros((8, width), F32)
    parts = CHUNK // ch
    chunks = ch * n_tp // CHUNK
    for r in range(chunks):
        at = (me // 2) ^ r if n_tp == 8 else r
        cols = pl.ds(pl.multiple_of(at * CHUNK, 128), CHUNK)
        part = lax.dot_general(
            weights[:, cols], taps[...], (((0,), (0,)), ((), ())), preferred_element_type=F32
        )
        for q in range(parts):
            prod = part[q * ch : (q + 1) * ch] * slope_ref[at * parts + q].astype(F32)
            inner = inner + jnp.sum(prod.reshape(ch // 8, 8, width), axis=0)
        if n_tp == 8:
            keep_ref, send_ref = out_refs
            zero = lax.rem(me, 2) == 0
            keep_ref[r] = jnp.where(zero, part[:ch], part[ch:]).astype(BF16)
            send_ref[r * ch : (r + 1) * ch, :] = jnp.where(zero, part[ch:], part[:ch]).astype(BF16)
        else:
            for q in range(parts):
                out_refs[0][at * parts + q] = part[q * ch : (q + 1) * ch].astype(BF16)
    row = lax.broadcasted_iota(jnp.int32, (8, width), 0)
    extra = jnp.where(row == 0, jnp.sum(inner, axis=0, keepdims=True), 0.0)
    if score is not None:
        score = jnp.concatenate([score, jnp.zeros((1, width - score.shape[1]), F32)], axis=1)
        extra = jnp.where(row == 1, score, extra)
    if n_tp == 8:
        out_refs[1][n_tp // 2 * ch :, :] = split_rows(extra)
    else:
        out_refs[1][...] = extra


def split_rows(x):
    high = x.astype(BF16).astype(F32)
    return jnp.concatenate([high, x - high], axis=0).astype(BF16)


def join_rows(x):
    x = x.astype(F32)
    return x[:8] + x[8:]


def junction_kernel(meta, w_ref, window_ref, rec_ref, rows_ref, slope_ref, *refs, n_tp, n_seq, root):
    pieces, refs = refs[:n_seq], refs[n_seq:]
    up_ref, grad_ref, *refs = refs
    *out_refs, weights, taps, donors, sem = refs
    ch, length = pieces[0].shape
    width = window_ref.shape[1]
    count = rec_ref.shape[1]
    share = count // n_seq
    me, seq_at = meta[n_tp + n_seq], meta[n_tp + n_seq + 1]
    copy = pltpu.make_async_copy(w_ref.at[LAYERS - 1], weights, sem)
    copy.start()
    donor = rec_ref[0:1, :].astype(jnp.int32)
    accept = rec_ref[1:2, :].astype(jnp.int32)
    weight = rec_ref[3:4, :] / root
    place = lax.broadcasted_iota(jnp.int32, (length, count), 0)
    accepts = jnp.zeros((ch, count), F32)
    for m in range(n_seq):
        at = meta[n_tp + m]
        cols = pl.ds(pl.multiple_of(at * share, 128), share)
        block = pieces[m][...]
        mine = rec_ref[0:1, cols].astype(jnp.int32) - at * length
        hit = lax.broadcasted_iota(jnp.int32, (length, share), 0) == mine
        donors[:, cols] = jnp.dot(block, jnp.where(hit, 1.0, 0.0).astype(BF16), preferred_element_type=F32)
        hit = place == accept - at * length
        accepts = accepts + jnp.dot(block, jnp.where(hit, 1.0, 0.0).astype(BF16), preferred_element_type=F32)
    rows = rows_ref[...]
    product = donors[...] * accepts * rows
    scored = jnp.sum(product, axis=0, keepdims=True) / root
    score = jnp.zeros((1, share), F32)
    for m in range(n_seq):
        score = jnp.where(seq_at == m, scored[:, m * share : (m + 1) * share], score)
    scale = rows * weight
    upstream = window_ref[...]
    spot = lax.broadcasted_iota(jnp.int32, (width, count), 0) + (seq_at * length - EDGE)
    for values, where in ((accepts * scale, donor), (donors[...] * scale, accept)):
        high = values.astype(BF16)
        low = (values - high.astype(F32)).astype(BF16)
        hit = jnp.where(spot == where, 1.0, 0.0).astype(BF16)
        both = lax.dot_general(
            jnp.concatenate([high, low], axis=0), hit, (((1,), (1,)), ((), ())), preferred_element_type=F32
        )
        upstream = upstream + (both[:ch] + both[ch:])
    up_ref[...] = upstream
    copy.wait()
    send_back(
        LAYERS - 1, upstream, meta, weights, slope_ref, taps, grad_ref, out_refs, score, n_tp, n_seq, length
    )


def pair_kernel(keep_ref, send_ref, got_ref, own_ref, *far_refs):
    count, ch, width = keep_ref.shape
    extra = join_rows(send_ref[count * ch :, :]) + join_rows(got_ref[count * ch :, :])
    split = split_rows(extra)
    for r in range(count):
        total = keep_ref[r].astype(F32) + got_ref[r * ch : (r + 1) * ch, :].astype(F32)
        if r == 0:
            own_ref[:ch, :] = total
            own_ref[ch:, :] = join_rows(split)
        else:
            far_refs[r - 1][:ch, :] = total.astype(BF16)
            far_refs[r - 1][ch:, :] = split


def backward_kernel(meta, w_ref, *refs, layer, n_far, n_tp, n_seq, length):
    own_ref, refs = refs[0], refs[1:]
    far, refs = refs[:n_far], refs[n_far:]
    up_ref, state_ref, inverse_ref, gain_ref, *refs = refs
    last = layer == 0
    if last:
        out_ref, part_ref = refs
    else:
        slope_ref, up_out, part_ref, grad_ref, *out_refs, weights, taps, sem = refs
        copy = pltpu.make_async_copy(w_ref.at[layer - 1], weights, sem)
        copy.start()
    if layer == LAYERS - 1:
        if last:
            score_ref = None
        else:
            score_ref, *out_refs = out_refs
    ch, width = up_ref.shape
    channels = ch * n_tp
    me = meta[n_tp + n_seq]
    sums = [own_ref[ch:, :]] + [join_rows(f[ch:, :]) for f in far]
    if n_far:
        extra = (sums[0] + sums[1]) + (sums[2] + sums[3])
    else:
        extra = sums[0]
    inner = extra[0:1, :]
    if layer == LAYERS - 1:
        score_ref[...] = extra
    inverse = inverse_ref[0:1, :]
    gain = gain_ref[me, :, layer : layer + 1]
    back = own_ref[:ch, :]
    for f in far:
        back = back + f[:ch, :].astype(F32)
    x = state_ref[...].astype(F32)
    pre = x * inverse * gain
    sq = pre * pre
    th = jnp.tanh(pre * (K0 + K1 * sq))
    half = 0.5 + 0.5 * th
    back = back * (half + (pre * half) * (1.0 - th) * (K0 + (3.0 * K1) * sq))
    lane = lax.broadcasted_iota(jnp.int32, (1, width), 1)
    mine = (lane >= EDGE) & (lane < EDGE + length)
    part = jnp.sum(jnp.where(mine, back * x * inverse, 0.0), axis=1, keepdims=True)
    part_ref[...] = jnp.broadcast_to(part, part_ref.shape)
    upstream = up_ref[...] + (inverse * gain) * back - x * (inverse * inverse * inverse * inner / channels)
    if last:
        out_ref[...] = own_part(upstream, length)
    else:
        up_out[...] = upstream
        copy.wait()
        send_back(
            layer - 1, upstream, meta, weights, slope_ref, taps, grad_ref, out_refs, None, n_tp, n_seq, length
        )


def weight_kernel(meta, *refs, layer, n_tp, n_seq):
    pieces, refs = refs[:n_seq], refs[n_seq:]
    every_ref, refs = refs[0], refs[1:]
    out_ref, whole, taps = refs[-3:]
    ch, length = pieces[0].shape
    reach = reach_of(layer)
    total = n_seq * length

    @pl.when(pl.program_id(0) == 0)
    def _():
        for m in range(n_seq):
            at = meta[n_tp + m]
            whole[:, pl.ds(pl.multiple_of(at * length, 128), length)] = pieces[m][...]
        grad = whole[...].astype(F32)
        lane = lax.broadcasted_iota(jnp.int32, (1, total), 1)
        taps[:ch, :] = jnp.where(lane < total - reach, roll(grad, -reach), 0.0).astype(BF16)
        taps[ch : 2 * ch, :] = whole[...]
        taps[2 * ch :, :] = jnp.where(lane >= reach, roll(grad, reach), 0.0).astype(BF16)

    acc = None
    for s in range(n_seq):
        block = every_ref[s].reshape(CHUNK, length)
        part = lax.dot_general(
            taps[:, s * length : (s + 1) * length],
            block,
            (((1,), (1,)), ((), ())),
            preferred_element_type=F32,
        )
        acc = part if acc is None else acc + part
    out_ref[...] = acc.reshape(3, ch, CHUNK)


def local(
    sequence_in,
    conv_weight,
    norm_gain,
    tissue_scale,
    donor_offset,
    acceptor_owner,
    acceptor_offset,
    tissue,
    tower_grad,
    score_grad,
):
    ch, length = sequence_in.shape
    n_tp, n_seq = lax.axis_size("tp"), lax.axis_size("seq")
    channels, total = ch * n_tp, length * n_seq
    width = length + 2 * EDGE
    share = donor_offset.shape[0]
    count = share * n_seq
    paired = n_tp == 8
    n_far = 3 if paired else 0
    me = lax.axis_index("tp").astype(jnp.int32)
    seq_at = lax.axis_index("seq").astype(jnp.int32)
    meta = jnp.concatenate([tp_order(me), seq_order(seq_at), jnp.stack([me, seq_at])])
    sizes = dict(n_tp=n_tp, n_seq=n_seq)
    weights = conv_weight.transpose(0, 2, 1, 3).reshape(LAYERS, 3 * ch, channels)

    high = lax.reduce_precision(tower_grad, 8, 7)
    low = tower_grad - high

    def edge(lanes):
        return jnp.concatenate(
            [
                sequence_in[:, lanes],
                high[:, lanes].astype(BF16),
                low[:, lanes].astype(BF16),
                jnp.zeros((ch, EDGE), BF16),
            ],
            axis=1,
        )

    left, right = edge(slice(0, EDGE)), edge(slice(length - EDGE, length))
    even = seq_at % 2 == 0
    first = lax.ppermute(jnp.where(even, right, left), "seq", [(i, i ^ 1) for i in range(n_seq)])
    pairs = [(i, i + 1) for i in range(1, n_seq - 1, 2)]
    second = lax.ppermute(jnp.where(even, left, right), "seq", pairs + [(j, i) for i, j in pairs])
    gain_cols = jnp.pad(norm_gain.T, ((0, 0), (0, 128 - LAYERS)))
    state, window = pl.pallas_call(
        functools.partial(prep_kernel, **sizes),
        out_shape=(jax.ShapeDtypeStruct((ch, width), BF16), jax.ShapeDtypeStruct((ch, width), F32)),
        in_specs=[SMEM] + [VMEM] * 5,
        out_specs=(VMEM, VMEM),
        compiler_params=params(),
        name="prep",
    )(meta, sequence_in, tower_grad, first, second, gain_cols)

    record = jnp.stack(
        [
            (donor_offset + seq_at * length).astype(F32),
            (acceptor_owner[:, 0] * length + acceptor_offset).astype(F32),
            tissue.astype(F32),
            score_grad,
        ]
        + [jnp.zeros((share,), F32)] * 4
    )
    table = lax.dynamic_slice_in_dim(tissue_scale, me * ch, ch, 1).T
    pad = -table.shape[1] % 128
    table = jnp.pad(table, ((0, 0), (0, pad)))
    records, rows = pl.pallas_call(
        functools.partial(lookup_kernel, **sizes),
        out_shape=(jax.ShapeDtypeStruct((8, count), F32), jax.ShapeDtypeStruct((ch, count), F32)),
        in_specs=[SMEM] + [VMEM] * (1 + n_seq),
        out_specs=(VMEM, VMEM),
        compiler_params=params(),
        name="lookup",
    )(meta, table, *gather_seq(record))

    stored = []
    gains = None
    for layer in range(LAYERS):
        pieces = gather_tp(state)
        final = layer == LAYERS - 1
        shapes = [
            jax.ShapeDtypeStruct((ch, length if final else width), BF16),
            jax.ShapeDtypeStruct((ch, length), BF16),
            jax.ShapeDtypeStruct((n_tp, ch, width), BF16),
            jax.ShapeDtypeStruct((8, width), F32),
        ]
        inputs = [meta, weights, state, *pieces]
        if layer == 0:
            shapes.append(jax.ShapeDtypeStruct((n_tp, ch, 128), F32))
        else:
            inputs.append(gains)
        got = pl.pallas_call(
            functools.partial(forward_kernel, layer=layer, length=length, **sizes),
            out_shape=shapes,
            in_specs=[SMEM, HBM] + [VMEM] * (len(inputs) - 2),
            out_specs=[VMEM] * len(shapes),
            scratch_shapes=[
                pltpu.VMEM((n_tp, ch, width), BF16),
                pltpu.VMEM((3 * ch, channels), BF16),
                pltpu.SemaphoreType.DMA,
            ],
            compiler_params=params(),
            name="forward",
        )(*inputs)
        if layer == 0:
            gains = got[4]
        every = lax.all_gather(got[1], ("seq", "tp"), axis=0).reshape(n_seq, n_tp, ch, length)
        stored.append((state, got[2], got[3], every))
        state = got[0]

    def product_shapes():
        if paired:
            return [
                jax.ShapeDtypeStruct((n_tp // 2, ch, width), BF16),
                jax.ShapeDtypeStruct((n_tp // 2 * ch + 16, width), BF16),
            ]
        return [jax.ShapeDtypeStruct((n_tp, ch, width), BF16), jax.ShapeDtypeStruct((8, width), F32)]

    def scratch():
        return [pltpu.VMEM((3 * ch, channels), BF16), pltpu.VMEM((3 * ch, width), BF16)]

    def reduce_tp(products):
        if not paired:
            whole, extra = products
            own = lax.psum_scatter(whole.reshape(channels, width), "tp", scatter_dimension=0, tiled=True)
            return [jnp.concatenate([own.astype(F32), lax.psum(extra, "tp")], axis=0)]
        keep, send = products
        got = swap(send, "tp", 1)
        far = jax.ShapeDtypeStruct((ch + 16, width), BF16)
        own, *far = pl.pallas_call(
            pair_kernel,
            out_shape=[jax.ShapeDtypeStruct((ch + 8, width), F32), far, far, far],
            in_specs=[VMEM] * 3,
            out_specs=[VMEM] * 4,
            compiler_params=params(),
            name="pair",
        )(keep, send, got)
        return [own] + [swap(v, "tp", 2 * r + 2) for r, v in enumerate(far)]

    blocks = gather_seq(state)
    shapes = [jax.ShapeDtypeStruct((ch, width), F32), jax.ShapeDtypeStruct((ch, length), BF16)] + product_shapes()
    upstream, grad, *products = pl.pallas_call(
        functools.partial(junction_kernel, root=math.sqrt(channels), **sizes),
        out_shape=shapes,
        in_specs=[SMEM, HBM] + [VMEM] * (4 + n_seq),
        out_specs=[VMEM] * len(shapes),
        scratch_shapes=scratch() + [pltpu.VMEM((ch, count), F32), pltpu.SemaphoreType.DMA],
        compiler_params=params(),
        name="junction",
    )(meta, weights, window, records, rows, stored[-1][1], *blocks)

    parts = [None] * LAYERS
    weight_grad = None
    scores = None
    for layer in reversed(range(LAYERS)):
        state, _, inverse, every = stored[layer]
        grads = gather_seq(grad)
        sums = reduce_tp(products)
        inputs = [meta, weights, *sums, upstream, state, inverse, gains]
        part_shape = jax.ShapeDtypeStruct((ch, 128), F32)
        if layer == 0:
            shapes = [jax.ShapeDtypeStruct((ch, length), F32), part_shape]
            extra_scratch = []
        else:
            inputs.append(stored[layer - 1][1])
            shapes = [jax.ShapeDtypeStruct((ch, width), F32), part_shape, jax.ShapeDtypeStruct((ch, length), BF16)]
            if layer == LAYERS - 1:
                shapes.append(jax.ShapeDtypeStruct((8, width), F32))
            shapes += product_shapes()
            extra_scratch = scratch() + [pltpu.SemaphoreType.DMA]
        got = pl.pallas_call(
            functools.partial(backward_kernel, layer=layer, n_far=n_far, length=length, **sizes),
            out_shape=shapes,
            in_specs=[SMEM, HBM] + [VMEM] * (len(inputs) - 2),
            out_specs=[VMEM] * len(shapes),
            scratch_shapes=extra_scratch,
            compiler_params=params(),
            name="backward",
        )(*inputs)
        parts[layer] = got[1]

        extra = [] if weight_grad is None else [weight_grad]
        weight_grad = pl.pallas_call(
            functools.partial(weight_kernel, layer=layer, **sizes),
            grid=(channels // CHUNK,),
            out_shape=jax.ShapeDtypeStruct((LAYERS, 3, ch, channels), F32),
            in_specs=[SMEM]
            + [pl.BlockSpec((ch, length), lambda i: (0, 0))] * n_seq
            + [pl.BlockSpec((n_seq, CHUNK // ch, ch, length), lambda i: (0, i, 0, 0))]
            + [HBM] * len(extra),
            out_specs=pl.BlockSpec((None, 3, ch, CHUNK), functools.partial(lambda i, layer: (layer, 0, 0, i), layer=layer)),
            scratch_shapes=[pltpu.VMEM((ch, total), BF16), pltpu.VMEM((3 * ch, total), BF16)],
            input_output_aliases={n_seq + 2: 0} if extra else {},
            compiler_params=params(),
            name="weight",
        )(meta, *grads, every, *extra)

        if layer == 0:
            input_grad = got[0]
        else:
            upstream, grad, products = got[0], got[2], got[3:]
            if layer == LAYERS - 1:
                scores, products = products[0][1, :share], products[1:]
    columns = jnp.pad(jnp.stack([p[:, 0] for p in parts]), ((0, 8 - LAYERS), (0, 0)))
    pieces = gather_seq(columns)
    if len(pieces) == 4:
        gain_grad = (pieces[0] + pieces[1]) + (pieces[2] + pieces[3])
    else:
        gain_grad = sum(pieces)
    return (scores, input_grad, weight_grad.transpose(0, 2, 1, 3), gain_grad[:LAYERS])


def solution(mesh):
    return jax.shard_map(
        local,
        mesh=mesh,
        in_specs=(
            P("tp", "seq"),
            P(None, "tp", None, None),
            P(None, "tp"),
            P(),
            P("seq"),
            P("seq", None),
            P("seq"),
            P("seq"),
            P("tp", "seq"),
            P("seq"),
        ),
        out_specs=(P("seq"), P("tp", "seq"), P(None, "tp", None, None), P(None, "tp")),
        check_vma=False,
    )
```

time: 649 us -> 365 us (0.56)
  waiting for transfers between devices: 339 us -> 177 us
  blocking collectives: 93 us -> 0 us
  Pallas kernels: 0 us -> 69.9 us
  matrix products: 45.3 us -> 0 us
  local copies, waits for them, and re-layouts: 75.8 us -> 34.9 us
  other arithmetic: 38.8 us -> 2.04 us
  starting transfers between devices: 40.1 us -> 66.8 us
    psum x1 -> x0, waiting for transfers between devices: 165 us -> none  [local(): lax.psum(weight_term.astype(jnp.bfloat16), 'seq').astype(jnp.float32)]
    psum x7 -> x0, blocking collectives: 93 us -> none  [the longest x3 41.3 us: local(): power = lax.psum(jnp.sum(stream * stream, axis=0), 'tp') / CHANNELS]
    reduce_scatter x3 -> x0, waiting for transfers between devices: 91.1 us -> none  [local(): lax.psum_scatter(term_rows(jnp.int32(0), local_ch * lax.axis_size('tp'))....]
    ppermute x12 -> x53, waiting for transfers between devices: 25.3 us -> 104 us  [the longest x51 103 us: swap(): return lax.ppermute(x, axis, [(i, i ^ mask) for i in range(count)])]
    pallas_call x0 -> x15, Pallas kernels: none -> 69.9 us  [the longest x3 25.2 us: local(): pl.pallas_call(functools.partial(weight_kernel, layer=layer, **sizes), gr...]
    scatter x3 -> x0, local copies, waits for them, and re-layouts: 52.6 us -> none  [the longest x1 38.6 us: local(): jnp.zeros((seq_count, CAP), jnp.int32).at[owner, slot].set(acceptor_offset)]
    dot_general x28 -> x0, matrix products: 45.3 us -> none  [the longest x9 17.1 us: forward_taps(): jnp.dot(weights[:, tap, :], padded[:, tap * reach:tap * reach + length],...]
    ppermute x12 -> x53, starting transfers between devices: 28.5 us -> 66.5 us  [the longest x51 62.8 us: swap(): return lax.ppermute(x, axis, [(i, i ^ mask) for i in range(count)])]
  transfers between devices with their start and end apart: 22 -> 56, of which waited for: 18 -> 30; matrix products, arithmetic and copies ran while one was open for 13% -> 1% of each run, Pallas kernels for 0% -> 10%
where the time goes in v1:
time: 365 us
  waiting for transfers between devices  177 us (48%)
  Pallas kernels  69.9 us (19%)
  starting transfers between devices  66.8 us (18%)
  local copies, waits for them, and re-layouts  34.9 us (10%)
  between operations  14.3 us (4%)
    ppermute x51, waiting for transfers between devices, swap(): return lax.ppermute(x, axis, [(i, i ^ mask) for i in range(count)])  103 us
    all_gather x3, waiting for transfers between devices, local(): lax.all_gather(got[1], ('seq', 'tp'), axis=0)  71.7 us
    ppermute x51, starting transfers between devices, swap(): return lax.ppermute(x, axis, [(i, i ^ mask) for i in range(count)])  62.8 us
    unnamed x88, local copies, waits for them, and re-layouts  31.9 us
    pallas_call x3, Pallas kernels, local(): pl.pallas_call(functools.partial(weight_kernel, layer=layer, **sizes), gr...  25.2 us
    pallas_call x3, Pallas kernels, local(): pl.pallas_call(functools.partial(forward_kernel, layer=layer, length=leng...  23.1 us
    pallas_call x3, Pallas kernels, local(): pl.pallas_call(functools.partial(backward_kernel, layer=layer, n_far=n_fa...  11.1 us
  transfers between devices with their start and end apart: 56, of which 30 were waited for; matrix products, arithmetic and copies ran while one was open for 1% of the time, Pallas kernels for 10%

profile of v1, /device:TPU:0, one launch (start us, length us, event | category | flops | bytes accessed | tf_op | source)
XLA Modules:
  0.0 364.7 jit_solution(17741042654442699449)
XLA Ops:
  9.7 3.1 collective-permute-start
  19.3 2.7 collective-permute-start.10
  22.8 6.3 %collective-permute-done.10.refs_6_ = bf16[192,640]{1,0:T(8,128)(2,1)S(1)} collective-permute-done((bf16[192,640]{1,0:T(8,128)(2,1)S(1)}, bf16[192,640]{1,0:T(8,128)(2,1)S(1)}, u32[]{:S(2)}, u32[]{:S(2)}) %collective-permute-start.10) | collective-permute-done | bytes 245792 | tf_op jit(solution)/shard_map/ppermute | solution.py:36
  29.2 3.2 collective-permute-done.6.refs_2_
  34.2 2.5 copy-done.2
  36.7 8.7 %forward.3 = (bf16[192,640]{1,0:T(8,128)(2,1)S(1)}, bf16[192,512]{1,0:T(8,128)(2,1)}, bf16[8,192,640]{2,1,0:T(8,128)(2,1)S(1)}, f32[8,640]{1,0:T(8,128)S(1)}, f32[8,192,128]{2,1,0:T(8,128)S(1)}) custom-call(s32[14]{0:T(128)S(1)} %pad_add_fusion.meta, bf16[3,576,1536]{2,1,0:T(8,128)(2,1)S(1)} %bitcast.20, ...), custom_call_target="tpu_custom_call" | custom-call | tf_op jit(solution)/shard_map/forward/pallas_call | solution.py:494
  45.5 1.3 copy-done.16
  46.8 1.5 collective-permute-start.13
  50.3 5.3 %collective-permute-done.13.refs_2_ = bf16[192,640]{1,0:T(8,128)(2,1)S(1)} collective-permute-done((bf16[192,640]{1,0:T(8,128)(2,1)S(1)}, bf16[192,640]{1,0:T(8,128)(2,1)S(1)}, u32[]{:S(2)}, u32[]{:S(2)}) %collective-permute-start.13) | collective-permute-done | bytes 245792 | tf_op jit(solution)/shard_map/ppermute | solution.py:36
  55.6 5.7 %collective-permute-done.15.refs_4_ = bf16[192,640]{1,0:T(8,128)(2,1)S(1)} collective-permute-done((bf16[192,640]{1,0:T(8,128)(2,1)S(1)}, bf16[192,640]{1,0:T(8,128)(2,1)S(1)}, u32[]{:S(2)}, u32[]{:S(2)}) %collective-permute-start.15) | collective-permute-done | bytes 245792 | tf_op jit(solution)/shard_map/ppermute | solution.py:36
  63.1 7.1 %forward.4 = (bf16[192,640]{1,0:T(8,128)(2,1)S(1)}, bf16[192,512]{1,0:T(8,128)(2,1)}, bf16[8,192,640]{2,1,0:T(8,128)(2,1)S(1)}, f32[8,640]{1,0:T(8,128)S(1)}) custom-call(s32[14]{0:T(128)S(1)} %pad_add_fusion.meta, bf16[3,576,1536]{2,1,0:T(8,128)(2,1)S(1)} %bitcast.21, bf16[192,640]{1,0:T(8,128)(2,1)S(1)} %get-tuple-element.54.own_ref.refs_0_.refs_5_, ...), custom_call_target="tpu_custom_call" | custom-call | tf_op jit(solution)/shard_map/forward/pallas_call | solution.py:494
  70.2 1.3 copy-done.18
  73.0 2.1 collective-permute-start.24
  75.1 5.3 %collective-permute-done.20.refs_2_ = bf16[192,640]{1,0:T(8,128)(2,1)S(1)} collective-permute-done((bf16[192,640]{1,0:T(8,128)(2,1)S(1)}, bf16[192,640]{1,0:T(8,128)(2,1)S(1)}, u32[]{:S(2)}, u32[]{:S(2)}) %collective-permute-start.20) | collective-permute-done | bytes 245792 | tf_op jit(solution)/shard_map/ppermute | solution.py:36
  80.9 4.4 %collective-permute-done.24.refs_6_ = bf16[192,640]{1,0:T(8,128)(2,1)S(1)} collective-permute-done((bf16[192,640]{1,0:T(8,128)(2,1)S(1)}, bf16[192,640]{1,0:T(8,128)(2,1)S(1)}, u32[]{:S(2)}, u32[]{:S(2)}) %collective-permute-start.24) | collective-permute-done | bytes 245792 | tf_op jit(solution)/shard_map/ppermute | solution.py:36
  85.4 1.5 collective-permute-done.25.refs_7_
  86.9 7.4 %forward.5 = (bf16[192,512]{1,0:T(8,128)(2,1)}, bf16[192,512]{1,0:T(8,128)(2,1)}, bf16[8,192,640]{2,1,0:T(8,128)(2,1)S(1)}, f32[8,640]{1,0:T(8,128)S(1)}) custom-call(s32[14]{0:T(128)S(1)} %pad_add_fusion.meta, bf16[3,576,1536]{2,1,0:T(8,128)(2,1)S(1)} %bitcast.22, bf16[192,640]{1,0:T(8,128)(2,1)S(1)} %get-tuple-element.56.own_ref.refs_0_.refs_5_, ...), custom_call_target="tpu_custom_call" | custom-call | tf_op jit(solution)/shard_map/forward/pallas_call | solution.py:494
  94.3 1.3 copy-done.20
  97.1 4.6 %collective-permute-start.26 = (bf16[192,512]{1,0:T(8,128)(2,1)}, bf16[192,512]{1,0:T(8,128)(2,1)}, u32[]{:S(2)}, u32[]{:S(2)}) collective-permute-start(bf16[192,512]{1,0:T(8,128)(2,1)} %get-tuple-element.58.refs_0_), channel_id=1, source_target_pairs={{0,8},{8,0},{16,24},{24,16},{1,9},{9,1},{17,25},{25,17},{2,10},{10... | collective-permute-start | bytes 589832 | tf_op jit(solution)/shard_map/ppermute | solution.py:36
  101.8 1.3 collective-permute-start.27
  103.0 1.4 collective-permute-start.28
  105.4 2.2 collective-permute-start.3
  107.5 9.6 %collective-permute-done.2.refs_1_ = f32[8,256]{1,0:T(8,128)S(1)} collective-permute-done((f32[8,256]{1,0:T(8,128)S(1)}, f32[8,256]{1,0:T(8,128)S(1)}, u32[]{:S(2)}, u32[]{:S(2)}) %collective-permute-start.2) | collective-permute-done | bytes 8224 | tf_op jit(solution)/shard_map/ppermute | solution.py:36
  117.1 2.6 collective-permute-start.4
  121.9 5.1 %collective-permute-done.3.refs_2_ = f32[8,256]{1,0:T(8,128)S(1)} collective-permute-done((f32[8,256]{1,0:T(8,128)S(1)}, f32[8,256]{1,0:T(8,128)S(1)}, u32[]{:S(2)}, u32[]{:S(2)}) %collective-permute-start.3) | collective-permute-done | bytes 8224 | tf_op jit(solution)/shard_map/ppermute | solution.py:36
  126.9 1.3 lookup.1
  128.3 2.5 copy-done.4
  130.8 1.5 copy-done.21
  133.4 7.3 %junction.1 = (f32[192,640]{1,0:T(8,128)S(1)}, bf16[192,512]{1,0:T(8,128)(2,1)S(1)}, bf16[4,192,640]{2,1,0:T(8,128)(2,1)S(1)}, bf16[784,640]{1,0:T(8,128)(2,1)S(1)}) custom-call(s32[14]{0:T(128)S(1)} %pad_add_fusion.meta, bf16[3,576,1536]{2,1,0:T(8,128)(2,1)S(1)} %bitcast.23, f32[192,640]{1,0:T(8,128)S(1)} %copy-done.24, ...), custom_call_target="tpu_custom_call" | custom-call | tf_op jit(solution)/shard_map/junction/pallas_call | solution.py:544
  140.8 2.6 collective-permute-done.29.got_ref
  143.6 1.7 collective-permute-start.30
  147.2 5.7 %collective-permute-done.30.refs_1_ = bf16[208,640]{1,0:T(8,128)(2,1)S(1)} collective-permute-done((bf16[208,640]{1,0:T(8,128)(2,1)S(1)}, bf16[208,640]{1,0:T(8,128)(2,1)S(1)}, u32[]{:S(2)}, u32[]{:S(2)}) %collective-permute-start.30) | collective-permute-done | bytes 266272 | tf_op jit(solution)/shard_map/ppermute | solution.py:36
  152.9 6.7 %collective-permute-done.31.refs_2_ = bf16[208,640]{1,0:T(8,128)(2,1)S(1)} collective-permute-done((bf16[208,640]{1,0:T(8,128)(2,1)S(1)}, bf16[208,640]{1,0:T(8,128)(2,1)S(1)}, u32[]{:S(2)}, u32[]{:S(2)}) %collective-permute-start.31) | collective-permute-done | bytes 266272 | tf_op jit(solution)/shard_map/ppermute | solution.py:36
  159.6 3.1 collective-permute-done.32.refs_3_
  163.8 4.4 %backward.3 = (f32[192,640]{1,0:T(8,128)S(1)}, f32[192,128]{1,0:T(8,128)S(1)}, bf16[192,512]{1,0:T(8,128)(2,1)}, f32[8,640]{1,0:T(8,128)S(1)}, bf16[4,192,640]{2...) custom-call(s32[14]{0:T(128)S(1)} %pad_add_fusion.meta, bf16[3,576,1536]{2,1,0:T(8,128)(2,1)S(1)} %bitcast.26, ...), custom_call_target="tpu_custom_call" | custom-call | tf_op jit(solution)/shard_map/backward/pallas_call | solution.py:573
  168.3 2.6 collective-permute-done.33.got_ref
  171.1 2.6 collective-permute-start.34
  173.7 1.8 collective-permute-start.35
  175.5 5.4 %collective-permute-done.34.refs_1_ = bf16[208,640]{1,0:T(8,128)(2,1)S(1)} collective-permute-done((bf16[208,640]{1,0:T(8,128)(2,1)S(1)}, bf16[208,640]{1,0:T(8,128)(2,1)S(1)}, u32[]{:S(2)}, u32[]{:S(2)}) %collective-permute-start.34) | collective-permute-done | bytes 266272 | tf_op jit(solution)/shard_map/ppermute | solution.py:36
  180.9 6.8 %collective-permute-done.35.refs_2_ = bf16[208,640]{1,0:T(8,128)(2,1)S(1)} collective-permute-done((bf16[208,640]{1,0:T(8,128)(2,1)S(1)}, bf16[208,640]{1,0:T(8,128)(2,1)S(1)}, u32[]{:S(2)}, u32[]{:S(2)}) %collective-permute-start.35) | collective-permute-done | bytes 266272 | tf_op jit(solution)/shard_map/ppermute | solution.py:36
  187.7 4.7 %backward.4 = (f32[192,640]{1,0:T(8,128)S(1)}, f32[192,128]{1,0:T(8,128)S(1)}, bf16[192,512]{1,0:T(8,128)(2,1)}, bf16[4,192,640]{2,1,0:T(8,128)(2,1)S(1)}, bf16[784,640]{1,0:T(8,128)(2,1)S(1)}) custom-call(s32[14]{0:T(128)S(1)} %pad_add_fusion.meta, bf16[3,576,1536]{2,1,0:T(8,128)(2,1)S(1)} %bitcast.27, f32[200,640]{1,0:T(8,128)S(1)} %get-tuple-element.71.refs_0_, ...), custom_call_target="tpu_custom_call" | custom-call | tf_op jit(solution)/shard_map/backward/pallas_call | solution.py:573
  192.4 2.6 collective-permute-done.37.got_ref
  195.3 1.5 collective-permute-start.38
  197.4 1.4 collective-permute-start.40
  198.8 2.3 collective-permute-start.48
  201.4 3.2 collective-permute-done.38.refs_1_
  204.6 1.8 collective-permute-start.49
  206.3 2.5 collective-permute-done.39.refs_2_
  208.8 1.8 collective-permute-done.40.refs_3_
  210.6 2.0 backward.5
  213.7 1.9 collective-permute-start.51
  215.6 2.7 collective-permute-done.48.refs_2_
  219.0 3.6 collective-permute-start.52
  223.8 11.6 %collective-permute-start.45 = (bf16[192,512]{1,0:T(8,128)(2,1)}, bf16[192,512]{1,0:T(8,128)(2,1)S(1)}, u32[]{:S(2)}, u32[]{:S(2)}) collective-permute-start(bf16[192,512]{1,0:T(8,128)(2,1)} %get-tuple-element.89.refs_0_), channel_id=1, source_target_pairs={{0,16},{8,24},{16,0},{24,8},{1,17},{9,25},{17,1},{25,9},{2,18},{10... | collective-permute-start | bytes 589832 | tf_op jit(solution)/shard_map/ppermute | solution.py:36
  236.7 3.8 %collective-permute-start.42 = (bf16[192,512]{1,0:T(8,128)(2,1)}, bf16[192,512]{1,0:T(8,128)(2,1)S(1)}, u32[]{:S(2)}, u32[]{:S(2)}) collective-permute-start(bf16[192,512]{1,0:T(8,128)(2,1)} %get-tuple-element.87.refs_0_), channel_id=1, source_target_pairs={{0,16},{8,24},{16,0},{24,8},{1,17},{9,25},{17,1},{25,9},{2,18},{10... | collective-permute-start | bytes 589832 | tf_op jit(solution)/shard_map/ppermute | solution.py:36
  241.5 2.8 copy-done.7
  248.0 8.1 %weight.3.refs_5_ = f32[3,3,192,1536]{3,2,1,0:T(8,128)} custom-call(s32[14]{0:T(128)S(1)} %pad_add_fusion.meta, bf16[192,512]{1,0:T(8,128)(2,1)S(1)} %copy-done.27, bf16[192,512]{1,0:T(8,128)(2,1)S(1)} %copy-done.29, bf16[192,512]{1,0:T(8,128)(2,1)S(1)} %copy-done.31, bf16[192,512]{1,0:T(8,128)(2,1)S(1)} %copy-done.33, bf16[4,8,192,512]{3,2,1,0:T(8,128)(2,1)S(1)} %bitcast.29), custom_call_target="tpu_custom_call" | custom-call | tf_op jit(solution)/shard_map/weight/pallas_call | solution.py:585
  256.1 7.6 %collective-permute-done.45.refs_2_ = bf16[192,512]{1,0:T(8,128)(2,1)S(1)} collective-permute-done((bf16[192,512]{1,0:T(8,128)(2,1)}, bf16[192,512]{1,0:T(8,128)(2,1)S(1)}, u32[]{:S(2)}, u32[]{:S(2)}) %collective-permute-start.45) | collective-permute-done | bytes 196640 | tf_op jit(solution)/shard_map/ppermute | solution.py:36
  263.7 11.8 %all-gather.9.cloned.1.call-done = bf16[6144,512]{1,0:T(8,128)(2,1)} async-done(((bf16[192,512]{1,0:T(8,128)(2,1)}), bf16[6144,512]{1,0:T(8,128)(2,1)}) %all-gather.9.cloned.1.call-update) | async-done | bytes 6291472 | tf_op jit(solution)/shard_map/all_gather | solution.py:509
  275.5 2.8 copy-done.9
  278.3 8.5 %weight.4.refs_5_ = f32[3,3,192,1536]{3,2,1,0:T(8,128)} custom-call(s32[14]{0:T(128)S(1)} %pad_add_fusion.meta, bf16[192,512]{1,0:T(8,128)(2,1)} %get-tuple-element.89.refs_0_, bf16[192,512]{1,0:T(8,128)(2,1)S(1)} %copy-done.35, bf16[192,512]{1,0:T(8,128)(2,1)S(1)} %collective-permute-done.45.refs_2_, ...), custom_call_target="tpu_custom_call", output_to_operand_aliasing={{}: (6, {})} | custom-call | tf_op jit(solution)/shard_map/weight/pallas_call | solution.py:585
  286.8 59.9 %all-gather.7.cloned.1.call-done = bf16[6144,512]{1,0:T(8,128)(2,1)} async-done(((bf16[192,512]{1,0:T(8,128)(2,1)}), bf16[6144,512]{1,0:T(8,128)(2,1)}) %all-gather.7.cloned.1.call-update) | async-done | bytes 6291472 | tf_op jit(solution)/shard_map/all_gather | solution.py:509
  346.7 2.8 copy-done.8
  349.5 8.6 %weight.5 = f32[3,3,192,1536]{3,2,1,0:T(8,128)} custom-call(s32[14]{0:T(128)S(1)} %pad_add_fusion.meta, bf16[192,512]{1,0:T(8,128)(2,1)} %get-tuple-element.87.refs_0_, bf16[192,512]{1,0:T(8,128)(2,1)S(1)} %collective-permute-done.41.refs_1_, bf16[192,512]{1,0:T(8,128)(2,1)S(1)} %collective-permute-done.42.refs_2_, ...), custom_call_target="tpu_custom_call", output_to_operand_aliasing={{}: (6, {})} | custom-call | tf_op jit(solution)/shard_map/weight/pallas_call | solution.py:585
  (179 shorter events, 36.7 us)
Async XLA Ops:
  7.2 112.6 %copy-start = (f32[367,1536]{1,0:T(8,128)S(1)}, f32[367,1536]{1,0:T(8,128)}, u32[]{:S(2)}) copy-start(f32[367,1536]{1,0:T(8,128)} %param.13) | copy-start | bytes 6764548
  7.2 234.3 %all-gather.11.cloned.1.call-start = ((), (), s32[]{:S(2)}) async-start(), calls=%async_computation.2 | async-start | bytes 6488064 | tf_op jit(solution)/shard_map/all_gather | solution.py:509
  9.7 5.9 %collective-permute-start = (bf16[192,256]{1,0:T(8,128)(2,1)S(1)}, bf16[192,256]{1,0:T(8,128)(2,1)S(1)}, u32[]{:S(2)}, u32[]{:S(2)}) collective-permute-start(bf16[192,256]{1,0:T(8,128)(2,1)S(1)} %get-tuple-element.99), channel_id=1, source_target_pairs={{0,8},{8,0},{16,24},{24,16},{1,9},{9,1},{17,25},{25,17},{2,10},{10... | collective-permute-start | bytes 294920 | tf_op jit(solution)/shard_map/ppermute | solution.py:444
  12.8 2.8 collective-permute-start.1
  19.3 43.8 %copy-start.14 = (bf16[192,640]{1,0:T(8,128)(2,1)}, bf16[192,640]{1,0:T(8,128)(2,1)S(1)}, u32[]{:S(2)}) copy-start(bf16[192,640]{1,0:T(8,128)(2,1)S(1)} %get-tuple-element.53.own_ref.refs_0_.refs_5_) | copy-start | bytes 737284
  19.3 9.8 %collective-permute-start.10 = (bf16[192,640]{1,0:T(8,128)(2,1)S(1)}, bf16[192,640]{1,0:T(8,128)(2,1)S(1)}, u32[]{:S(2)}, u32[]{:S(2)}) collective-permute-start(bf16[192,640]{1,0:T(8,128)(2,1)S(1)} %get-tuple-element.53.own_ref.refs_0_.refs_5_), channel_id=1, source_target_pairs={{0,6},{1,7},{2,4},{3,5},{4,2},{5,3},{6,0},{7,1},{8,14},{9,15},{10,... | collective-permute-start | bytes 737288 | tf_op jit(solution)/shard_map/ppermute | solution.py:36
  22.0 10.4 %collective-permute-start.6 = (bf16[192,640]{1,0:T(8,128)(2,1)S(1)}, bf16[192,640]{1,0:T(8,128)(2,1)S(1)}, u32[]{:S(2)}, u32[]{:S(2)}) collective-permute-start(bf16[192,640]{1,0:T(8,128)(2,1)S(1)} %get-tuple-element.53.own_ref.refs_0_.refs_5_), channel_id=1, source_target_pairs={{0,2},{1,3},{2,0},{3,1},{4,6},{5,7},{6,4},{7,5},{8,10},{9,11},{10,... | collective-permute-start | bytes 737288 | tf_op jit(solution)/shard_map/ppermute | solution.py:36
  22.5 10.1 %collective-permute-start.8 = (bf16[192,640]{1,0:T(8,128)(2,1)S(1)}, bf16[192,640]{1,0:T(8,128)(2,1)S(1)}, u32[]{:S(2)}, u32[]{:S(2)}) collective-permute-start(bf16[192,640]{1,0:T(8,128)(2,1)S(1)} %get-tuple-element.53.own_ref.refs_0_.refs_5_), channel_id=1, source_target_pairs={{0,4},{1,5},{2,6},{3,7},{4,0},{5,1},{6,2},{7,3},{8,12},{9,13},{10,... | collective-permute-start | bytes 737288 | tf_op jit(solution)/shard_map/ppermute | solution.py:36
  22.8 10.1 %collective-permute-start.5 = (bf16[192,640]{1,0:T(8,128)(2,1)S(1)}, bf16[192,640]{1,0:T(8,128)(2,1)S(1)}, u32[]{:S(2)}, u32[]{:S(2)}) collective-permute-start(bf16[192,640]{1,0:T(8,128)(2,1)S(1)} %get-tuple-element.53.own_ref.refs_0_.refs_5_), channel_id=1, source_target_pairs={{0,1},{1,0},{2,3},{3,2},{4,5},{5,4},{6,7},{7,6},{8,9},{9,8},{10,11... | collective-permute-start | bytes 737288 | tf_op jit(solution)/shard_map/ppermute | solution.py:36
  29.2 3.7 %collective-permute-start.11 = (bf16[192,640]{1,0:T(8,128)(2,1)S(1)}, bf16[192,640]{1,0:T(8,128)(2,1)S(1)}, u32[]{:S(2)}, u32[]{:S(2)}) collective-permute-start(bf16[192,640]{1,0:T(8,128)(2,1)S(1)} %collective-permute-done.10.refs_6_), channel_id=1, source_target_pairs={{0,1},{1,0},{2,3},{3,2},{4,5},{5,4},{6,7},{7,6},{8,9},{9,8},{10,11... | collective-permute-start | bytes 737288 | tf_op jit(solution)/shard_map/ppermute | solution.py:36
  32.4 1.5 collective-permute-start.7
  32.6 1.6 collective-permute-start.9
  46.8 47.5 %copy-start.5 = (f32[8,192,128]{2,1,0:T(8,128)}, f32[8,192,128]{2,1,0:T(8,128)S(1)}, u32[]{:S(2)}) copy-start(f32[8,192,128]{2,1,0:T(8,128)S(1)} %get-tuple-element.55.refs_8_.refs_7_) | copy-start | bytes 2359300
  46.8 47.5 %copy-start.10 = (bf16[192,640]{1,0:T(8,128)(2,1)}, bf16[192,640]{1,0:T(8,128)(2,1)S(1)}, u32[]{:S(2)}) copy-start(bf16[192,640]{1,0:T(8,128)(2,1)S(1)} %get-tuple-element.54.own_ref.refs_0_.refs_5_) | copy-start | bytes 737284
  46.8 8.8 %collective-permute-start.13 = (bf16[192,640]{1,0:T(8,128)(2,1)S(1)}, bf16[192,640]{1,0:T(8,128)(2,1)S(1)}, u32[]{:S(2)}, u32[]{:S(2)}) collective-permute-start(bf16[192,640]{1,0:T(8,128)(2,1)S(1)} %get-tuple-element.54.own_ref.refs_0_.refs_5_), channel_id=1, source_target_pairs={{0,2},{1,3},{2,0},{3,1},{4,6},{5,7},{6,4},{7,5},{8,10},{9,11},{10,... | collective-permute-start | bytes 737288 | tf_op jit(solution)/shard_map/ppermute | solution.py:36
  48.2 13.0 %collective-permute-start.15 = (bf16[192,640]{1,0:T(8,128)(2,1)S(1)}, bf16[192,640]{1,0:T(8,128)(2,1)S(1)}, u32[]{:S(2)}, u32[]{:S(2)}) collective-permute-start(bf16[192,640]{1,0:T(8,128)(2,1)S(1)} %get-tuple-element.54.own_ref.refs_0_.refs_5_), channel_id=1, source_target_pairs={{0,4},{1,5},{2,6},{3,7},{4,0},{5,1},{6,2},{7,3},{8,12},{9,13},{10,... | collective-permute-start | bytes 737288 | tf_op jit(solution)/shard_map/ppermute | solution.py:36
  49.3 11.9 %collective-permute-start.17 = (bf16[192,640]{1,0:T(8,128)(2,1)S(1)}, bf16[192,640]{1,0:T(8,128)(2,1)S(1)}, u32[]{:S(2)}, u32[]{:S(2)}) collective-permute-start(bf16[192,640]{1,0:T(8,128)(2,1)S(1)} %get-tuple-element.54.own_ref.refs_0_.refs_5_), channel_id=1, source_target_pairs={{0,6},{1,7},{2,4},{3,5},{4,2},{5,3},{6,0},{7,1},{8,14},{9,15},{10,... | collective-permute-start | bytes 737288 | tf_op jit(solution)/shard_map/ppermute | solution.py:36
  50.3 11.5 %collective-permute-start.12 = (bf16[192,640]{1,0:T(8,128)(2,1)S(1)}, bf16[192,640]{1,0:T(8,128)(2,1)S(1)}, u32[]{:S(2)}, u32[]{:S(2)}) collective-permute-start(bf16[192,640]{1,0:T(8,128)(2,1)S(1)} %get-tuple-element.54.own_ref.refs_0_.refs_5_), channel_id=1, source_target_pairs={{0,1},{1,0},{2,3},{3,2},{4,5},{5,4},{6,7},{7,6},{8,9},{9,8},{10,11... | collective-permute-start | bytes 737288 | tf_op jit(solution)/shard_map/ppermute | solution.py:36
  55.6 6.2 %collective-permute-start.14 = (bf16[192,640]{1,0:T(8,128)(2,1)S(1)}, bf16[192,640]{1,0:T(8,128)(2,1)S(1)}, u32[]{:S(2)}, u32[]{:S(2)}) collective-permute-start(bf16[192,640]{1,0:T(8,128)(2,1)S(1)} %collective-permute-done.13.refs_2_), channel_id=1, source_target_pairs={{0,1},{1,0},{2,3},{3,2},{4,5},{5,4},{6,7},{7,6},{8,9},{9,8},{10,11... | collective-permute-start | bytes 737288 | tf_op jit(solution)/shard_map/ppermute | solution.py:36
  61.3 1.5 collective-permute-start.16
  61.3 1.9 collective-permute-start.18
  71.5 32.9 %copy-start.37 = (f32[256]{0:T(256)S(1)}, f32[256]{0:T(256)}, u32[]{:S(2)}) copy-start(f32[256]{0:T(256)} %param.19) | copy-start | bytes 3076
  71.5 8.9 %collective-permute-start.20 = (bf16[192,640]{1,0:T(8,128)(2,1)S(1)}, bf16[192,640]{1,0:T(8,128)(2,1)S(1)}, u32[]{:S(2)}, u32[]{:S(2)}) collective-permute-start(bf16[192,640]{1,0:T(8,128)(2,1)S(1)} %get-tuple-element.56.own_ref.refs_0_.refs_5_), channel_id=1, source_target_pairs={{0,2},{1,3},{2,0},{3,1},{4,6},{5,7},{6,4},{7,5},{8,10},{9,11},{10,... | collective-permute-start | bytes 737288 | tf_op jit(solution)/shard_map/ppermute | solution.py:36
  72.0 8.4 %collective-permute-start.22 = (bf16[192,640]{1,0:T(8,128)(2,1)S(1)}, bf16[192,640]{1,0:T(8,128)(2,1)S(1)}, u32[]{:S(2)}, u32[]{:S(2)}) collective-permute-start(bf16[192,640]{1,0:T(8,128)(2,1)S(1)} %get-tuple-element.56.own_ref.refs_0_.refs_5_), channel_id=1, source_target_pairs={{0,4},{1,5},{2,6},{3,7},{4,0},{5,1},{6,2},{7,3},{8,12},{9,13},{10,... | collective-permute-start | bytes 737288 | tf_op jit(solution)/shard_map/ppermute | solution.py:36
  73.0 12.4 %collective-permute-start.24 = (bf16[192,640]{1,0:T(8,128)(2,1)S(1)}, bf16[192,640]{1,0:T(8,128)(2,1)S(1)}, u32[]{:S(2)}, u32[]{:S(2)}) collective-permute-start(bf16[192,640]{1,0:T(8,128)(2,1)S(1)} %get-tuple-element.56.own_ref.refs_0_.refs_5_), channel_id=1, source_target_pairs={{0,6},{1,7},{2,4},{3,5},{4,2},{5,3},{6,0},{7,1},{8,14},{9,15},{10,... | collective-permute-start | bytes 737288 | tf_op jit(solution)/shard_map/ppermute | solution.py:36
  75.1 10.3 %collective-permute-start.19 = (bf16[192,640]{1,0:T(8,128)(2,1)S(1)}, bf16[192,640]{1,0:T(8,128)(2,1)S(1)}, u32[]{:S(2)}, u32[]{:S(2)}) collective-permute-start(bf16[192,640]{1,0:T(8,128)(2,1)S(1)} %get-tuple-element.56.own_ref.refs_0_.refs_5_), channel_id=1, source_target_pairs={{0,1},{1,0},{2,3},{3,2},{4,5},{5,4},{6,7},{7,6},{8,9},{9,8},{10,11... | collective-permute-start | bytes 737288 | tf_op jit(solution)/shard_map/ppermute | solution.py:36
  80.4 5.0 %collective-permute-start.21 = (bf16[192,640]{1,0:T(8,128)(2,1)S(1)}, bf16[192,640]{1,0:T(8,128)(2,1)S(1)}, u32[]{:S(2)}, u32[]{:S(2)}) collective-permute-start(bf16[192,640]{1,0:T(8,128)(2,1)S(1)} %collective-permute-done.20.refs_2_), channel_id=1, source_target_pairs={{0,1},{1,0},{2,3},{3,2},{4,5},{5,4},{6,7},{7,6},{8,9},{9,8},{10,11... | collective-permute-start | bytes 737288 | tf_op jit(solution)/shard_map/ppermute | solution.py:36
  80.4 5.0 %collective-permute-start.23 = (bf16[192,640]{1,0:T(8,128)(2,1)S(1)}, bf16[192,640]{1,0:T(8,128)(2,1)S(1)}, u32[]{:S(2)}, u32[]{:S(2)}) collective-permute-start(bf16[192,640]{1,0:T(8,128)(2,1)S(1)} %collective-permute-done.22.refs_4_), channel_id=1, source_target_pairs={{0,1},{1,0},{2,3},{3,2},{4,5},{5,4},{6,7},{7,6},{8,9},{9,8},{10,11... | collective-permute-start | bytes 737288 | tf_op jit(solution)/shard_map/ppermute | solution.py:36
  85.3 1.5 collective-permute-start.25
  95.6 179.9 %all-gather.9.cloned.1.call-start = ((), (), s32[]{:S(2)}) async-start(), calls=%async_computation.1 | async-start | bytes 6488064 | tf_op jit(solution)/shard_map/all_gather | solution.py:509
  96.3 250.4 %all-gather.7.cloned.1.call-start = ((), (), s32[]{:S(2)}) async-start(), calls=%async_computation | async-start | bytes 6488064 | tf_op jit(solution)/shard_map/all_gather | solution.py:509
  97.1 31.2 %collective-permute-start.26 = (bf16[192,512]{1,0:T(8,128)(2,1)}, bf16[192,512]{1,0:T(8,128)(2,1)}, u32[]{:S(2)}, u32[]{:S(2)}) collective-permute-start(bf16[192,512]{1,0:T(8,128)(2,1)} %get-tuple-element.58.refs_0_), channel_id=1, source_target_pairs={{0,8},{8,0},{16,24},{24,16},{1,9},{9,1},{17,25},{25,17},{2,10},{10... | collective-permute-start | bytes 589832 | tf_op jit(solution)/shard_map/ppermute | solution.py:36
  101.8 26.5 %collective-permute-start.27 = (bf16[192,512]{1,0:T(8,128)(2,1)}, bf16[192,512]{1,0:T(8,128)(2,1)}, u32[]{:S(2)}, u32[]{:S(2)}) collective-permute-start(bf16[192,512]{1,0:T(8,128)(2,1)} %get-tuple-element.58.refs_0_), channel_id=1, source_target_pairs={{0,16},{8,24},{16,0},{24,8},{1,17},{9,25},{17,1},{25,9},{2,18},{10... | collective-permute-start | bytes 589832 | tf_op jit(solution)/shard_map/ppermute | solution.py:36
  103.0 25.3 %collective-permute-start.28 = (bf16[192,512]{1,0:T(8,128)(2,1)}, bf16[192,512]{1,0:T(8,128)(2,1)}, u32[]{:S(2)}, u32[]{:S(2)}) collective-permute-start(bf16[192,512]{1,0:T(8,128)(2,1)} %get-tuple-element.58.refs_0_), channel_id=1, source_target_pairs={{0,24},{8,16},{16,8},{24,0},{1,25},{9,17},{17,9},{25,1},{2,26},{10... | collective-permute-start | bytes 589832 | tf_op jit(solution)/shard_map/ppermute | solution.py:36
  104.5 12.6 %collective-permute-start.2 = (f32[8,256]{1,0:T(8,128)S(1)}, f32[8,256]{1,0:T(8,128)S(1)}, u32[]{:S(2)}, u32[]{:S(2)}) collective-permute-start(f32[8,256]{1,0:T(8,128)S(1)} %stack.34.refs_0_), channel_id=1, source_target_pairs={{0,8},{8,0},{16,24},{24,16},{1,9},{9,1},{17,25},{25,17},{2,10},{10... | collective-permute-start | bytes 24584 | tf_op jit(solution)/shard_map/ppermute | solution.py:36
  105.4 21.6 %collective-permute-start.3 = (f32[8,256]{1,0:T(8,128)S(1)}, f32[8,256]{1,0:T(8,128)S(1)}, u32[]{:S(2)}, u32[]{:S(2)}) collective-permute-start(f32[8,256]{1,0:T(8,128)S(1)} %stack.34.refs_0_), channel_id=1, source_target_pairs={{0,16},{8,24},{16,0},{24,8},{1,17},{9,25},{17,1},{25,9},{2,18},{10... | collective-permute-start | bytes 24584 | tf_op jit(solution)/shard_map/ppermute | solution.py:36
  117.1 9.8 %collective-permute-start.4 = (f32[8,256]{1,0:T(8,128)S(1)}, f32[8,256]{1,0:T(8,128)S(1)}, u32[]{:S(2)}, u32[]{:S(2)}) collective-permute-start(f32[8,256]{1,0:T(8,128)S(1)} %stack.34.refs_0_), channel_id=1, source_target_pairs={{0,24},{8,16},{16,8},{24,0},{1,25},{9,17},{17,9},{25,1},{2,26},{10... | collective-permute-start | bytes 24584 | tf_op jit(solution)/shard_map/ppermute | solution.py:36
  119.8 43.0 %slice-start = ((s8[5308416]{0:T(1024)(128)(4,1)}), s8[1114112]{0:T(1024)(128)(4,1)S(1)}, s32[]{:S(2)}) async-start(s8[5308416]{0:T(1024)(128)(4,1)} %bitcast.24), calls=%async_computation.3 | async-start | bytes 2228224
  121.8 41.0 %copy-start.6 = (f32[8,192,128]{2,1,0:T(8,128)S(1)}, f32[8,192,128]{2,1,0:T(8,128)}, u32[]{:S(2)}) copy-start(f32[8,192,128]{2,1,0:T(8,128)} %copy-done.5) | copy-start | bytes 2359300
  140.7 63.9 %copy-start.26 = (bf16[192,512]{1,0:T(8,128)(2,1)}, bf16[192,512]{1,0:T(8,128)(2,1)S(1)}, u32[]{:S(2)}) copy-start(bf16[192,512]{1,0:T(8,128)(2,1)S(1)} %get-tuple-element.91.refs_0_) | copy-start | bytes 589828
  140.7 2.7 collective-permute-start.29
  143.6 9.3 %collective-permute-start.30 = (bf16[208,640]{1,0:T(8,128)(2,1)S(1)}, bf16[208,640]{1,0:T(8,128)(2,1)S(1)}, u32[]{:S(2)}, u32[]{:S(2)}) collective-permute-start(bf16[208,640]{1,0:T(8,128)(2,1)S(1)} %get-tuple-element.62), channel_id=1, source_target_pairs={{0,2},{1,3},{2,0},{3,1},{4,6},{5,7},{6,4},{7,5},{8,10},{9,11},{10,... | collective-permute-start | bytes 798728 | tf_op jit(solution)/shard_map/ppermute | solution.py:36
  145.4 14.3 %collective-permute-start.31 = (bf16[208,640]{1,0:T(8,128)(2,1)S(1)}, bf16[208,640]{1,0:T(8,128)(2,1)S(1)}, u32[]{:S(2)}, u32[]{:S(2)}) collective-permute-start(bf16[208,640]{1,0:T(8,128)(2,1)S(1)} %get-tuple-element.63), channel_id=1, source_target_pairs={{0,4},{1,5},{2,6},{3,7},{4,0},{5,1},{6,2},{7,3},{8,12},{9,13},{10,... | collective-permute-start | bytes 798728 | tf_op jit(solution)/shard_map/ppermute | solution.py:36
  146.5 16.3 %collective-permute-start.32 = (bf16[208,640]{1,0:T(8,128)(2,1)S(1)}, bf16[208,640]{1,0:T(8,128)(2,1)S(1)}, u32[]{:S(2)}, u32[]{:S(2)}) collective-permute-start(bf16[208,640]{1,0:T(8,128)(2,1)S(1)} %get-tuple-element.64), channel_id=1, source_target_pairs={{0,6},{1,7},{2,4},{3,5},{4,2},{5,3},{6,0},{7,1},{8,14},{9,15},{10,... | collective-permute-start | bytes 798728 | tf_op jit(solution)/shard_map/ppermute | solution.py:36
  168.2 2.7 collective-permute-start.33
  171.1 9.7 %collective-permute-start.34 = (bf16[208,640]{1,0:T(8,128)(2,1)S(1)}, bf16[208,640]{1,0:T(8,128)(2,1)S(1)}, u32[]{:S(2)}, u32[]{:S(2)}) collective-permute-start(bf16[208,640]{1,0:T(8,128)(2,1)S(1)} %get-tuple-element.72), channel_id=1, source_target_pairs={{0,2},{1,3},{2,0},{3,1},{4,6},{5,7},{6,4},{7,5},{8,10},{9,11},{10,... | collective-permute-start | bytes 798728 | tf_op jit(solution)/shard_map/ppermute | solution.py:36
  173.7 13.9 %collective-permute-start.35 = (bf16[208,640]{1,0:T(8,128)(2,1)S(1)}, bf16[208,640]{1,0:T(8,128)(2,1)S(1)}, u32[]{:S(2)}, u32[]{:S(2)}) collective-permute-start(bf16[208,640]{1,0:T(8,128)(2,1)S(1)} %get-tuple-element.73), channel_id=1, source_target_pairs={{0,4},{1,5},{2,6},{3,7},{4,0},{5,1},{6,2},{7,3},{8,12},{9,13},{10,... | collective-permute-start | bytes 798728 | tf_op jit(solution)/shard_map/ppermute | solution.py:36
  175.5 12.1 %collective-permute-start.36 = (bf16[208,640]{1,0:T(8,128)(2,1)S(1)}, bf16[208,640]{1,0:T(8,128)(2,1)S(1)}, u32[]{:S(2)}, u32[]{:S(2)}) collective-permute-start(bf16[208,640]{1,0:T(8,128)(2,1)S(1)} %get-tuple-element.74), channel_id=1, source_target_pairs={{0,6},{1,7},{2,4},{3,5},{4,2},{5,3},{6,0},{7,1},{8,14},{9,15},{10,... | collective-permute-start | bytes 798728 | tf_op jit(solution)/shard_map/ppermute | solution.py:36
  192.3 2.7 collective-permute-start.37
  195.3 9.3 %collective-permute-start.38 = (bf16[208,640]{1,0:T(8,128)(2,1)S(1)}, bf16[208,640]{1,0:T(8,128)(2,1)S(1)}, u32[]{:S(2)}, u32[]{:S(2)}) collective-permute-start(bf16[208,640]{1,0:T(8,128)(2,1)S(1)} %get-tuple-element.81), channel_id=1, source_target_pairs={{0,2},{1,3},{2,0},{3,1},{4,6},{5,7},{6,4},{7,5},{8,10},{9,11},{10,... | collective-permute-start | bytes 798728 | tf_op jit(solution)/shard_map/ppermute | solution.py:36
  196.8 12.1 %collective-permute-start.39 = (bf16[208,640]{1,0:T(8,128)(2,1)S(1)}, bf16[208,640]{1,0:T(8,128)(2,1)S(1)}, u32[]{:S(2)}, u32[]{:S(2)}) collective-permute-start(bf16[208,640]{1,0:T(8,128)(2,1)S(1)} %get-tuple-element.82), channel_id=1, source_target_pairs={{0,4},{1,5},{2,6},{3,7},{4,0},{5,1},{6,2},{7,3},{8,12},{9,13},{10,... | collective-permute-start | bytes 798728 | tf_op jit(solution)/shard_map/ppermute | solution.py:36
  197.4 13.2 %collective-permute-start.40 = (bf16[208,640]{1,0:T(8,128)(2,1)S(1)}, bf16[208,640]{1,0:T(8,128)(2,1)S(1)}, u32[]{:S(2)}, u32[]{:S(2)}) collective-permute-start(bf16[208,640]{1,0:T(8,128)(2,1)S(1)} %get-tuple-element.83), channel_id=1, source_target_pairs={{0,6},{1,7},{2,4},{3,5},{4,2},{5,3},{6,0},{7,1},{8,14},{9,15},{10,... | collective-permute-start | bytes 798728 | tf_op jit(solution)/shard_map/ppermute | solution.py:36
  198.8 14.2 %collective-permute-start.47 = (bf16[192,512]{1,0:T(8,128)(2,1)S(1)}, bf16[192,512]{1,0:T(8,128)(2,1)S(1)}, u32[]{:S(2)}, u32[]{:S(2)}) collective-permute-start(bf16[192,512]{1,0:T(8,128)(2,1)S(1)} %get-tuple-element.91.refs_0_), channel_id=1, source_target_pairs={{0,8},{8,0},{16,24},{24,16},{1,9},{9,1},{17,25},{25,17},{2,10},{10... | collective-permute-start | bytes 589832 | tf_op jit(solution)/shard_map/ppermute | solution.py:36
  198.8 19.5 %collective-permute-start.48 = (bf16[192,512]{1,0:T(8,128)(2,1)S(1)}, bf16[192,512]{1,0:T(8,128)(2,1)S(1)}, u32[]{:S(2)}, u32[]{:S(2)}) collective-permute-start(bf16[192,512]{1,0:T(8,128)(2,1)S(1)} %get-tuple-element.91.refs_0_), channel_id=1, source_target_pairs={{0,16},{8,24},{16,0},{24,8},{1,17},{9,25},{17,1},{25,9},{2,18},{10... | collective-permute-start | bytes 589832 | tf_op jit(solution)/shard_map/ppermute | solution.py:36
  204.6 18.6 %collective-permute-start.49 = (bf16[192,512]{1,0:T(8,128)(2,1)S(1)}, bf16[192,512]{1,0:T(8,128)(2,1)S(1)}, u32[]{:S(2)}, u32[]{:S(2)}) collective-permute-start(bf16[192,512]{1,0:T(8,128)(2,1)S(1)} %get-tuple-element.91.refs_0_), channel_id=1, source_target_pairs={{0,24},{8,16},{16,8},{24,0},{1,25},{9,17},{17,9},{25,1},{2,26},{10... | collective-permute-start | bytes 589832 | tf_op jit(solution)/shard_map/ppermute | solution.py:36
  208.8 26.6 %collective-permute-start.44 = (bf16[192,512]{1,0:T(8,128)(2,1)}, bf16[192,512]{1,0:T(8,128)(2,1)S(1)}, u32[]{:S(2)}, u32[]{:S(2)}) collective-permute-start(bf16[192,512]{1,0:T(8,128)(2,1)} %get-tuple-element.89.refs_0_), channel_id=1, source_target_pairs={{0,8},{8,0},{16,24},{24,16},{1,9},{9,1},{17,25},{25,17},{2,10},{10... | collective-permute-start | bytes 589832 | tf_op jit(solution)/shard_map/ppermute | solution.py:36
  212.8 23.7 %collective-permute-start.50 = (f32[8,192]{1,0:T(8,128)S(1)}, f32[8,192]{1,0:T(8,128)S(1)}, u32[]{:S(2)}, u32[]{:S(2)}) collective-permute-start(f32[8,192]{1,0:T(8,128)S(1)} %select_maximum_fusion), channel_id=1, source_target_pairs={{0,8},{8,0},{16,24},{24,16},{1,9},{9,1},{17,25},{25,17},{2,10},{10... | collective-permute-start | bytes 18440 | tf_op jit(solution)/shard_map/ppermute | solution.py:36
  213.7 23.0 %collective-permute-start.51 = (f32[8,192]{1,0:T(8,128)S(1)}, f32[8,192]{1,0:T(8,128)S(1)}, u32[]{:S(2)}, u32[]{:S(2)}) collective-permute-start(f32[8,192]{1,0:T(8,128)S(1)} %select_maximum_fusion), channel_id=1, source_target_pairs={{0,16},{8,24},{16,0},{24,8},{1,17},{9,25},{17,1},{25,9},{2,18},{10... | collective-permute-start | bytes 18440 | tf_op jit(solution)/shard_map/ppermute | solution.py:36
  219.0 21.6 %collective-permute-start.52 = (f32[8,192]{1,0:T(8,128)S(1)}, f32[8,192]{1,0:T(8,128)S(1)}, u32[]{:S(2)}, u32[]{:S(2)}) collective-permute-start(f32[8,192]{1,0:T(8,128)S(1)} %select_maximum_fusion), channel_id=1, source_target_pairs={{0,24},{8,16},{16,8},{24,0},{1,25},{9,17},{17,9},{25,1},{2,26},{10... | collective-permute-start | bytes 18440 | tf_op jit(solution)/shard_map/ppermute | solution.py:36
  223.8 39.9 %collective-permute-start.45 = (bf16[192,512]{1,0:T(8,128)(2,1)}, bf16[192,512]{1,0:T(8,128)(2,1)S(1)}, u32[]{:S(2)}, u32[]{:S(2)}) collective-permute-start(bf16[192,512]{1,0:T(8,128)(2,1)} %get-tuple-element.89.refs_0_), channel_id=1, source_target_pairs={{0,16},{8,24},{16,0},{24,8},{1,17},{9,25},{17,1},{25,9},{2,18},{10... | collective-permute-start | bytes 589832 | tf_op jit(solution)/shard_map/ppermute | solution.py:36
  236.1 27.6 %collective-permute-start.46 = (bf16[192,512]{1,0:T(8,128)(2,1)}, bf16[192,512]{1,0:T(8,128)(2,1)S(1)}, u32[]{:S(2)}, u32[]{:S(2)}) collective-permute-start(bf16[192,512]{1,0:T(8,128)(2,1)} %get-tuple-element.89.refs_0_), channel_id=1, source_target_pairs={{0,24},{8,16},{16,8},{24,0},{1,25},{9,17},{17,9},{25,1},{2,26},{10... | collective-permute-start | bytes 589832 | tf_op jit(solution)/shard_map/ppermute | solution.py:36
  236.4 50.3 %collective-permute-start.41 = (bf16[192,512]{1,0:T(8,128)(2,1)}, bf16[192,512]{1,0:T(8,128)(2,1)S(1)}, u32[]{:S(2)}, u32[]{:S(2)}) collective-permute-start(bf16[192,512]{1,0:T(8,128)(2,1)} %get-tuple-element.87.refs_0_), channel_id=1, source_target_pairs={{0,8},{8,0},{16,24},{24,16},{1,9},{9,1},{17,25},{25,17},{2,10},{10... | collective-permute-start | bytes 589832 | tf_op jit(solution)/shard_map/ppermute | solution.py:36
  236.7 50.1 %collective-permute-start.42 = (bf16[192,512]{1,0:T(8,128)(2,1)}, bf16[192,512]{1,0:T(8,128)(2,1)S(1)}, u32[]{:S(2)}, u32[]{:S(2)}) collective-permute-start(bf16[192,512]{1,0:T(8,128)(2,1)} %get-tuple-element.87.refs_0_), channel_id=1, source_target_pairs={{0,16},{8,24},{16,0},{24,8},{1,17},{9,25},{17,1},{25,9},{2,18},{10... | collective-permute-start | bytes 589832 | tf_op jit(solution)/shard_map/ppermute | solution.py:36
  240.5 46.2 %collective-permute-start.43 = (bf16[192,512]{1,0:T(8,128)(2,1)}, bf16[192,512]{1,0:T(8,128)(2,1)S(1)}, u32[]{:S(2)}, u32[]{:S(2)}) collective-permute-start(bf16[192,512]{1,0:T(8,128)(2,1)} %get-tuple-element.87.refs_0_), channel_id=1, source_target_pairs={{0,24},{8,16},{16,8},{24,0},{1,25},{9,17},{17,9},{25,1},{2,26},{10... | collective-permute-start | bytes 589832 | tf_op jit(solution)/shard_map/ppermute | solution.py:36
  (35 other events, 361.8 us)
Sparse Core Ops, SparseCore 0:
  95.7 85.3 all-gather.10
  184.0 91.4 all-gather.8
  278.3 68.3 all-gather.6

commit v2 on v1

v2 whole, which is shorter than its diff:
```python
import functools
import math

import jax
import jax.numpy as jnp
from jax import lax
from jax.experimental import pallas as pl
from jax.experimental.pallas import tpu as pltpu
from jax.sharding import PartitionSpec as P

LAYERS = 3
EPSILON = 1e-06
EDGE = 64
SPARE = 56
CHUNK = 384
ROWS = 16
K0 = math.sqrt(2.0 / math.pi)
K1 = K0 * 0.044715
F32 = jnp.float32
BF16 = jnp.bfloat16

VMEM = pl.BlockSpec(memory_space=pltpu.VMEM)
SMEM = pl.BlockSpec(memory_space=pltpu.SMEM)
HBM = pl.BlockSpec(memory_space=pltpu.HBM)


def params(mib=24):
    return pltpu.CompilerParams(vmem_limit_bytes=mib * 1024 * 1024)


def cost(flops, nbytes, special=0):
    return pl.CostEstimate(flops=flops, bytes_accessed=nbytes, transcendentals=special)


def tie(first, then):
    out = lax.optimization_barrier((tuple(first), tuple(then)))
    return list(out[0]), list(out[1])


def reach_of(layer):
    return 2 ** (layer + 3)


def swap(x, axis, mask):
    count = lax.axis_size(axis)
    return lax.ppermute(x, axis, [(i, i ^ mask) for i in range(count)])


def gather_tp(x):
    if lax.axis_size("tp") == 8:
        far = [x] + [swap(x, "tp", m) for m in (2, 4, 6)]
        near = [swap(v, "tp", 1) for v in far]
        return [v for pair in zip(far, near) for v in pair]
    whole = lax.all_gather(x, "tp", axis=0)
    return [whole[i] for i in range(whole.shape[0])]


def tp_order(me):
    count = lax.axis_size("tp")
    steps = jnp.arange(count, dtype=jnp.int32)
    return me ^ steps if count == 8 else steps


def gather_seq(x):
    if lax.axis_size("seq") == 4:
        one = swap(x, "seq", 1)
        two = swap(x, "seq", 2)
        return [x, one, two, swap(x, "seq", 3)]
    whole = lax.all_gather(x, "seq", axis=0)
    return [whole[i] for i in range(whole.shape[0])]


def seq_order(me):
    count = lax.axis_size("seq")
    steps = jnp.arange(count, dtype=jnp.int32)
    return me ^ steps if count == 4 else steps


def roll(x, shift):
    shift = shift % x.shape[1]
    return x if shift == 0 else pltpu.roll(x, shift, 1)


def position(shape, dim, length):
    at = lax.broadcasted_iota(jnp.int32, shape, dim)
    return jnp.where(at < length + EDGE, at, at - (length + 2 * EDGE))


def in_sequence(seq_at, width, length, total):
    at = position((1, width), 1, length) + seq_at * length
    return (at >= 0) & (at < total)


def halo_kernel(meta, tower_ref, first_ref, second_ref, gain_ref, halo_ref, window_ref, *, n_tp, n_seq):
    ch = tower_ref.shape[0]
    even = lax.rem(meta[n_tp + n_seq + 1], 2) == 0
    first = first_ref[...].astype(F32)
    second = second_ref[...].astype(F32)
    right = jnp.where(even, first, second)
    left = jnp.where(even, second, first)
    lane = lax.broadcasted_iota(jnp.int32, (ch, 128), 1)
    low = lane < EDGE
    halo = jnp.where(low, right[:, :128], roll(left[:, :128], EDGE))
    gains = gain_ref[...]
    high = gains.astype(BF16).astype(F32)
    rest = gains - high
    middle = rest.astype(BF16).astype(F32)
    last = rest - middle
    for k, part in enumerate((high, middle, last)):
        for layer in range(LAYERS):
            halo = jnp.where(lane == SPARE + k * LAYERS + layer, part[:, layer : layer + 1], halo)
    halo_ref[...] = halo.astype(BF16)
    length = tower_ref.shape[1]
    window_ref[:, :length] = tower_ref[...]
    th = jnp.where(low, roll(right[:, :128], EDGE), left[:, :128])
    tl = jnp.where(low, right[:, 128:], roll(left[:, 128:], EDGE))
    window_ref[:, length:] = th + tl


def lookup_kernel(meta, table_ref, *refs, n_tp, n_seq):
    pieces = refs[:n_seq]
    rec_ref, rows_ref = refs[n_seq:]
    count = pieces[0].shape[1]
    for m in range(n_seq):
        at = meta[n_tp + m]
        rec_ref[:, pl.ds(pl.multiple_of(at * count, 128), count)] = pieces[m][...]
    table = table_ref[...]
    ch, tissues = table.shape
    high = table.astype(BF16)
    rest = table - high.astype(F32)
    middle = rest.astype(BF16)
    last = (rest - middle.astype(F32)).astype(BF16)
    stack = jnp.concatenate([high, middle, last], axis=0)
    which = rec_ref[2:3, :].astype(jnp.int32)
    hit = lax.broadcasted_iota(jnp.int32, (tissues, which.shape[1]), 0) == which
    got = jnp.dot(stack, jnp.where(hit, 1.0, 0.0).astype(BF16), preferred_element_type=F32)
    rows_ref[...] = got[:ch] + (got[ch : 2 * ch] + got[2 * ch :])


def load(piece, rows):
    if isinstance(piece, tuple):
        return jnp.concatenate([part[rows, :].astype(F32) for part in piece], axis=1)
    return piece[rows, :].astype(F32)


def blocks_of(refs, layer, n_tp):
    if layer == 0:
        return list(zip(refs[:n_tp], refs[n_tp : 2 * n_tp])), refs[2 * n_tp :]
    return list(refs[:n_tp]), refs[n_tp:]


def forward_kernel(meta, w_ref, *refs, layer, n_tp, n_seq, length):
    own = refs[:2] if layer == 0 else refs[0]
    pieces, refs = blocks_of(refs[2 if layer == 0 else 1 :], layer, n_tp)
    if layer == 0:
        state_ref, inverse_ref, hidden_ref, gain_ref, *refs = refs
    else:
        gain_ref, *refs = refs
        if layer == 1:
            before_ref, *refs = refs
        state_ref, inverse_ref, *refs = refs
        *hidden_refs, held, weights, sem = refs
    if layer == 0:
        held, weights, sem = refs
    _, ch, width = held.shape
    channels = ch * n_tp
    reach = reach_of(layer)
    me, seq_at = meta[n_tp + n_seq], meta[n_tp + n_seq + 1]
    copy = pltpu.make_async_copy(w_ref.at[layer], weights, sem)
    copy.start()

    def add_power(j, acc):
        rows = pl.ds(pl.multiple_of(j * ROWS, ROWS), ROWS)
        for piece in pieces:
            x = load(piece, rows)
            sq = x * x
            for i in range(0, ROWS, 8):
                acc = acc + sq[i : i + 8]
        return acc

    acc = lax.fori_loop(0, ch // ROWS, add_power, jnp.zeros((8, width), F32))
    power = jnp.sum(acc, axis=0, keepdims=True) / channels
    inverse = 1.0 / jnp.sqrt(power + EPSILON)
    inverse_ref[...] = jnp.broadcast_to(inverse, (8, width))

    def activate(j, carry):
        rows = pl.ds(pl.multiple_of(j * ROWS, ROWS), ROWS)
        for m, piece in enumerate(pieces):
            at = meta[m]
            x = load(piece, rows)
            if layer == 0:
                halo = x[:, length:]
                cols = [
                    halo[:, SPARE + l : SPARE + l + 1]
                    + (
                        halo[:, SPARE + LAYERS + l : SPARE + LAYERS + l + 1]
                        + halo[:, SPARE + 2 * LAYERS + l : SPARE + 2 * LAYERS + l + 1]
                    )
                    for l in range(LAYERS)
                ]
                lane = lax.broadcasted_iota(jnp.int32, (ROWS, 128), 1)
                gain_ref[at, rows, :] = jnp.where(lane == 0, cols[0], jnp.where(lane == 1, cols[1], cols[2]))
                gain = cols[0]
            else:
                gain = gain_ref[at, rows, layer : layer + 1]
            pre = x * gain * inverse
            th = jnp.tanh(pre * (K0 + K1 * (pre * pre)))
            held[at, rows, :] = (pre * (0.5 + 0.5 * th)).astype(BF16)
        return carry

    lax.fori_loop(0, ch // ROWS, activate, 0)
    if layer == 0:
        hidden_ref[...] = held[me, :, :length]
    elif layer == 1:
        hidden_refs[0][:ch, :] = before_ref[...]
        hidden_refs[0][ch:, :] = held[me, :, :length]
    elif len(hidden_refs) == 1:
        hidden_refs[0][...] = held[me, :, :length]
    else:
        core = lax.rem(me, 2)
        for i in range(n_tp // 2):
            hidden_refs[0][i] = held[2 * i + core, :, :length]
            hidden_refs[1][i] = held[2 * i + 1 - core, :, :length]
    copy.wait()
    every = held[...].reshape(channels, width)
    total = load(own, slice(None))
    for tap in range(3):
        part = jnp.dot(weights[tap * ch : (tap + 1) * ch, :], every, preferred_element_type=F32)
        total = total + roll(part, (1 - tap) * reach)
    total = jnp.where(in_sequence(seq_at, width, length, n_seq * length), total, 0.0).astype(BF16)
    state_ref[...] = total[:, : state_ref.shape[1]]


def slope_kernel(meta, gain_ref, inverse_ref, *refs, layer, n_tp):
    pieces, (slope_ref, held, sems) = blocks_of(refs, layer, n_tp)
    _, ch, width = held.shape
    inverse = inverse_ref[0:1, :width]
    copies = []
    for m, piece in enumerate(pieces):
        at = meta[m]

        def derive(j, carry, m=m, piece=piece, at=at):
            rows = pl.ds(pl.multiple_of(j * ROWS, ROWS), ROWS)
            scaled = load(piece, rows)[:, :width] * gain_ref[at, rows, layer : layer + 1]
            pre = scaled * inverse
            sq = pre * pre
            th = jnp.tanh(pre * (K0 + K1 * sq))
            half = 0.5 + 0.5 * th
            hidden = pre * half
            slope = half + (hidden - hidden * th) * (K0 + (3.0 * K1) * sq)
            held[m, rows, :] = (slope * scaled).astype(BF16)
            return carry

        lax.fori_loop(0, ch // ROWS, derive, 0, unroll=2)
        copies.append(pltpu.make_async_copy(held.at[m], slope_ref.at[at], sems.at[m]))
        copies[-1].start()
    for copy in copies:
        copy.wait()


def send_back(layer, upstream, meta, weights, slopes, taps, grad_ref, out_refs, score, n_tp, n_seq, length):
    ch, width = upstream.shape
    wide = taps.shape[1]
    reach = reach_of(layer)
    me, seq_at = meta[n_tp + n_seq], meta[n_tp + n_seq + 1]
    grad = jnp.where(in_sequence(seq_at, width, length, n_seq * length), upstream, 0.0)
    grad = grad.astype(BF16).astype(F32)
    grad_ref[...] = grad[:, :length].astype(BF16)
    for tap in range(3):
        taps[tap * ch : (tap + 1) * ch, :] = roll(grad, (tap - 1) * reach)[:, :wide].astype(BF16)
    for copy in slopes[1:]:
        copy.wait()
    inner = jnp.zeros((8, wide), F32)
    parts = CHUNK // ch
    chunks = ch * n_tp // CHUNK
    for r in range(chunks):
        at = (me // 2) ^ r if n_tp == 8 else r
        cols = pl.ds(pl.multiple_of(at * CHUNK, 128), CHUNK)
        part = lax.dot_general(weights[:, cols], taps[...], (((0,), (0,)), ((), ())), preferred_element_type=F32)
        for q in range(parts):
            prod = part[q * ch : (q + 1) * ch] * slopes[0][at * parts + q].astype(F32)
            inner = inner + jnp.sum(prod.reshape(ch // 8, 8, wide), axis=0)
        if n_tp == 8:
            keep_ref, send_ref = out_refs
            zero = lax.rem(me, 2) == 0
            keep_ref[r] = jnp.where(zero, part[:ch], part[ch:]).astype(BF16)
            send_ref[r * ch : (r + 1) * ch, :] = jnp.where(zero, part[ch:], part[:ch]).astype(BF16)
        else:
            for q in range(parts):
                out_refs[0][at * parts + q] = part[q * ch : (q + 1) * ch].astype(BF16)
    row = lax.broadcasted_iota(jnp.int32, (8, wide), 0)
    extra = jnp.where(row == 0, jnp.sum(inner, axis=0, keepdims=True), 0.0)
    if score is not None:
        score = jnp.concatenate([score, jnp.zeros((1, wide - score.shape[1]), F32)], axis=1)
        extra = jnp.where(row == 1, score, extra)
    if n_tp == 8:
        out_refs[1][n_tp // 2 * ch :, :] = split_rows(extra)
    else:
        out_refs[1][...] = extra


def split_rows(x):
    high = x.astype(BF16).astype(F32)
    return jnp.concatenate([high, x - high], axis=0).astype(BF16)


def join_rows(x):
    x = x.astype(F32)
    return x[:8] + x[8:]


def fetch(layer, w_ref, slope_ref, weights, slopes, sems):
    copies = [
        pltpu.make_async_copy(w_ref.at[layer], weights, sems.at[0]),
        pltpu.make_async_copy(slope_ref, slopes, sems.at[1]),
    ]
    for copy in copies:
        copy.start()
    return [slopes] + copies


def junction_kernel(meta, w_ref, slope_ref, window_ref, rec_ref, rows_ref, *refs, n_tp, n_seq, root):
    pieces, refs = refs[:n_seq], refs[n_seq:]
    up_ref, grad_ref, *refs = refs
    *out_refs, weights, taps, slopes, donors, sems = refs
    ch, length = pieces[0].shape
    width = window_ref.shape[1]
    count = rec_ref.shape[1]
    share = count // n_seq
    seq_at = meta[n_tp + n_seq + 1]
    slopes = fetch(LAYERS - 1, w_ref, slope_ref, weights, slopes, sems)
    donor = rec_ref[0:1, :].astype(jnp.int32)
    accept = rec_ref[1:2, :].astype(jnp.int32)
    weight = rec_ref[3:4, :] / root
    place = lax.broadcasted_iota(jnp.int32, (length, count), 0)
    accepts = jnp.zeros((ch, count), F32)
    for m in range(n_seq):
        at = meta[n_tp + m]
        cols = pl.ds(pl.multiple_of(at * share, 128), share)
        block = pieces[m][...]
        mine = rec_ref[0:1, cols].astype(jnp.int32) - at * length
        hit = lax.broadcasted_iota(jnp.int32, (length, share), 0) == mine
        donors[:, cols] = jnp.dot(block, jnp.where(hit, 1.0, 0.0).astype(BF16), preferred_element_type=F32)
        hit = place == accept - at * length
        accepts = accepts + jnp.dot(block, jnp.where(hit, 1.0, 0.0).astype(BF16), preferred_element_type=F32)
    rows = rows_ref[...]
    product = donors[...] * accepts * rows
    scored = jnp.sum(product, axis=0, keepdims=True) / root
    score = jnp.zeros((1, share), F32)
    for m in range(n_seq):
        score = jnp.where(seq_at == m, scored[:, m * share : (m + 1) * share], score)
    scale = rows * weight
    upstream = window_ref[...]
    spot = position((width, count), 0, length) + seq_at * length
    for values, where in ((accepts * scale, donor), (donors[...] * scale, accept)):
        high = values.astype(BF16)
        low = (values - high.astype(F32)).astype(BF16)
        hit = jnp.where(spot == where, 1.0, 0.0).astype(BF16)
        both = lax.dot_general(
            jnp.concatenate([high, low], axis=0), hit, (((1,), (1,)), ((), ())), preferred_element_type=F32
        )
        upstream = upstream + (both[:ch] + both[ch:])
    up_ref[...] = upstream
    send_back(LAYERS - 1, upstream, meta, weights, slopes, taps, grad_ref, out_refs, score, n_tp, n_seq, length)


def pair_kernel(keep_ref, send_ref, got_ref, own_ref, *far_refs):
    count, ch, width = keep_ref.shape
    extra = join_rows(send_ref[count * ch :, :]) + join_rows(got_ref[count * ch :, :])
    split = split_rows(extra)
    for r in range(count):
        total = keep_ref[r].astype(F32) + got_ref[r * ch : (r + 1) * ch, :].astype(F32)
        if r == 0:
            own_ref[:ch, :] = total
            own_ref[ch:, :] = join_rows(split)
        else:
            far_refs[r - 1][:ch, :] = total.astype(BF16)
            far_refs[r - 1][ch:, :] = split


def backward_kernel(meta, *refs, layer, n_far, n_tp, n_seq, length):
    last = layer == 0
    if last:
        slopes = None
    else:
        w_ref, slope_ref, *refs = refs
        *refs, weights, taps, slopes, sems = refs
        slopes = fetch(layer - 1, w_ref, slope_ref, weights, slopes, sems)
    own_ref, refs = refs[0], refs[1:]
    far, refs = refs[:n_far], refs[n_far:]
    up_ref, state_ref, inverse_ref, gain_ref, *refs = refs
    out_ref, part_ref, *refs = refs
    if not last:
        grad_ref, *out_refs = refs
        if layer == LAYERS - 1:
            score_ref, *out_refs = out_refs
    ch, width = state_ref.shape
    channels = ch * n_tp
    sums = [own_ref[ch:, :]] + [join_rows(f[ch:, :]) for f in far]
    extra = (sums[0] + sums[1]) + (sums[2] + sums[3]) if n_far else sums[0]
    inner = extra[0:1, :]
    if layer == LAYERS - 1:
        score_ref[...] = extra
    inverse = inverse_ref[0:1, :width]
    gain = gain_ref[:, layer : layer + 1]
    back = own_ref[:ch, :]
    for f in far:
        back = back + f[:ch, :].astype(F32)
    x = state_ref[...].astype(F32)
    pre = x * gain * inverse
    sq = pre * pre
    th = jnp.tanh(pre * (K0 + K1 * sq))
    half = 0.5 + 0.5 * th
    back = back * (half + (pre * half) * (1.0 - th) * (K0 + (3.0 * K1) * sq))
    mine = back * x * inverse
    part = jnp.sum(mine[:, :length], axis=1, keepdims=True)
    part_ref[...] = jnp.broadcast_to(part, part_ref.shape)
    upstream = up_ref[:, :width] + (inverse * gain) * back - x * (inverse * inverse * inverse * inner / channels)
    out_ref[...] = upstream
    if not last:
        send_back(layer - 1, upstream, meta, weights, slopes, taps, grad_ref, out_refs, None, n_tp, n_seq, length)


def weight_kernel(meta, *refs, layer, n_tp, n_seq, swapped):
    pieces, refs = refs[:n_seq], refs[n_seq:]
    count = 2 * n_seq if swapped else 1
    sources, refs = refs[:count], refs[count:]
    out_ref, whole, taps, held, done, in_sems, out_sems = refs[-7:]
    ch, length = pieces[0].shape
    reach = reach_of(layer)
    total = n_seq * length
    parts = CHUNK // ch
    chunks = ch * n_tp // CHUNK
    core = lax.rem(meta[n_tp + n_seq], 2)

    def arrive(i):
        slot = i % 2
        if not swapped:
            source = sources[0]
            if len(source.shape) == 5:
                source = source.at[:, i * parts : (i + 1) * parts, layer]
            else:
                source = source.at[:, i * parts : (i + 1) * parts]
            return [pltpu.make_async_copy(source, held.at[slot], in_sems.at[slot, 0])]
        copies = []
        for m in range(n_seq):
            for q in range(2):
                where = core if q == 0 else 1 - core
                copies.append(
                    pltpu.make_async_copy(
                        sources[2 * m + q].at[i], held.at[slot, meta[n_tp + m], where], in_sems.at[slot, 2 * m + q]
                    )
                )
        return copies

    def leave(i):
        cols = pl.ds(i * CHUNK, CHUNK)
        return pltpu.make_async_copy(done.at[i % 2], out_ref.at[layer, :, :, cols], out_sems.at[i % 2])

    for copy in arrive(0):
        copy.start()
    for m in range(n_seq):
        at = meta[n_tp + m]
        whole[:, pl.ds(pl.multiple_of(at * length, 128), length)] = pieces[m][...]
    grad = whole[...].astype(F32)
    lane = lax.broadcasted_iota(jnp.int32, (1, total), 1)
    taps[:ch, :] = jnp.where(lane < total - reach, roll(grad, -reach), 0.0).astype(BF16)
    taps[ch : 2 * ch, :] = whole[...]
    taps[2 * ch :, :] = jnp.where(lane >= reach, roll(grad, reach), 0.0).astype(BF16)
    for i in range(chunks):
        if i + 1 < chunks:
            for copy in arrive(i + 1):
                copy.start()
        for copy in arrive(i):
            copy.wait()
        acc = None
        for s in range(n_seq):
            part = lax.dot_general(
                taps[:, s * length : (s + 1) * length],
                held[i % 2, s].reshape(CHUNK, length),
                (((1,), (1,)), ((), ())),
                preferred_element_type=F32,
            )
            acc = part if acc is None else acc + part
        if i >= 2:
            leave(i - 2).wait()
        done[i % 2] = acc.reshape(3, ch, CHUNK)
        leave(i).start()
    for i in range(max(0, chunks - 2), chunks):
        leave(i).wait()


def local(
    sequence_in,
    conv_weight,
    norm_gain,
    tissue_scale,
    donor_offset,
    acceptor_owner,
    acceptor_offset,
    tissue,
    tower_grad,
    score_grad,
):
    ch, length = sequence_in.shape
    n_tp, n_seq = lax.axis_size("tp"), lax.axis_size("seq")
    channels, total = ch * n_tp, length * n_seq
    width = length + 2 * EDGE
    share = donor_offset.shape[0]
    count = share * n_seq
    paired = n_tp == 8
    swapped = paired and n_seq == 4
    n_far = 3 if paired else 0
    me = lax.axis_index("tp").astype(jnp.int32)
    seq_at = lax.axis_index("seq").astype(jnp.int32)
    meta = jnp.concatenate([tp_order(me), seq_order(seq_at), jnp.stack([me, seq_at])])
    sizes = dict(n_tp=n_tp, n_seq=n_seq)
    weights = conv_weight.transpose(0, 2, 1, 3).reshape(LAYERS, 3 * ch, channels)
    conv_flops = 6 * ch * channels * width

    def call(kernel, inputs, shapes, scratch=(), hbm_in=(), hbm_out=(), estimate=None, mib=24, **kw):
        return pl.pallas_call(
            kernel,
            out_shape=list(shapes),
            in_specs=[SMEM] + [HBM if i in hbm_in else VMEM for i in range(len(inputs))],
            out_specs=[HBM if i in hbm_out else VMEM for i in range(len(shapes))],
            scratch_shapes=list(scratch),
            compiler_params=params(mib),
            cost_estimate=estimate,
            **kw,
        )(meta, *inputs)

    def array(shape, dtype=BF16):
        return jax.ShapeDtypeStruct(shape, dtype)

    high = lax.reduce_precision(tower_grad, 8, 7)
    low = tower_grad - high

    def edge(lanes):
        return jnp.concatenate(
            [
                sequence_in[:, lanes],
                high[:, lanes].astype(BF16),
                low[:, lanes].astype(BF16),
                jnp.zeros((ch, EDGE), BF16),
            ],
            axis=1,
        )

    left, right = edge(slice(0, EDGE)), edge(slice(length - EDGE, length))
    even = seq_at % 2 == 0
    first = lax.ppermute(jnp.where(even, right, left), "seq", [(i, i ^ 1) for i in range(n_seq)])
    pairs = [(i, i + 1) for i in range(1, n_seq - 1, 2)]
    second = lax.ppermute(jnp.where(even, left, right), "seq", pairs + [(j, i) for i, j in pairs])
    gain_cols = jnp.pad(norm_gain.T, ((0, 0), (0, 128 - LAYERS)))
    halo, window = call(
        functools.partial(halo_kernel, **sizes),
        [tower_grad, first, second, gain_cols],
        [array((ch, 128)), array((ch, width), F32)],
        name="halo",
    )

    def forward(layer, own, pieces, extra, shapes):
        inputs = [weights, *own, *pieces, *extra]
        return call(
            functools.partial(forward_kernel, layer=layer, length=length, **sizes),
            inputs,
            shapes,
            scratch=[
                pltpu.VMEM((n_tp, ch, width), BF16),
                pltpu.VMEM((3 * ch, channels), BF16),
                pltpu.SemaphoreType.DMA,
            ],
            hbm_in=(0,),
            estimate=cost(conv_flops, 4 * channels * width, channels * width),
            name="forward",
        )

    def slope(layer, pieces, inverse):
        wide = length if layer == 0 else width
        return call(
            functools.partial(slope_kernel, layer=layer, n_tp=n_tp),
            [gains, inverse, *pieces],
            [array((n_tp, ch, wide))],
            scratch=[pltpu.VMEM((n_tp, ch, wide), BF16), pltpu.SemaphoreType.DMA((n_tp,))],
            hbm_out=(0,),
            estimate=cost(40 * channels * wide, 4 * channels * wide, channels * wide),
            name="slope",
        )[0]

    blocks0 = gather_tp(sequence_in) + gather_tp(halo)
    state1, inverse0, hidden0, gains = forward(
        0,
        [sequence_in, halo],
        blocks0,
        [],
        [array((ch, width)), array((8, width), F32), array((ch, length)), array((n_tp, ch, 128), F32)],
    )

    record = jnp.stack(
        [
            (donor_offset + seq_at * length).astype(F32),
            (acceptor_owner[:, 0] * length + acceptor_offset).astype(F32),
            tissue.astype(F32),
            score_grad,
        ]
        + [jnp.zeros((share,), F32)] * 4
    )
    table = lax.dynamic_slice_in_dim(tissue_scale, me * ch, ch, 1).T
    table = jnp.pad(table, ((0, 0), (0, -table.shape[1] % 128)))
    records, rows = call(
        functools.partial(lookup_kernel, **sizes),
        [table, *gather_seq(record)],
        [array((8, count), F32), array((ch, count), F32)],
        name="lookup",
    )

    blocks1 = gather_tp(state1)
    slope0 = slope(0, blocks0, inverse0)
    blocks1, (records, rows, slope0) = tie(blocks1, [records, rows, slope0])
    state2, inverse1, hidden = forward(
        1, [state1], blocks1, [gains, hidden0], [array((ch, width)), array((8, width), F32), array((2 * ch, length))]
    )
    every = lax.all_gather(hidden, ("seq", "tp"), axis=0).reshape(n_seq, n_tp, 2, ch, length)

    blocks2 = gather_tp(state2)
    slope1 = slope(1, blocks1, inverse1)
    blocks2, (slope1,) = tie(blocks2, [slope1])
    half = array((n_tp // 2, ch, length))
    state3, inverse2, *halves = forward(
        2,
        [state2],
        blocks2,
        [gains],
        [array((ch, length)), array((8, width), F32)] + ([half, half] if swapped else [array((ch, length))]),
    )
    slope2 = slope(2, blocks2, inverse2)

    def product_shapes(layer):
        wide = length if layer == 0 else width
        if paired:
            return [array((n_tp // 2, ch, wide)), array((n_tp // 2 * ch + 16, wide))]
        return [array((n_tp, ch, wide)), array((8, wide), F32)]

    def scratch(layer):
        wide = length if layer == 0 else width
        return [
            pltpu.VMEM((3 * ch, channels), BF16),
            pltpu.VMEM((3 * ch, wide), BF16),
            pltpu.VMEM((n_tp, ch, wide), BF16),
        ]

    def reduce_tp(products):
        if not paired:
            whole, extra = products
            own = lax.psum_scatter(whole.reshape(channels, -1), "tp", scatter_dimension=0, tiled=True)
            return [jnp.concatenate([own.astype(F32), lax.psum(extra, "tp")], axis=0)]
        keep, send = products
        wide = keep.shape[2]
        got = swap(send, "tp", 1)
        far = array((ch + 16, wide))
        own, *far = pl.pallas_call(
            pair_kernel,
            out_shape=[array((ch + 8, wide), F32), far, far, far],
            in_specs=[VMEM] * 3,
            out_specs=[VMEM] * 4,
            compiler_params=params(),
            name="pair",
        )(keep, send, got)
        return [own] + [swap(v, "tp", 2 * r + 2) for r, v in enumerate(far)]

    pieces = gather_seq(state3)
    pieces, halves = tie(pieces, halves)
    upstream, grad2, *products = call(
        functools.partial(junction_kernel, root=math.sqrt(channels), **sizes),
        [weights, slope2, window, records, rows, *pieces],
        [array((ch, width), F32), array((ch, length))] + product_shapes(2),
        scratch=scratch(2) + [pltpu.VMEM((ch, count), F32), pltpu.SemaphoreType.DMA((2,))],
        hbm_in=(0, 1),
        estimate=cost(4 * conv_flops, 4 * channels * width),
        mib=32,
        name="junction",
    )

    if swapped:
        one, two = swap(halves[0], "seq", 1), swap(halves[0], "seq", 2)
    else:
        last = [lax.all_gather(halves[0], ("seq", "tp"), axis=0).reshape(n_seq, n_tp, ch, length)]

    def backward(layer, sums, upstream, state, inverse, slopes):
        wide = length if layer == 0 else width
        inputs = [*sums, upstream, state, inverse, gain_cols]
        shapes = [array((ch, wide), F32), array((ch, 128), F32)]
        extra, hbm = [], ()
        if layer > 0:
            inputs = [weights, slopes, *inputs]
            hbm = (0, 1)
            shapes.append(array((ch, length)))
            if layer == LAYERS - 1:
                shapes.append(array((8, width), F32))
            shapes += product_shapes(layer - 1)
            extra = scratch(layer - 1) + [pltpu.SemaphoreType.DMA((2,))]
        return call(
            functools.partial(backward_kernel, layer=layer, n_far=n_far, length=length, **sizes),
            inputs,
            shapes,
            scratch=extra,
            hbm_in=hbm,
            estimate=cost(conv_flops, 4 * channels * width),
            name="backward",
        )

    def weigh(layer, grads, sources, before):
        inputs = [*grads, *sources, *before]
        flops = 6 * ch * channels * total
        return call(
            functools.partial(weight_kernel, layer=layer, swapped=len(sources) > 1, **sizes),
            inputs,
            [array((LAYERS, 3, ch, channels), F32)],
            scratch=[
                pltpu.VMEM((ch, total), BF16),
                pltpu.VMEM((3 * ch, total), BF16),
                pltpu.VMEM((2, n_seq, CHUNK // ch, ch, length), BF16),
                pltpu.VMEM((2, 3, ch, CHUNK), F32),
                pltpu.SemaphoreType.DMA((2, 2 * n_seq)),
                pltpu.SemaphoreType.DMA((2,)),
            ],
            hbm_in=range(n_seq, len(inputs)),
            hbm_out=(0,),
            estimate=cost(2 * flops, 2 * channels * total),
            input_output_aliases={len(inputs): 0} if before else {},
            name="weight",
        )[0]

    sums = reduce_tp(products)
    if swapped:
        sums, (one, two) = tie(sums, [one, two])
        three = swap(two, "seq", 1)
    upstream, part2, grad1, score_rows, *products = backward(2, sums, upstream, state2, inverse2, slope1)
    scores = score_rows[1, :share]

    grads = gather_seq(grad2)
    sums = reduce_tp(products)
    if swapped:
        mine = [halves[0], one, two, three]
        near = [halves[1]] + [swap(v, "tp", 1) for v in mine[1:]]
        last = [v for pair in zip(mine, near) for v in pair]
    sums, got = tie(sums, grads + last)
    grads, last = got[:n_seq], got[n_seq:]
    upstream, part1, grad0, *products = backward(1, sums, upstream, state1, inverse1, slope0)

    weight_grad = weigh(2, grads, last, [])
    grads = gather_seq(grad1)
    sums = reduce_tp(products)
    sums, got = tie(sums, grads + [weight_grad, every])
    grads, weight_grad, every = got[:n_seq], got[n_seq], got[n_seq + 1]
    input_grad, part0 = backward(0, sums, upstream, sequence_in, inverse0, None)

    weight_grad = weigh(1, grads, [every], [weight_grad])
    columns = jnp.pad(jnp.stack([p[:, 0] for p in (part0, part1, part2)]), ((0, 8 - LAYERS), (0, 0)))
    pieces = gather_seq(columns)
    if len(pieces) == 4:
        gain_grad = (pieces[0] + pieces[1]) + (pieces[2] + pieces[3])
    else:
        gain_grad = sum(pieces)
    weight_grad = weigh(0, gather_seq(grad0), [every], [weight_grad])
    return (scores, input_grad, weight_grad.transpose(0, 2, 1, 3), gain_grad[:LAYERS])


def solution(mesh):
    return jax.shard_map(
        local,
        mesh=mesh,
        in_specs=(
            P("tp", "seq"),
            P(None, "tp", None, None),
            P(None, "tp"),
            P(),
            P("seq"),
            P("seq", None),
            P("seq"),
            P("seq"),
            P("tp", "seq"),
            P("seq"),
        ),
        out_specs=(P("seq"), P("tp", "seq"), P(None, "tp", None, None), P(None, "tp")),
        check_vma=False,
    )
```

time: 365 us -> 411 us (1.13); the launches traced: 365 us -> 406 us
  Pallas kernels: 69.9 us -> 108 us
  waiting for transfers between devices: 177 us -> 148 us
  starting transfers between devices: 66.8 us -> 80.9 us
  local copies, waits for them, and re-layouts: 34.9 us -> 48.8 us
    all_gather x3 -> x1, waiting for transfers between devices: 71.7 us -> 0.01 us  [local(): lax.all_gather(hidden, ('seq', 'tp'), axis=0)]
    ppermute x51 -> x64, waiting for transfers between devices: 103 us -> 147 us  [swap(): return lax.ppermute(x, axis, [(i, i ^ mask) for i in range(count)])]
    pallas_call x15 -> x18, Pallas kernels: 69.9 us -> 108 us  [the longest x15 108 us: call(): pl.pallas_call(kernel, out_shape=list(shapes), in_specs=[SMEM] + [HBM if...]
    ppermute x51 -> x64, starting transfers between devices: 62.8 us -> 78.1 us  [swap(): return lax.ppermute(x, axis, [(i, i ^ mask) for i in range(count)])]
    unnamed x88 -> x136, local copies, waits for them, and re-layouts: 31.9 us -> 45.1 us
  transfers between devices with their start and end apart: 56 -> 67, of which waited for: 30 -> 25; matrix products, arithmetic and copies ran while one was open for 1% -> 2% of each run, Pallas kernels for 10% -> 23%
where the time goes in v2:
time: 411 us; the launch traced here: 406 us
  waiting for transfers between devices  148 us (36%)
  Pallas kernels  108 us (26%)
  starting transfers between devices  80.9 us (20%)
  local copies, waits for them, and re-layouts  48.8 us (12%)
  between operations  15 us (4%)
  other arithmetic  4.94 us (1%)
    ppermute x64, waiting for transfers between devices, swap(): return lax.ppermute(x, axis, [(i, i ^ mask) for i in range(count)])  147 us
    pallas_call x15, Pallas kernels, call(): pl.pallas_call(kernel, out_shape=list(shapes), in_specs=[SMEM] + [HBM if...  108 us
    ppermute x64, starting transfers between devices, swap(): return lax.ppermute(x, axis, [(i, i ^ mask) for i in range(count)])  78.1 us
    unnamed x136, local copies, waits for them, and re-layouts  45.1 us
  transfers between devices with their start and end apart: 67, of which 25 were waited for; matrix products, arithmetic and copies ran while one was open for 2% of the time, Pallas kernels for 23%

profile of v2, /device:TPU:0, one launch (start us, length us, event | category | flops | bytes accessed | tf_op | source)
XLA Modules:
  0.0 405.9 jit_solution(16311491892534752765)
XLA Ops:
  7.2 3.0 collective-permute-start.3
  10.3 1.5 collective-permute-start.5
  14.1 2.1 collective-permute-start
  21.4 1.9 collective-permute-start.10
  23.3 1.5 collective-permute-start.12
  25.5 3.2 collective-permute-start.14
  28.7 2.1 collective-permute-done.14.refs_16_.refs_14_
  37.6 2.7 copy-done.2
  44.0 7.2 %forward.3 = (bf16[192,640]{1,0:T(8,128)(2,1)S(1)}, f32[8,640]{1,0:T(8,128)S(1)}, bf16[192,512]{1,0:T(8,128)(2,1)S(1)}, f32[8,192,128]{2,1,0:T(8,128)S(1)}) custom-call(s32[14]{0:T(128)S(1)} %pad_add_fusion.meta, bf16[3,576,1536]{2,1,0:T(8,128)(2,1)S(1)} %bitcast.18, bf16[192,512]{1,0:T(8,128)(2,1)S(1)} %copy-done.8, ...), custom_call_target="tpu_custom_call" | custom-call | flops 1132462080 | bytes 3932160 | tf_op jit(solution)/shard_map/forward/pallas_call | solution.py:522
  54.4 1.7 collective-permute-start.17
  56.1 1.8 collective-permute-start.19
  58.7 4.6 %collective-permute-done.17.refs_3_.refs_2_ = bf16[192,640]{1,0:T(8,128)(2,1)} collective-permute-done((bf16[192,640]{1,0:T(8,128)(2,1)S(1)}, bf16[192,640]{1,0:T(8,128)(2,1)}, u32[]{:S(2)}, u32[]{:S(2)}) %collective-permute-start.17) | collective-permute-done | bytes 245792 | tf_op jit(solution)/shard_map/ppermute | solution.py:46
  63.3 5.1 %collective-permute-done.19.refs_5_.refs_4_ = bf16[192,640]{1,0:T(8,128)(2,1)} collective-permute-done((bf16[192,640]{1,0:T(8,128)(2,1)S(1)}, bf16[192,640]{1,0:T(8,128)(2,1)}, u32[]{:S(2)}, u32[]{:S(2)}) %collective-permute-start.19) | collective-permute-done | bytes 245792 | tf_op jit(solution)/shard_map/ppermute | solution.py:46
  72.6 4.7 %collective-permute-start.23 = (f32[8,256]{1,0:T(8,128)S(1)}, f32[8,256]{1,0:T(8,128)S(1)}, u32[]{:S(2)}, u32[]{:S(2)}) collective-permute-start(f32[8,256]{1,0:T(8,128)S(1)} %stack.34.refs_0_), channel_id=1, source_target_pairs={{0,8},{8,0},{16,24},{24,16},{1,9},{9,1},{17,25},{25,17},{2,10},{10... | collective-permute-start | bytes 24584 | tf_op jit(solution)/shard_map/ppermute | solution.py:46
  77.3 1.6 collective-permute-done.23.refs_1_
  79.5 3.3 collective-permute-start.24
  82.9 1.7 collective-permute-done.24.refs_2_
  84.6 2.4 collective-permute-start.25
  90.9 1.5 lookup.1
  106.1 8.1 %slope.3.refs_1_ = bf16[8,192,512]{2,1,0:T(8,128)(2,1)S(1)} custom-call(s32[14]{0:T(128)S(1)} %pad_add_fusion.meta, f32[8,192,128]{2,1,0:T(8,128)S(1)} %get-tuple-element.110.gain_ref.refs_9_, f32[8,640]{1,0:T(8,128)S(1)} %copy-done.53, bf16[192,512]{1,0:T(8,128)(2,1)S(1)} %copy-done.9, bf16[192,512]{1,0:T(8,128)(2,1)S(1)} %copy-done.23, ...), custom_call_target="tpu_custom_call" | custom-call | flops 31457280 | bytes 3145728 | tf_op jit(solution)/shard_map/slope/pallas_call | solution.py:522
  114.2 2.5 copy-done.3
  116.7 6.9 %forward.4 = (bf16[192,640]{1,0:T(8,128)(2,1)S(1)}, f32[8,640]{1,0:T(8,128)S(1)}, bf16[384,512]{1,0:T(8,128)(2,1)}) custom-call(s32[14]{0:T(128)S(1)} %pad_add_fusion.meta, bf16[3,576,1536]{2,1,0:T(8,128)(2,1)S(1)} %bitcast.19, bf16[192,640]{1,0:T(8,128)(2,1)S(1)} %get-tuple-element.112.refs_0_.refs_1_.refs_7_, ...), custom_call_target="tpu_custom_call" | custom-call | flops 1132462080 | bytes 3932160 | tf_op jit(solution)/shard_map/forward/pallas_call | solution.py:522
  123.7 1.5 collective-permute-start.27
  127.5 4.2 %collective-permute-done.27.refs_3_.refs_2_ = bf16[192,640]{1,0:T(8,128)(2,1)S(1)} collective-permute-done((bf16[192,640]{1,0:T(8,128)(2,1)S(1)}, bf16[192,640]{1,0:T(8,128)(2,1)S(1)}, u32[]{:S(2)}, u32[]{:S(2)}) %collective-permute-start.27) | collective-permute-done | bytes 245792 | tf_op jit(solution)/shard_map/ppermute | solution.py:46
  131.6 3.1 collective-permute-done.29.refs_5_.refs_4_
  135.4 10.1 %slope.4.refs_1_ = bf16[8,192,640]{2,1,0:T(8,128)(2,1)S(1)} custom-call(s32[14]{0:T(128)S(1)} %pad_add_fusion.meta, f32[8,192,128]{2,1,0:T(8,128)S(1)} %get-tuple-element.110.gain_ref.refs_9_, f32[8,640]{1,0:T(8,128)S(1)} %get-tuple-element.122.inverse_ref.refs_8_, bf16[192,640]{1,0:T(8,128)(2,1)S(1)} %get-tuple-element.112.refs_0_.refs_1_.refs_7_, ...), custom_call_target="tpu_custom_call" | custom-call | flops 39321600 | bytes 3932160 | tf_op jit(solution)/shard_map/slope/pallas_call | solution.py:522
  145.6 2.5 copy-done.4
  148.1 5.3 %forward.5 = (bf16[192,512]{1,0:T(8,128)(2,1)S(1)}, f32[8,640]{1,0:T(8,128)S(1)}, bf16[4,192,512]{2,1,0:T(8,128)(2,1)S(1)}, bf16[4,192,512]{2,1,0:T(8,128)(2,1)S(1)}) custom-call(s32[14]{0:T(128)S(1)} %pad_add_fusion.meta, bf16[3,576,1536]{2,1,0:T(8,128)(2,1)S(1)} %bitcast.20, bf16[192,640]{1,0:T(8,128)(2,1)S(1)} %get-tuple-element.124.refs_0_.refs_1_.refs_7_, ...), custom_call_target="tpu_custom_call" | custom-call | flops 1132462080 | bytes 3932160 | tf_op jit(solution)/shard_map/forward/pallas_call | solution.py:522
  154.2 2.3 collective-permute-start.34
  156.4 1.5 collective-permute-start.35
  157.9 9.0 %slope.5.slope_ref = bf16[8,192,640]{2,1,0:T(8,128)(2,1)S(1)} custom-call(s32[14]{0:T(128)S(1)} %pad_add_fusion.meta, f32[8,192,128]{2,1,0:T(8,128)S(1)} %get-tuple-element.110.gain_ref.refs_9_, f32[8,640]{1,0:T(8,128)S(1)} %get-tuple-element.132.inverse_ref.refs_8_, bf16[192,640]{1,0:T(8,128)(2,1)S(1)} %get-tuple-element.124.refs_0_.refs_1_.refs_7_, ...), custom_call_target="tpu_custom_call" | custom-call | flops 39321600 | bytes 3932160 | tf_op jit(solution)/shard_map/slope/pallas_call | solution.py:522
  167.0 6.7 %collective-permute-done.33.refs_1_ = bf16[192,512]{1,0:T(8,128)(2,1)S(1)} collective-permute-done((bf16[192,512]{1,0:T(8,128)(2,1)S(1)}, bf16[192,512]{1,0:T(8,128)(2,1)S(1)}, u32[]{:S(2)}, u32[]{:S(2)}) %collective-permute-start.33) | collective-permute-done | bytes 196640 | tf_op jit(solution)/shard_map/ppermute | solution.py:46
  175.0 7.6 %collective-permute-done.35.refs_3_ = bf16[192,512]{1,0:T(8,128)(2,1)S(1)} collective-permute-done((bf16[192,512]{1,0:T(8,128)(2,1)S(1)}, bf16[192,512]{1,0:T(8,128)(2,1)S(1)}, u32[]{:S(2)}, u32[]{:S(2)}) %collective-permute-start.35) | collective-permute-done | bytes 196640 | tf_op jit(solution)/shard_map/ppermute | solution.py:46
  182.6 2.5 copy-done.5
  185.1 7.0 %junction.1 = (f32[192,640]{1,0:T(8,128)S(1)}, bf16[192,512]{1,0:T(8,128)(2,1)S(1)}, bf16[4,192,640]{2,1,0:T(8,128)(2,1)S(1)}, bf16[784,640]{1,0:T(8,128)(2,1)S(1)}) custom-call(s32[14]{0:T(128)S(1)} %pad_add_fusion.meta, bf16[3,576,1536]{2,1,0:T(8,128)(2,1)S(1)} %bitcast.21, bf16[8,192,640]{2,1,0:T(8,128)(2,1)S(1)} %slope.5.slope_ref, ...), custom_call_target="tpu_custom_call" | custom-call | flops 4529848320 | bytes 3932160 | tf_op jit(solution)/shard_map/junction/pallas_call | solution.py:522
  192.2 6.3 %collective-permute-start.40 = (bf16[4,192,512]{2,1,0:T(8,128)(2,1)S(1)}, bf16[4,192,512]{2,1,0:T(8,128)(2,1)S(1)}, u32[]{:S(2)}, u32[]{:S(2)}) collective-permute-start(bf16[4,192,512]{2,1,0:T(8,128)(2,1)S(1)} %get-tuple-element.183.refs_4_), channel_id=1, source_target_pairs={{0,8},{8,0},{16,24},{24,16},{1,9},{9,1},{17,25},{25,17},{2,10},{10... | collective-permute-start | bytes 2359304 | tf_op jit(solution)/shard_map/ppermute | solution.py:46
  198.7 1.6 collective-permute-start.37
  200.3 1.5 collective-permute-start.38
  202.3 58.8 %collective-permute-done.40.refs_6_ = bf16[4,192,512]{2,1,0:T(8,128)(2,1)S(1)} collective-permute-done((bf16[4,192,512]{2,1,0:T(8,128)(2,1)S(1)}, bf16[4,192,512]{2,1,0:T(8,128)(2,1)S(1)}, u32[]{:S(2)}, u32[]{:S(2)}) %collective-permute-start.40) | collective-permute-done | bytes 786464 | tf_op jit(solution)/shard_map/ppermute | solution.py:46
  261.1 2.5 collective-permute-start.51
  263.6 4.1 %backward.3 = (f32[192,640]{1,0:T(8,128)S(1)}, f32[192,128]{1,0:T(8,128)S(1)}, bf16[192,512]{1,0:T(8,128)(2,1)S(1)}, f32[8,640]{1,0:T(8,128)S(1)}, bf16[4,192,64...) custom-call(s32[14]{0:T(128)S(1)} %pad_add_fusion.meta, bf16[3,576,1536]{2,1,0:T(8,128)(2,1)S(1)} %bitcast.24, ...), custom_call_target="tpu_custom_call" | custom-call | flops 1132462080 | bytes 3932160 | tf_op jit(solution)/shard_map/backward/pallas_call | solution.py:522
  268.4 12.9 %collective-permute-done.51.refs_10_ = bf16[4,192,512]{2,1,0:T(8,128)(2,1)S(1)} collective-permute-done((bf16[4,192,512]{2,1,0:T(8,128)(2,1)S(1)}, bf16[4,192,512]{2,1,0:T(8,128)(2,1)S(1)}, u32[]{:S(2)}, u32[]{:S(2)}) %collective-permute-start.51) | collective-permute-done | bytes 786464 | tf_op jit(solution)/shard_map/ppermute | solution.py:46
  281.3 1.7 collective-permute-start.46
  283.0 5.6 %collective-permute-done.46.refs_1_ = bf16[192,512]{1,0:T(8,128)(2,1)S(1)} collective-permute-done((bf16[192,512]{1,0:T(8,128)(2,1)S(1)}, bf16[192,512]{1,0:T(8,128)(2,1)S(1)}, u32[]{:S(2)}, u32[]{:S(2)}) %collective-permute-start.46) | collective-permute-done | bytes 196640 | tf_op jit(solution)/shard_map/ppermute | solution.py:46
  289.3 3.4 collective-permute-start.48
  292.9 12.8 %collective-permute-done.47.refs_2_ = bf16[192,512]{1,0:T(8,128)(2,1)S(1)} collective-permute-done((bf16[192,512]{1,0:T(8,128)(2,1)S(1)}, bf16[192,512]{1,0:T(8,128)(2,1)S(1)}, u32[]{:S(2)}, u32[]{:S(2)}) %collective-permute-start.47) | collective-permute-done | bytes 196640 | tf_op jit(solution)/shard_map/ppermute | solution.py:46
  307.2 1.5 collective-permute-start.44
  309.2 5.2 %collective-permute-done.43.refs_3_ = bf16[208,640]{1,0:T(8,128)(2,1)S(1)} collective-permute-done((bf16[208,640]{1,0:T(8,128)(2,1)S(1)}, bf16[208,640]{1,0:T(8,128)(2,1)S(1)}, u32[]{:S(2)}, u32[]{:S(2)}) %collective-permute-start.43) | collective-permute-done | bytes 266272 | tf_op jit(solution)/shard_map/ppermute | solution.py:46
  314.4 4.0 collective-permute-done.44.refs_4_
  318.5 3.3 backward.4
  321.9 3.7 collective-permute-start.57
  329.3 1.5 collective-permute-start.54
  330.8 1.5 collective-permute-start.55
  332.3 2.7 collective-permute-done.57.refs_1_
  335.0 2.4 collective-permute-start.56
  337.4 25.7 %weight.3.refs_5_ = f32[3,3,192,1536]{3,2,1,0:T(8,128)} custom-call(s32[14]{0:T(128)S(1)} %pad_add_fusion.meta, bf16[192,512]{1,0:T(8,128)(2,1)S(1)} %get-tuple-element.179.refs_0_, bf16[192,512]{1,0:T(8,128)(2,1)S(1)} %collective-permute-done.46.refs_1_, bf16[192,512]{1,0:T(8,128)(2,1)S(1)} %collective-permute-done.47.refs_2_, ...), custom_call_target="tpu_custom_call" | custom-call | flops 7247757312 | bytes 6291456 | tf_op jit(solution)/shard_map/weight/pallas_call | solution.py:522
  363.3 2.1 collective-permute-start.61
  365.4 2.3 collective-permute-start.62
  368.7 1.8 backward.5
  370.7 2.1 collective-permute-start.64
  372.8 4.6 %copy-done.6 = bf16[12288,512]{1,0:T(8,128)(2,1)S(1)} copy-done((bf16[12288,512]{1,0:T(8,128)(2,1)S(1)}, bf16[12288,512]{1,0:T(8,128)(2,1)}, u32[]{:S(2)}) %copy-start.6) | copy-done | bytes 12582936
  377.4 8.4 %weight.4.refs_5_ = f32[3,3,192,1536]{3,2,1,0:T(8,128)} custom-call(s32[14]{0:T(128)S(1)} %pad_add_fusion.meta, bf16[192,512]{1,0:T(8,128)(2,1)S(1)} %copy-done.31, bf16[192,512]{1,0:T(8,128)(2,1)S(1)} %collective-permute-done.57.refs_1_, bf16[192,512]{1,0:T(8,128)(2,1)S(1)} %collective-permute-done.58.refs_2_, ...), custom_call_target="tpu_custom_call", output_to_operand_aliasing={{}: (6, {})} | custom-call | flops 7247757312 | bytes 6291456 | tf_op jit(solution)/shard_map/weight/pallas_call | solution.py:522
  385.8 2.4 collective-permute-start.65
  389.8 8.4 %weight.5 = f32[3,3,192,1536]{3,2,1,0:T(8,128)} custom-call(s32[14]{0:T(128)S(1)} %pad_add_fusion.meta, bf16[192,512]{1,0:T(8,128)(2,1)S(1)} %copy-done.33, bf16[192,512]{1,0:T(8,128)(2,1)S(1)} %collective-permute-done.60.refs_1_, bf16[192,512]{1,0:T(8,128)(2,1)S(1)} %collective-permute-done.61.refs_2_, ...), custom_call_target="tpu_custom_call", output_to_operand_aliasing={{}: (6, {})} | custom-call | flops 7247757312 | bytes 6291456 | tf_op jit(solution)/shard_map/weight/pallas_call | solution.py:522
  (250 shorter events, 61.7 us)
Async XLA Ops:
  7.2 360.5 %all-gather.3.cloned.1.call-start = ((), (), s32[]{:S(2)}) async-start(), calls=%async_computation | async-start | bytes 12976128 | tf_op jit(solution)/shard_map/all_gather | solution.py:624
  7.2 23.5 %collective-permute-start.3 = (bf16[192,512]{1,0:T(8,128)(2,1)}, bf16[192,512]{1,0:T(8,128)(2,1)S(1)}, u32[]{:S(2)}, u32[]{:S(2)}) collective-permute-start(bf16[192,512]{1,0:T(8,128)(2,1)} %refs_5_.1), channel_id=1, source_target_pairs={{0,2},{1,3},{2,0},{3,1},{4,6},{5,7},{6,4},{7,5},{8,10},{9,11},{10,... | collective-permute-start | bytes 589832 | tf_op jit(solution)/shard_map/ppermute | solution.py:46
  10.3 21.7 %collective-permute-start.5 = (bf16[192,512]{1,0:T(8,128)(2,1)}, bf16[192,512]{1,0:T(8,128)(2,1)S(1)}, u32[]{:S(2)}, u32[]{:S(2)}) collective-permute-start(bf16[192,512]{1,0:T(8,128)(2,1)} %refs_5_.1), channel_id=1, source_target_pairs={{0,4},{1,5},{2,6},{3,7},{4,0},{5,1},{6,2},{7,3},{8,12},{9,13},{10,... | collective-permute-start | bytes 589832 | tf_op jit(solution)/shard_map/ppermute | solution.py:46
  11.8 20.8 %collective-permute-start.7 = (bf16[192,512]{1,0:T(8,128)(2,1)}, bf16[192,512]{1,0:T(8,128)(2,1)S(1)}, u32[]{:S(2)}, u32[]{:S(2)}) collective-permute-start(bf16[192,512]{1,0:T(8,128)(2,1)} %refs_5_.1), channel_id=1, source_target_pairs={{0,6},{1,7},{2,4},{3,5},{4,2},{5,3},{6,0},{7,1},{8,14},{9,15},{10,... | collective-permute-start | bytes 589832 | tf_op jit(solution)/shard_map/ppermute | solution.py:46
  14.1 4.7 %collective-permute-start = (bf16[192,256]{1,0:T(8,128)(2,1)S(1)}, bf16[192,256]{1,0:T(8,128)(2,1)S(1)}, u32[]{:S(2)}, u32[]{:S(2)}) collective-permute-start(bf16[192,256]{1,0:T(8,128)(2,1)S(1)} %get-tuple-element.211), channel_id=1, source_target_pairs={{0,8},{8,0},{16,24},{24,16},{1,9},{9,1},{17,25},{25,17},{2,10},{10... | collective-permute-start | bytes 294920 | tf_op jit(solution)/shard_map/ppermute | solution.py:552
  16.2 2.6 collective-permute-start.1
  21.4 4.1 %collective-permute-start.10 = (bf16[192,128]{1,0:T(8,128)(2,1)S(1)}, bf16[192,128]{1,0:T(8,128)(2,1)S(1)}, u32[]{:S(2)}, u32[]{:S(2)}) collective-permute-start(bf16[192,128]{1,0:T(8,128)(2,1)S(1)} %get-tuple-element.106.refs_1_.refs_10_.refs_8_), channel_id=1, source_target_pairs={{0,2},{1,3},{2,0},{3,1},{4,6},{5,7},{6,4},{7,5},{8,10},{9,11},{10,... | collective-permute-start | bytes 147464 | tf_op jit(solution)/shard_map/ppermute | solution.py:46
  23.3 5.3 %collective-permute-start.12 = (bf16[192,128]{1,0:T(8,128)(2,1)S(1)}, bf16[192,128]{1,0:T(8,128)(2,1)S(1)}, u32[]{:S(2)}, u32[]{:S(2)}) collective-permute-start(bf16[192,128]{1,0:T(8,128)(2,1)S(1)} %get-tuple-element.106.refs_1_.refs_10_.refs_8_), channel_id=1, source_target_pairs={{0,4},{1,5},{2,6},{3,7},{4,0},{5,1},{6,2},{7,3},{8,12},{9,13},{10,... | collective-permute-start | bytes 147464 | tf_op jit(solution)/shard_map/ppermute | solution.py:46
  25.5 5.2 %collective-permute-start.14 = (bf16[192,128]{1,0:T(8,128)(2,1)S(1)}, bf16[192,128]{1,0:T(8,128)(2,1)S(1)}, u32[]{:S(2)}, u32[]{:S(2)}) collective-permute-start(bf16[192,128]{1,0:T(8,128)(2,1)S(1)} %get-tuple-element.106.refs_1_.refs_10_.refs_8_), channel_id=1, source_target_pairs={{0,6},{1,7},{2,4},{3,5},{4,2},{5,3},{6,0},{7,1},{8,14},{9,15},{10,... | collective-permute-start | bytes 147464 | tf_op jit(solution)/shard_map/ppermute | solution.py:46
  28.7 5.1 %collective-permute-start.9 = (bf16[192,128]{1,0:T(8,128)(2,1)S(1)}, bf16[192,128]{1,0:T(8,128)(2,1)S(1)}, u32[]{:S(2)}, u32[]{:S(2)}) collective-permute-start(bf16[192,128]{1,0:T(8,128)(2,1)S(1)} %get-tuple-element.106.refs_1_.refs_10_.refs_8_), channel_id=1, source_target_pairs={{0,1},{1,0},{2,3},{3,2},{4,5},{5,4},{6,7},{7,6},{8,9},{9,8},{10,11... | collective-permute-start | bytes 147464 | tf_op jit(solution)/shard_map/ppermute | solution.py:46
  30.7 6.8 %collective-permute-start.2 = (bf16[192,512]{1,0:T(8,128)(2,1)}, bf16[192,512]{1,0:T(8,128)(2,1)S(1)}, u32[]{:S(2)}, u32[]{:S(2)}) collective-permute-start(bf16[192,512]{1,0:T(8,128)(2,1)} %refs_5_.1), channel_id=1, source_target_pairs={{0,1},{1,0},{2,3},{3,2},{4,5},{5,4},{6,7},{7,6},{8,9},{9,8},{10,11... | collective-permute-start | bytes 589832 | tf_op jit(solution)/shard_map/ppermute | solution.py:46
  30.7 6.8 %collective-permute-start.4 = (bf16[192,512]{1,0:T(8,128)(2,1)S(1)}, bf16[192,512]{1,0:T(8,128)(2,1)S(1)}, u32[]{:S(2)}, u32[]{:S(2)}) collective-permute-start(bf16[192,512]{1,0:T(8,128)(2,1)S(1)} %collective-permute-done.3.refs_4_.refs_2_), channel_id=1, source_target_pairs={{0,1},{1,0},{2,3},{3,2},{4,5},{5,4},{6,7},{7,6},{8,9},{9,8},{10,11... | collective-permute-start | bytes 589832 | tf_op jit(solution)/shard_map/ppermute | solution.py:46
  31.9 5.6 %collective-permute-start.6 = (bf16[192,512]{1,0:T(8,128)(2,1)S(1)}, bf16[192,512]{1,0:T(8,128)(2,1)S(1)}, u32[]{:S(2)}, u32[]{:S(2)}) collective-permute-start(bf16[192,512]{1,0:T(8,128)(2,1)S(1)} %collective-permute-done.5.refs_6_.refs_4_), channel_id=1, source_target_pairs={{0,1},{1,0},{2,3},{3,2},{4,5},{5,4},{6,7},{7,6},{8,9},{9,8},{10,11... | collective-permute-start | bytes 589832 | tf_op jit(solution)/shard_map/ppermute | solution.py:46
  32.6 4.9 %collective-permute-start.8 = (bf16[192,512]{1,0:T(8,128)(2,1)S(1)}, bf16[192,512]{1,0:T(8,128)(2,1)S(1)}, u32[]{:S(2)}, u32[]{:S(2)}) collective-permute-start(bf16[192,512]{1,0:T(8,128)(2,1)S(1)} %collective-permute-done.7.refs_8_.refs_6_), channel_id=1, source_target_pairs={{0,1},{1,0},{2,3},{3,2},{4,5},{5,4},{6,7},{7,6},{8,9},{9,8},{10,11... | collective-permute-start | bytes 589832 | tf_op jit(solution)/shard_map/ppermute | solution.py:46
  54.4 8.9 %collective-permute-start.17 = (bf16[192,640]{1,0:T(8,128)(2,1)S(1)}, bf16[192,640]{1,0:T(8,128)(2,1)}, u32[]{:S(2)}, u32[]{:S(2)}) collective-permute-start(bf16[192,640]{1,0:T(8,128)(2,1)S(1)} %get-tuple-element.112.refs_0_.refs_1_.refs_7_), channel_id=1, source_target_pairs={{0,2},{1,3},{2,0},{3,1},{4,6},{5,7},{6,4},{7,5},{8,10},{9,11},{10,... | collective-permute-start | bytes 737288 | tf_op jit(solution)/shard_map/ppermute | solution.py:46
  56.1 12.3 %collective-permute-start.19 = (bf16[192,640]{1,0:T(8,128)(2,1)S(1)}, bf16[192,640]{1,0:T(8,128)(2,1)}, u32[]{:S(2)}, u32[]{:S(2)}) collective-permute-start(bf16[192,640]{1,0:T(8,128)(2,1)S(1)} %get-tuple-element.112.refs_0_.refs_1_.refs_7_), channel_id=1, source_target_pairs={{0,4},{1,5},{2,6},{3,7},{4,0},{5,1},{6,2},{7,3},{8,12},{9,13},{10,... | collective-permute-start | bytes 737288 | tf_op jit(solution)/shard_map/ppermute | solution.py:46
  57.9 11.5 %collective-permute-start.21 = (bf16[192,640]{1,0:T(8,128)(2,1)S(1)}, bf16[192,640]{1,0:T(8,128)(2,1)}, u32[]{:S(2)}, u32[]{:S(2)}) collective-permute-start(bf16[192,640]{1,0:T(8,128)(2,1)S(1)} %get-tuple-element.112.refs_0_.refs_1_.refs_7_), channel_id=1, source_target_pairs={{0,6},{1,7},{2,4},{3,5},{4,2},{5,3},{6,0},{7,1},{8,14},{9,15},{10,... | collective-permute-start | bytes 737288 | tf_op jit(solution)/shard_map/ppermute | solution.py:46
  58.7 55.5 %collective-permute-start.16 = (bf16[192,640]{1,0:T(8,128)(2,1)S(1)}, bf16[192,640]{1,0:T(8,128)(2,1)}, u32[]{:S(2)}, u32[]{:S(2)}) collective-permute-start(bf16[192,640]{1,0:T(8,128)(2,1)S(1)} %get-tuple-element.112.refs_0_.refs_1_.refs_7_), channel_id=1, source_target_pairs={{0,1},{1,0},{2,3},{3,2},{4,5},{5,4},{6,7},{7,6},{8,9},{9,8},{10,11... | collective-permute-start | bytes 737288 | tf_op jit(solution)/shard_map/ppermute | solution.py:46
  63.3 50.9 %collective-permute-start.18 = (bf16[192,640]{1,0:T(8,128)(2,1)}, bf16[192,640]{1,0:T(8,128)(2,1)}, u32[]{:S(2)}, u32[]{:S(2)}) collective-permute-start(bf16[192,640]{1,0:T(8,128)(2,1)} %collective-permute-done.17.refs_3_.refs_2_), channel_id=1, source_target_pairs={{0,1},{1,0},{2,3},{3,2},{4,5},{5,4},{6,7},{7,6},{8,9},{9,8},{10,11... | collective-permute-start | bytes 737288 | tf_op jit(solution)/shard_map/ppermute | solution.py:46
  68.4 45.8 %collective-permute-start.20 = (bf16[192,640]{1,0:T(8,128)(2,1)}, bf16[192,640]{1,0:T(8,128)(2,1)}, u32[]{:S(2)}, u32[]{:S(2)}) collective-permute-start(bf16[192,640]{1,0:T(8,128)(2,1)} %collective-permute-done.19.refs_5_.refs_4_), channel_id=1, source_target_pairs={{0,1},{1,0},{2,3},{3,2},{4,5},{5,4},{6,7},{7,6},{8,9},{9,8},{10,11... | collective-permute-start | bytes 737288 | tf_op jit(solution)/shard_map/ppermute | solution.py:46
  69.3 44.9 %collective-permute-start.22 = (bf16[192,640]{1,0:T(8,128)(2,1)}, bf16[192,640]{1,0:T(8,128)(2,1)}, u32[]{:S(2)}, u32[]{:S(2)}) collective-permute-start(bf16[192,640]{1,0:T(8,128)(2,1)} %collective-permute-done.21.refs_7_.refs_6_), channel_id=1, source_target_pairs={{0,1},{1,0},{2,3},{3,2},{4,5},{5,4},{6,7},{7,6},{8,9},{9,8},{10,11... | collective-permute-start | bytes 737288 | tf_op jit(solution)/shard_map/ppermute | solution.py:46
  72.6 6.4 %collective-permute-start.23 = (f32[8,256]{1,0:T(8,128)S(1)}, f32[8,256]{1,0:T(8,128)S(1)}, u32[]{:S(2)}, u32[]{:S(2)}) collective-permute-start(f32[8,256]{1,0:T(8,128)S(1)} %stack.34.refs_0_), channel_id=1, source_target_pairs={{0,8},{8,0},{16,24},{24,16},{1,9},{9,1},{17,25},{25,17},{2,10},{10... | collective-permute-start | bytes 24584 | tf_op jit(solution)/shard_map/ppermute | solution.py:46
  79.5 5.1 %collective-permute-start.24 = (f32[8,256]{1,0:T(8,128)S(1)}, f32[8,256]{1,0:T(8,128)}, u32[]{:S(2)}, u32[]{:S(2)}) collective-permute-start(f32[8,256]{1,0:T(8,128)S(1)} %stack.34.refs_0_), channel_id=1, source_target_pairs={{0,16},{8,24},{16,0},{24,8},{1,17},{9,25},{17,1},{25,9},{2,18},{10... | collective-permute-start | bytes 24584 | tf_op jit(solution)/shard_map/ppermute | solution.py:46
  84.6 5.6 %collective-permute-start.25 = (f32[8,256]{1,0:T(8,128)S(1)}, f32[8,256]{1,0:T(8,128)}, u32[]{:S(2)}, u32[]{:S(2)}) collective-permute-start(f32[8,256]{1,0:T(8,128)S(1)} %stack.34.refs_0_), channel_id=1, source_target_pairs={{0,24},{8,16},{16,8},{24,0},{1,25},{9,17},{17,9},{25,1},{2,26},{10... | collective-permute-start | bytes 24584 | tf_op jit(solution)/shard_map/ppermute | solution.py:46
  123.7 7.9 %collective-permute-start.27 = (bf16[192,640]{1,0:T(8,128)(2,1)S(1)}, bf16[192,640]{1,0:T(8,128)(2,1)S(1)}, u32[]{:S(2)}, u32[]{:S(2)}) collective-permute-start(bf16[192,640]{1,0:T(8,128)(2,1)S(1)} %get-tuple-element.124.refs_0_.refs_1_.refs_7_), channel_id=1, source_target_pairs={{0,2},{1,3},{2,0},{3,1},{4,6},{5,7},{6,4},{7,5},{8,10},{9,11},{10,... | collective-permute-start | bytes 737288 | tf_op jit(solution)/shard_map/ppermute | solution.py:46
  125.2 9.6 %collective-permute-start.29 = (bf16[192,640]{1,0:T(8,128)(2,1)S(1)}, bf16[192,640]{1,0:T(8,128)(2,1)S(1)}, u32[]{:S(2)}, u32[]{:S(2)}) collective-permute-start(bf16[192,640]{1,0:T(8,128)(2,1)S(1)} %get-tuple-element.124.refs_0_.refs_1_.refs_7_), channel_id=1, source_target_pairs={{0,4},{1,5},{2,6},{3,7},{4,0},{5,1},{6,2},{7,3},{8,12},{9,13},{10,... | collective-permute-start | bytes 737288 | tf_op jit(solution)/shard_map/ppermute | solution.py:46
  126.5 8.9 %collective-permute-start.31 = (bf16[192,640]{1,0:T(8,128)(2,1)S(1)}, bf16[192,640]{1,0:T(8,128)(2,1)S(1)}, u32[]{:S(2)}, u32[]{:S(2)}) collective-permute-start(bf16[192,640]{1,0:T(8,128)(2,1)S(1)} %get-tuple-element.124.refs_0_.refs_1_.refs_7_), channel_id=1, source_target_pairs={{0,6},{1,7},{2,4},{3,5},{4,2},{5,3},{6,0},{7,1},{8,14},{9,15},{10,... | collective-permute-start | bytes 737288 | tf_op jit(solution)/shard_map/ppermute | solution.py:46
  127.5 18.1 %collective-permute-start.26 = (bf16[192,640]{1,0:T(8,128)(2,1)S(1)}, bf16[192,640]{1,0:T(8,128)(2,1)S(1)}, u32[]{:S(2)}, u32[]{:S(2)}) collective-permute-start(bf16[192,640]{1,0:T(8,128)(2,1)S(1)} %get-tuple-element.124.refs_0_.refs_1_.refs_7_), channel_id=1, source_target_pairs={{0,1},{1,0},{2,3},{3,2},{4,5},{5,4},{6,7},{7,6},{8,9},{9,8},{10,11... | collective-permute-start | bytes 737288 | tf_op jit(solution)/shard_map/ppermute | solution.py:46
  131.6 13.9 %collective-permute-start.28 = (bf16[192,640]{1,0:T(8,128)(2,1)S(1)}, bf16[192,640]{1,0:T(8,128)(2,1)S(1)}, u32[]{:S(2)}, u32[]{:S(2)}) collective-permute-start(bf16[192,640]{1,0:T(8,128)(2,1)S(1)} %collective-permute-done.27.refs_3_.refs_2_), channel_id=1, source_target_pairs={{0,1},{1,0},{2,3},{3,2},{4,5},{5,4},{6,7},{7,6},{8,9},{9,8},{10,11... | collective-permute-start | bytes 737288 | tf_op jit(solution)/shard_map/ppermute | solution.py:46
  134.8 10.8 %collective-permute-start.30 = (bf16[192,640]{1,0:T(8,128)(2,1)S(1)}, bf16[192,640]{1,0:T(8,128)(2,1)S(1)}, u32[]{:S(2)}, u32[]{:S(2)}) collective-permute-start(bf16[192,640]{1,0:T(8,128)(2,1)S(1)} %collective-permute-done.29.refs_5_.refs_4_), channel_id=1, source_target_pairs={{0,1},{1,0},{2,3},{3,2},{4,5},{5,4},{6,7},{7,6},{8,9},{9,8},{10,11... | collective-permute-start | bytes 737288 | tf_op jit(solution)/shard_map/ppermute | solution.py:46
  135.4 10.2 %collective-permute-start.32 = (bf16[192,640]{1,0:T(8,128)(2,1)S(1)}, bf16[192,640]{1,0:T(8,128)(2,1)S(1)}, u32[]{:S(2)}, u32[]{:S(2)}) collective-permute-start(bf16[192,640]{1,0:T(8,128)(2,1)S(1)} %collective-permute-done.31.refs_7_.refs_6_), channel_id=1, source_target_pairs={{0,1},{1,0},{2,3},{3,2},{4,5},{5,4},{6,7},{7,6},{8,9},{9,8},{10,11... | collective-permute-start | bytes 737288 | tf_op jit(solution)/shard_map/ppermute | solution.py:46
  153.5 20.2 %collective-permute-start.33 = (bf16[192,512]{1,0:T(8,128)(2,1)S(1)}, bf16[192,512]{1,0:T(8,128)(2,1)S(1)}, u32[]{:S(2)}, u32[]{:S(2)}) collective-permute-start(bf16[192,512]{1,0:T(8,128)(2,1)S(1)} %get-tuple-element.139.refs_0_), channel_id=1, source_target_pairs={{0,8},{8,0},{16,24},{24,16},{1,9},{9,1},{17,25},{25,17},{2,10},{10... | collective-permute-start | bytes 589832 | tf_op jit(solution)/shard_map/ppermute | solution.py:46
  154.2 20.8 %collective-permute-start.34 = (bf16[192,512]{1,0:T(8,128)(2,1)S(1)}, bf16[192,512]{1,0:T(8,128)(2,1)S(1)}, u32[]{:S(2)}, u32[]{:S(2)}) collective-permute-start(bf16[192,512]{1,0:T(8,128)(2,1)S(1)} %get-tuple-element.139.refs_0_), channel_id=1, source_target_pairs={{0,16},{8,24},{16,0},{24,8},{1,17},{9,25},{17,1},{25,9},{2,18},{10... | collective-permute-start | bytes 589832 | tf_op jit(solution)/shard_map/ppermute | solution.py:46
  156.4 26.1 %collective-permute-start.35 = (bf16[192,512]{1,0:T(8,128)(2,1)S(1)}, bf16[192,512]{1,0:T(8,128)(2,1)S(1)}, u32[]{:S(2)}, u32[]{:S(2)}) collective-permute-start(bf16[192,512]{1,0:T(8,128)(2,1)S(1)} %get-tuple-element.139.refs_0_), channel_id=1, source_target_pairs={{0,24},{8,16},{16,8},{24,0},{1,25},{9,17},{17,9},{25,1},{2,26},{10... | collective-permute-start | bytes 589832 | tf_op jit(solution)/shard_map/ppermute | solution.py:46
  192.1 6.4 %collective-permute-start.36 = (bf16[784,640]{1,0:T(8,128)(2,1)S(1)}, bf16[784,640]{1,0:T(8,128)(2,1)S(1)}, u32[]{:S(2)}, u32[]{:S(2)}) collective-permute-start(bf16[784,640]{1,0:T(8,128)(2,1)S(1)} %get-tuple-element.144.send_ref), channel_id=1, source_target_pairs={{0,1},{1,0},{2,3},{3,2},{4,5},{5,4},{6,7},{7,6},{8,9},{9,8},{10,11... | collective-permute-start | bytes 3010568 | tf_op jit(solution)/shard_map/ppermute | solution.py:46
  192.2 68.9 %collective-permute-start.40 = (bf16[4,192,512]{2,1,0:T(8,128)(2,1)S(1)}, bf16[4,192,512]{2,1,0:T(8,128)(2,1)S(1)}, u32[]{:S(2)}, u32[]{:S(2)}) collective-permute-start(bf16[4,192,512]{2,1,0:T(8,128)(2,1)S(1)} %get-tuple-element.183.refs_4_), channel_id=1, source_target_pairs={{0,8},{8,0},{16,24},{24,16},{1,9},{9,1},{17,25},{25,17},{2,10},{10... | collective-permute-start | bytes 2359304 | tf_op jit(solution)/shard_map/ppermute | solution.py:46
  198.5 62.6 %collective-permute-start.41 = (bf16[4,192,512]{2,1,0:T(8,128)(2,1)S(1)}, bf16[4,192,512]{2,1,0:T(8,128)(2,1)S(1)}, u32[]{:S(2)}, u32[]{:S(2)}) collective-permute-start(bf16[4,192,512]{2,1,0:T(8,128)(2,1)S(1)} %get-tuple-element.183.refs_4_), channel_id=1, source_target_pairs={{0,16},{8,24},{16,0},{24,8},{1,17},{9,25},{17,1},{25,9},{2,18},{10... | collective-permute-start | bytes 2359304 | tf_op jit(solution)/shard_map/ppermute | solution.py:46
  198.7 62.3 %collective-permute-start.37 = (bf16[208,640]{1,0:T(8,128)(2,1)S(1)}, bf16[208,640]{1,0:T(8,128)(2,1)S(1)}, u32[]{:S(2)}, u32[]{:S(2)}) collective-permute-start(bf16[208,640]{1,0:T(8,128)(2,1)S(1)} %get-tuple-element.146), channel_id=1, source_target_pairs={{0,2},{1,3},{2,0},{3,1},{4,6},{5,7},{6,4},{7,5},{8,10},{9,11},{10,... | collective-permute-start | bytes 798728 | tf_op jit(solution)/shard_map/ppermute | solution.py:46
  200.3 60.8 %collective-permute-start.38 = (bf16[208,640]{1,0:T(8,128)(2,1)S(1)}, bf16[208,640]{1,0:T(8,128)(2,1)S(1)}, u32[]{:S(2)}, u32[]{:S(2)}) collective-permute-start(bf16[208,640]{1,0:T(8,128)(2,1)S(1)} %get-tuple-element.147), channel_id=1, source_target_pairs={{0,4},{1,5},{2,6},{3,7},{4,0},{5,1},{6,2},{7,3},{8,12},{9,13},{10,... | collective-permute-start | bytes 798728 | tf_op jit(solution)/shard_map/ppermute | solution.py:46
  201.8 59.3 %collective-permute-start.39 = (bf16[208,640]{1,0:T(8,128)(2,1)S(1)}, bf16[208,640]{1,0:T(8,128)(2,1)S(1)}, u32[]{:S(2)}, u32[]{:S(2)}) collective-permute-start(bf16[208,640]{1,0:T(8,128)(2,1)S(1)} %get-tuple-element.148), channel_id=1, source_target_pairs={{0,6},{1,7},{2,4},{3,5},{4,2},{5,3},{6,0},{7,1},{8,14},{9,15},{10,... | collective-permute-start | bytes 798728 | tf_op jit(solution)/shard_map/ppermute | solution.py:46
  261.1 20.1 %collective-permute-start.51 = (bf16[4,192,512]{2,1,0:T(8,128)(2,1)S(1)}, bf16[4,192,512]{2,1,0:T(8,128)(2,1)S(1)}, u32[]{:S(2)}, u32[]{:S(2)}) collective-permute-start(bf16[4,192,512]{2,1,0:T(8,128)(2,1)S(1)} %collective-permute-done.41.refs_8_), channel_id=1, source_target_pairs={{0,8},{8,0},{16,24},{24,16},{1,9},{9,1},{17,25},{25,17},{2,10},{10... | collective-permute-start | bytes 2359304 | tf_op jit(solution)/shard_map/ppermute | solution.py:46
  267.7 21.6 %collective-permute-start.42 = (bf16[784,640]{1,0:T(8,128)(2,1)S(1)}, bf16[784,640]{1,0:T(8,128)(2,1)S(1)}, u32[]{:S(2)}, u32[]{:S(2)}) collective-permute-start(bf16[784,640]{1,0:T(8,128)(2,1)S(1)} %get-tuple-element.158.send_ref), channel_id=1, source_target_pairs={{0,1},{1,0},{2,3},{3,2},{4,5},{5,4},{6,7},{7,6},{8,9},{9,8},{10,11... | collective-permute-start | bytes 3010568 | tf_op jit(solution)/shard_map/ppermute | solution.py:46
  267.8 40.9 %collective-permute-start.49 = (bf16[4,192,512]{2,1,0:T(8,128)(2,1)S(1)}, bf16[4,192,512]{2,1,0:T(8,128)(2,1)S(1)}, u32[]{:S(2)}, u32[]{:S(2)}) collective-permute-start(bf16[4,192,512]{2,1,0:T(8,128)(2,1)S(1)} %collective-permute-done.40.refs_6_), channel_id=1, source_target_pairs={{0,1},{1,0},{2,3},{3,2},{4,5},{5,4},{6,7},{7,6},{8,9},{9,8},{10,11... | collective-permute-start | bytes 2359304 | tf_op jit(solution)/shard_map/ppermute | solution.py:46
  268.3 40.9 %collective-permute-start.50 = (bf16[4,192,512]{2,1,0:T(8,128)(2,1)S(1)}, bf16[4,192,512]{2,1,0:T(8,128)(2,1)S(1)}, u32[]{:S(2)}, u32[]{:S(2)}) collective-permute-start(bf16[4,192,512]{2,1,0:T(8,128)(2,1)S(1)} %collective-permute-done.41.refs_8_), channel_id=1, source_target_pairs={{0,1},{1,0},{2,3},{3,2},{4,5},{5,4},{6,7},{7,6},{8,9},{9,8},{10,11... | collective-permute-start | bytes 2359304 | tf_op jit(solution)/shard_map/ppermute | solution.py:46
  281.3 37.2 %collective-permute-start.52 = (bf16[4,192,512]{2,1,0:T(8,128)(2,1)S(1)}, bf16[4,192,512]{2,1,0:T(8,128)(2,1)S(1)}, u32[]{:S(2)}, u32[]{:S(2)}) collective-permute-start(bf16[4,192,512]{2,1,0:T(8,128)(2,1)S(1)} %collective-permute-done.51.refs_10_), channel_id=1, source_target_pairs={{0,1},{1,0},{2,3},{3,2},{4,5},{5,4},{6,7},{7,6},{8,9},{9,8},{10,11... | collective-permute-start | bytes 2359304 | tf_op jit(solution)/shard_map/ppermute | solution.py:46
  281.3 7.3 %collective-permute-start.46 = (bf16[192,512]{1,0:T(8,128)(2,1)S(1)}, bf16[192,512]{1,0:T(8,128)(2,1)S(1)}, u32[]{:S(2)}, u32[]{:S(2)}) collective-permute-start(bf16[192,512]{1,0:T(8,128)(2,1)S(1)} %get-tuple-element.179.refs_0_), channel_id=1, source_target_pairs={{0,8},{8,0},{16,24},{24,16},{1,9},{9,1},{17,25},{25,17},{2,10},{10... | collective-permute-start | bytes 589832 | tf_op jit(solution)/shard_map/ppermute | solution.py:46
  288.6 17.1 %collective-permute-start.47 = (bf16[192,512]{1,0:T(8,128)(2,1)S(1)}, bf16[192,512]{1,0:T(8,128)(2,1)S(1)}, u32[]{:S(2)}, u32[]{:S(2)}) collective-permute-start(bf16[192,512]{1,0:T(8,128)(2,1)S(1)} %get-tuple-element.179.refs_0_), channel_id=1, source_target_pairs={{0,16},{8,24},{16,0},{24,8},{1,17},{9,25},{17,1},{25,9},{2,18},{10... | collective-permute-start | bytes 589832 | tf_op jit(solution)/shard_map/ppermute | solution.py:46
  289.3 17.9 %collective-permute-start.48 = (bf16[192,512]{1,0:T(8,128)(2,1)S(1)}, bf16[192,512]{1,0:T(8,128)(2,1)S(1)}, u32[]{:S(2)}, u32[]{:S(2)}) collective-permute-start(bf16[192,512]{1,0:T(8,128)(2,1)S(1)} %get-tuple-element.179.refs_0_), channel_id=1, source_target_pairs={{0,24},{8,16},{16,8},{24,0},{1,25},{9,17},{17,9},{25,1},{2,26},{10... | collective-permute-start | bytes 589832 | tf_op jit(solution)/shard_map/ppermute | solution.py:46
  305.7 8.7 %collective-permute-start.43 = (bf16[208,640]{1,0:T(8,128)(2,1)S(1)}, bf16[208,640]{1,0:T(8,128)(2,1)S(1)}, u32[]{:S(2)}, u32[]{:S(2)}) collective-permute-start(bf16[208,640]{1,0:T(8,128)(2,1)S(1)} %get-tuple-element.160), channel_id=1, source_target_pairs={{0,2},{1,3},{2,0},{3,1},{4,6},{5,7},{6,4},{7,5},{8,10},{9,11},{10,... | collective-permute-start | bytes 798728 | tf_op jit(solution)/shard_map/ppermute | solution.py:46
  307.2 11.3 %collective-permute-start.44 = (bf16[208,640]{1,0:T(8,128)(2,1)S(1)}, bf16[208,640]{1,0:T(8,128)(2,1)S(1)}, u32[]{:S(2)}, u32[]{:S(2)}) collective-permute-start(bf16[208,640]{1,0:T(8,128)(2,1)S(1)} %get-tuple-element.161), channel_id=1, source_target_pairs={{0,4},{1,5},{2,6},{3,7},{4,0},{5,1},{6,2},{7,3},{8,12},{9,13},{10,... | collective-permute-start | bytes 798728 | tf_op jit(solution)/shard_map/ppermute | solution.py:46
  308.6 9.8 %collective-permute-start.45 = (bf16[208,640]{1,0:T(8,128)(2,1)S(1)}, bf16[208,640]{1,0:T(8,128)(2,1)S(1)}, u32[]{:S(2)}, u32[]{:S(2)}) collective-permute-start(bf16[208,640]{1,0:T(8,128)(2,1)S(1)} %get-tuple-element.162), channel_id=1, source_target_pairs={{0,6},{1,7},{2,4},{3,5},{4,2},{5,3},{6,0},{7,1},{8,14},{9,15},{10,... | collective-permute-start | bytes 798728 | tf_op jit(solution)/shard_map/ppermute | solution.py:46
  321.9 7.2 %collective-permute-start.53 = (bf16[784,512]{1,0:T(8,128)(2,1)S(1)}, bf16[784,512]{1,0:T(8,128)(2,1)S(1)}, u32[]{:S(2)}, u32[]{:S(2)}) collective-permute-start(bf16[784,512]{1,0:T(8,128)(2,1)S(1)} %get-tuple-element.173.send_ref), channel_id=1, source_target_pairs={{0,1},{1,0},{2,3},{3,2},{4,5},{5,4},{6,7},{7,6},{8,9},{9,8},{10,11... | collective-permute-start | bytes 2408456 | tf_op jit(solution)/shard_map/ppermute | solution.py:46
  321.9 13.1 %collective-permute-start.57 = (bf16[192,512]{1,0:T(8,128)(2,1)S(1)}, bf16[192,512]{1,0:T(8,128)(2,1)S(1)}, u32[]{:S(2)}, u32[]{:S(2)}) collective-permute-start(bf16[192,512]{1,0:T(8,128)(2,1)S(1)} %get-tuple-element.200.refs_0_), channel_id=1, source_target_pairs={{0,8},{8,0},{16,24},{24,16},{1,9},{9,1},{17,25},{25,17},{2,10},{10... | collective-permute-start | bytes 589832 | tf_op jit(solution)/shard_map/ppermute | solution.py:46
  325.6 37.6 %collective-permute-start.58 = (bf16[192,512]{1,0:T(8,128)(2,1)S(1)}, bf16[192,512]{1,0:T(8,128)(2,1)S(1)}, u32[]{:S(2)}, u32[]{:S(2)}) collective-permute-start(bf16[192,512]{1,0:T(8,128)(2,1)S(1)} %get-tuple-element.200.refs_0_), channel_id=1, source_target_pairs={{0,16},{8,24},{16,0},{24,8},{1,17},{9,25},{17,1},{25,9},{2,18},{10... | collective-permute-start | bytes 589832 | tf_op jit(solution)/shard_map/ppermute | solution.py:46
  327.0 36.3 %collective-permute-start.59 = (bf16[192,512]{1,0:T(8,128)(2,1)S(1)}, bf16[192,512]{1,0:T(8,128)(2,1)S(1)}, u32[]{:S(2)}, u32[]{:S(2)}) collective-permute-start(bf16[192,512]{1,0:T(8,128)(2,1)S(1)} %get-tuple-element.200.refs_0_), channel_id=1, source_target_pairs={{0,24},{8,16},{16,8},{24,0},{1,25},{9,17},{17,9},{25,1},{2,26},{10... | collective-permute-start | bytes 589832 | tf_op jit(solution)/shard_map/ppermute | solution.py:46
  329.3 36.1 %collective-permute-start.54 = (bf16[208,512]{1,0:T(8,128)(2,1)S(1)}, bf16[208,512]{1,0:T(8,128)(2,1)S(1)}, u32[]{:S(2)}, u32[]{:S(2)}) collective-permute-start(bf16[208,512]{1,0:T(8,128)(2,1)S(1)} %get-tuple-element.175), channel_id=1, source_target_pairs={{0,2},{1,3},{2,0},{3,1},{4,6},{5,7},{6,4},{7,5},{8,10},{9,11},{10,... | collective-permute-start | bytes 638984 | tf_op jit(solution)/shard_map/ppermute | solution.py:46
  330.8 36.9 %collective-permute-start.55 = (bf16[208,512]{1,0:T(8,128)(2,1)S(1)}, bf16[208,512]{1,0:T(8,128)(2,1)S(1)}, u32[]{:S(2)}, u32[]{:S(2)}) collective-permute-start(bf16[208,512]{1,0:T(8,128)(2,1)S(1)} %get-tuple-element.176), channel_id=1, source_target_pairs={{0,4},{1,5},{2,6},{3,7},{4,0},{5,1},{6,2},{7,3},{8,12},{9,13},{10,... | collective-permute-start | bytes 638984 | tf_op jit(solution)/shard_map/ppermute | solution.py:46
  335.0 32.7 %collective-permute-start.56 = (bf16[208,512]{1,0:T(8,128)(2,1)S(1)}, bf16[208,512]{1,0:T(8,128)(2,1)S(1)}, u32[]{:S(2)}, u32[]{:S(2)}) collective-permute-start(bf16[208,512]{1,0:T(8,128)(2,1)S(1)} %get-tuple-element.177), channel_id=1, source_target_pairs={{0,6},{1,7},{2,4},{3,5},{4,2},{5,3},{6,0},{7,1},{8,14},{9,15},{10,... | collective-permute-start | bytes 638984 | tf_op jit(solution)/shard_map/ppermute | solution.py:46
  363.2 22.6 %collective-permute-start.60 = (bf16[192,512]{1,0:T(8,128)(2,1)S(1)}, bf16[192,512]{1,0:T(8,128)(2,1)S(1)}, u32[]{:S(2)}, u32[]{:S(2)}) collective-permute-start(bf16[192,512]{1,0:T(8,128)(2,1)S(1)} %get-tuple-element.198.refs_0_), channel_id=1, source_target_pairs={{0,8},{8,0},{16,24},{24,16},{1,9},{9,1},{17,25},{25,17},{2,10},{10... | collective-permute-start | bytes 589832 | tf_op jit(solution)/shard_map/ppermute | solution.py:46
  363.3 24.9 %collective-permute-start.61 = (bf16[192,512]{1,0:T(8,128)(2,1)S(1)}, bf16[192,512]{1,0:T(8,128)(2,1)S(1)}, u32[]{:S(2)}, u32[]{:S(2)}) collective-permute-start(bf16[192,512]{1,0:T(8,128)(2,1)S(1)} %get-tuple-element.198.refs_0_), channel_id=1, source_target_pairs={{0,16},{8,24},{16,0},{24,8},{1,17},{9,25},{17,1},{25,9},{2,18},{10... | collective-permute-start | bytes 589832 | tf_op jit(solution)/shard_map/ppermute | solution.py:46
  365.4 22.8 %collective-permute-start.62 = (bf16[192,512]{1,0:T(8,128)(2,1)S(1)}, bf16[192,512]{1,0:T(8,128)(2,1)S(1)}, u32[]{:S(2)}, u32[]{:S(2)}) collective-permute-start(bf16[192,512]{1,0:T(8,128)(2,1)S(1)} %get-tuple-element.198.refs_0_), channel_id=1, source_target_pairs={{0,24},{8,16},{16,8},{24,0},{1,25},{9,17},{17,9},{25,1},{2,26},{10... | collective-permute-start | bytes 589832 | tf_op jit(solution)/shard_map/ppermute | solution.py:46
  370.6 27.6 %collective-permute-start.63 = (f32[8,192]{1,0:T(8,128)S(1)}, f32[8,192]{1,0:T(8,128)S(1)}, u32[]{:S(2)}, u32[]{:S(2)}) collective-permute-start(f32[8,192]{1,0:T(8,128)S(1)} %select_maximum_fusion), channel_id=1, source_target_pairs={{0,8},{8,0},{16,24},{24,16},{1,9},{9,1},{17,25},{25,17},{2,10},{10... | collective-permute-start | bytes 18440 | tf_op jit(solution)/shard_map/ppermute | solution.py:46
  370.7 27.5 %collective-permute-start.64 = (f32[8,192]{1,0:T(8,128)S(1)}, f32[8,192]{1,0:T(8,128)S(1)}, u32[]{:S(2)}, u32[]{:S(2)}) collective-permute-start(f32[8,192]{1,0:T(8,128)S(1)} %select_maximum_fusion), channel_id=1, source_target_pairs={{0,16},{8,24},{16,0},{24,8},{1,17},{9,25},{17,1},{25,9},{2,18},{10... | collective-permute-start | bytes 18440 | tf_op jit(solution)/shard_map/ppermute | solution.py:46
  385.8 12.4 %collective-permute-start.65 = (f32[8,192]{1,0:T(8,128)S(1)}, f32[8,192]{1,0:T(8,128)S(1)}, u32[]{:S(2)}, u32[]{:S(2)}) collective-permute-start(f32[8,192]{1,0:T(8,128)S(1)} %select_maximum_fusion), channel_id=1, source_target_pairs={{0,24},{8,16},{16,8},{24,0},{1,25},{9,17},{17,9},{25,1},{2,26},{10... | collective-permute-start | bytes 18440 | tf_op jit(solution)/shard_map/ppermute | solution.py:46
  (70 other events, 1133.2 us)
Sparse Core Ops, SparseCore 0:
  123.8 136.2 all-gather.2

commit v3 on v2

v3 whole, which is shorter than its diff:
```python
import functools
import math

import jax
import jax.numpy as jnp
from jax import lax
from jax.experimental import pallas as pl
from jax.experimental.pallas import tpu as pltpu
from jax.sharding import PartitionSpec as P

LAYERS = 3
EPSILON = 1e-06
EDGE = 64
SPARE = 56
CHUNK = 384
ROWS = 16
K0 = math.sqrt(2.0 / math.pi)
K1 = K0 * 0.044715
F32 = jnp.float32
BF16 = jnp.bfloat16

VMEM = pl.BlockSpec(memory_space=pltpu.VMEM)
SMEM = pl.BlockSpec(memory_space=pltpu.SMEM)
HBM = pl.BlockSpec(memory_space=pltpu.HBM)

TP = ("pair", "side")


def params(mib=24):
    return pltpu.CompilerParams(vmem_limit_bytes=mib * 1024 * 1024)


def cost(flops, nbytes, special=0):
    return pl.CostEstimate(flops=flops, bytes_accessed=nbytes, transcendentals=special)


def tie(first, then):
    out = lax.optimization_barrier((tuple(first), tuple(then)))
    return list(out[0]), list(out[1])


def reach_of(layer):
    return 2 ** (layer + 3)


def size_of(axis):
    return math.prod(lax.axis_size(name) for name in axis) if isinstance(axis, tuple) else lax.axis_size(axis)


def swap(x, axis, mask):
    return lax.ppermute(x, axis, [(i, i ^ mask) for i in range(size_of(axis))])


def gather_tp(x):
    if size_of(TP) == 8:
        far = [x] + [swap(x, TP, m) for m in (2, 4, 6)]
        near = [swap(v, TP, 1) for v in far]
        return [v for pair in zip(far, near) for v in pair]
    whole = lax.all_gather(x, TP, axis=0)
    return [whole[i] for i in range(whole.shape[0])]


def tp_order(me):
    count = size_of(TP)
    steps = jnp.arange(count, dtype=jnp.int32)
    return me ^ steps if count == 8 else steps


def gather_seq(x):
    if size_of("seq") == 4:
        two = swap(x, "seq", 2)
        return [x, swap(x, "seq", 1), two, swap(two, "seq", 1)]
    whole = lax.all_gather(x, "seq", axis=0)
    return [whole[i] for i in range(whole.shape[0])]


def seq_order(me):
    count = size_of("seq")
    steps = jnp.arange(count, dtype=jnp.int32)
    return me ^ steps if count == 4 else steps


def roll(x, shift):
    shift = shift % x.shape[1]
    return x if shift == 0 else pltpu.roll(x, shift, 1)


def position(shape, dim, length):
    at = lax.broadcasted_iota(jnp.int32, shape, dim)
    return jnp.where(at < length + EDGE, at, at - (length + 2 * EDGE))


def in_sequence(seq_at, width, length, total):
    at = position((1, width), 1, length) + seq_at * length
    return (at >= 0) & (at < total)


def record_kernel(donor_ref, owner_ref, accept_ref, tissue_ref, grad_ref, out_ref, *, span):
    row = lax.broadcasted_iota(jnp.int32, (16, out_ref.shape[1]), 0)
    out = jnp.zeros(row.shape, F32)
    values = []
    for x in (donor_ref[...], owner_ref[...] * span + accept_ref[...], tissue_ref[...]):
        values += [(x >> 8).astype(F32), (x & 255).astype(F32)]
    grad = grad_ref[...]
    high = grad.astype(BF16).astype(F32)
    middle = (grad - high).astype(BF16).astype(F32)
    values += [high, middle, grad - high - middle]
    for k, value in enumerate(values):
        value = jnp.concatenate([value, jnp.zeros((1, row.shape[1] - value.shape[1]), F32)], axis=1)
        out = jnp.where(row == k, value, out)
    out_ref[...] = out.astype(BF16)


def edge_kernel(meta, seq_ref, tower_ref, first_ref, second_ref, states, grads, sems, *, n_tp, n_seq):
    ch, length = seq_ref.shape
    copies = []
    for i, start in enumerate((0, length - 128)):
        copies.append(pltpu.make_async_copy(seq_ref.at[:, start : start + 128], states.at[i], sems.at[2 * i]))
        copies.append(pltpu.make_async_copy(tower_ref.at[:, start : start + 128], grads.at[i], sems.at[2 * i + 1]))
    for copy in copies:
        copy.start()
    for copy in copies:
        copy.wait()
    even = lax.rem(meta[n_tp + n_seq + 1], 2) == 0
    low = lax.broadcasted_iota(jnp.int32, (ch, 128), 1) < EDGE

    def pack(state, grad):
        high = grad.astype(BF16).astype(F32)
        return [jnp.where(low, state, roll(high, EDGE)), jnp.where(low, grad - high, 0.0)]

    left = pack(states[0].astype(F32), grads[0])
    right = pack(roll(states[1].astype(F32), EDGE), roll(grads[1], EDGE))
    for i in range(2):
        first_ref[:, i * 128 : (i + 1) * 128] = jnp.where(even, right[i], left[i]).astype(BF16)
        second_ref[:, i * 128 : (i + 1) * 128] = jnp.where(even, left[i], right[i]).astype(BF16)


def window_kernel(
    meta, seq_ref, first_ref, second_ref, gain_ref, state_ref, halo_ref, held, sem, *, n_tp, n_seq
):
    ch, length = held.shape
    copy = pltpu.make_async_copy(seq_ref, held, sem)
    copy.start()
    even = lax.rem(meta[n_tp + n_seq + 1], 2) == 0
    first = first_ref[...].astype(F32)
    second = second_ref[...].astype(F32)
    right = jnp.where(even, first, second)
    left = jnp.where(even, second, first)
    lane = lax.broadcasted_iota(jnp.int32, (ch, 128), 1)
    low = lane < EDGE
    halo = jnp.where(low, right[:, :128], roll(left[:, :128], EDGE))
    gains = gain_ref[...]
    high = gains.astype(BF16).astype(F32)
    rest = gains - high
    middle = rest.astype(BF16).astype(F32)
    for k, part in enumerate((high, middle, rest - middle)):
        for layer in range(LAYERS):
            halo = jnp.where(lane == SPARE + k * LAYERS + layer, part[:, layer : layer + 1], halo)
    state_ref[:, length:] = halo.astype(BF16)
    th = jnp.where(low, roll(right[:, :128], EDGE), left[:, :128])
    tl = jnp.where(low, right[:, 128:], roll(left[:, 128:], EDGE))
    halo_ref[...] = th + tl
    copy.wait()
    state_ref[:, :length] = held[...]


def forward_kernel(meta, w_ref, own_ref, *refs, layer, n_tp, n_seq, length):
    pieces, refs = refs[:n_tp], refs[n_tp:]
    *refs, held, slopes, weights, sems = refs
    if layer == 0:
        state_ref, slope_ref, inverse_ref, hidden_ref, gain_ref = refs
    elif layer < LAYERS - 1:
        gain_ref, state_ref, slope_ref, inverse_ref, hidden_ref = refs
    else:
        gain_ref, digit_ref, state_ref, slope_ref, inverse_ref, hidden_ref = refs
    _, ch, width = held.shape
    wide = slopes.shape[2]
    channels = ch * n_tp
    reach = reach_of(layer)
    me, seq_at = meta[n_tp + n_seq], meta[n_tp + n_seq + 1]
    copy = pltpu.make_async_copy(w_ref.at[layer], weights, sems.at[0])
    copy.start()

    def add_power(j, acc):
        rows = pl.ds(pl.multiple_of(j * ROWS, ROWS), ROWS)
        for piece in pieces:
            x = piece[rows, :].astype(F32)
            sq = x * x
            for i in range(0, ROWS, 8):
                acc = acc + sq[i : i + 8]
        return acc

    acc = lax.fori_loop(0, ch // ROWS, add_power, jnp.zeros((8, width), F32))
    power = jnp.sum(acc, axis=0, keepdims=True) / channels
    inverse = 1.0 / jnp.sqrt(power + EPSILON)
    inverse_ref[...] = jnp.broadcast_to(inverse, (8, width))

    def activate(j, carry):
        rows = pl.ds(pl.multiple_of(j * ROWS, ROWS), ROWS)
        for m, piece in enumerate(pieces):
            at = meta[m]
            x = piece[rows, :].astype(F32)
            if layer == 0:
                halo = x[:, length:]
                cols = [
                    halo[:, SPARE + l : SPARE + l + 1]
                    + (
                        halo[:, SPARE + LAYERS + l : SPARE + LAYERS + l + 1]
                        + halo[:, SPARE + 2 * LAYERS + l : SPARE + 2 * LAYERS + l + 1]
                    )
                    for l in range(LAYERS)
                ]
                lane = lax.broadcasted_iota(jnp.int32, (ROWS, 128), 1)
                gain_ref[at, rows, :] = jnp.where(lane == 0, cols[0], jnp.where(lane == 1, cols[1], cols[2]))
                gain = cols[0]
            else:
                gain = gain_ref[at, rows, layer : layer + 1]
            scaled = x * gain
            pre = scaled * inverse
            sq = pre * pre
            th = jnp.tanh(pre * (K0 + K1 * sq))
            half = 0.5 + 0.5 * th
            hidden = pre * half
            held[at, rows, :] = hidden.astype(BF16)
            slope = half + (hidden - hidden * th) * (K0 + (3.0 * K1) * sq)
            slopes[at, rows, :] = (slope * scaled)[:, :wide].astype(BF16)
        return carry

    lax.fori_loop(0, ch // ROWS, activate, 0)
    leave = pltpu.make_async_copy(slopes, slope_ref, sems.at[1])
    leave.start()
    if layer == 0 and n_tp == 8:
        for i in range(n_tp // 2):
            hidden_ref[i] = held[2 * i + lax.rem(me, 2), :, :length]
    else:
        hidden_ref[...] = held[me, :, :length]
    copy.wait()
    every = held[...].reshape(channels, width)
    total = own_ref[...].astype(F32)
    for tap in range(3):
        part = jnp.dot(weights[tap * ch : (tap + 1) * ch, :], every, preferred_element_type=F32)
        total = total + roll(part, (1 - tap) * reach)
    total = jnp.where(in_sequence(seq_at, width, length, n_seq * length), total, 0.0).astype(BF16)
    if layer < LAYERS - 1:
        state_ref[...] = total
    else:
        state_ref[:ch, :] = total[:, :length]
        state_ref[ch:, :] = digit_ref[...]
    leave.wait()


def send_back(layer, upstream, meta, weights, slopes, taps, grad_ref, out_refs, score, n_tp, n_seq, length):
    ch, width = upstream.shape
    wide = taps.shape[1]
    reach = reach_of(layer)
    me, seq_at = meta[n_tp + n_seq], meta[n_tp + n_seq + 1]
    grad = jnp.where(in_sequence(seq_at, width, length, n_seq * length), upstream, 0.0)
    grad = grad.astype(BF16).astype(F32)
    grad_ref[...] = grad[:, :length].astype(BF16)
    for tap in range(3):
        taps[tap * ch : (tap + 1) * ch, :] = roll(grad, (tap - 1) * reach)[:, :wide].astype(BF16)
    for copy in slopes[1:]:
        copy.wait()
    inner = jnp.zeros((8, wide), F32)
    parts = CHUNK // ch
    chunks = ch * n_tp // CHUNK
    for r in range(chunks):
        at = (me // 2) ^ r if n_tp == 8 else r
        cols = pl.ds(pl.multiple_of(at * CHUNK, 128), CHUNK)
        part = lax.dot_general(weights[:, cols], taps[...], (((0,), (0,)), ((), ())), preferred_element_type=F32)
        for q in range(parts):
            prod = part[q * ch : (q + 1) * ch] * slopes[0][at * parts + q].astype(F32)
            inner = inner + jnp.sum(prod.reshape(ch // 8, 8, wide), axis=0)
        if n_tp == 8:
            keep_ref, send_ref = out_refs
            zero = lax.rem(me, 2) == 0
            keep_ref[r] = jnp.where(zero, part[:ch], part[ch:]).astype(BF16)
            send_ref[r * ch : (r + 1) * ch, :] = jnp.where(zero, part[ch:], part[:ch]).astype(BF16)
        else:
            for q in range(parts):
                out_refs[0][at * parts + q] = part[q * ch : (q + 1) * ch].astype(BF16)
    row = lax.broadcasted_iota(jnp.int32, (8, wide), 0)
    extra = jnp.where(row == 0, jnp.sum(inner, axis=0, keepdims=True), 0.0)
    if score is not None:
        score = jnp.concatenate([score, jnp.zeros((1, wide - score.shape[1]), F32)], axis=1)
        extra = jnp.where(row == 1, score, extra)
    if n_tp == 8:
        out_refs[1][n_tp // 2 * ch :, :] = split_rows(extra)
    else:
        out_refs[1][...] = extra


def split_rows(x):
    high = x.astype(BF16).astype(F32)
    return jnp.concatenate([high, x - high], axis=0).astype(BF16)


def join_rows(x):
    x = x.astype(F32)
    return x[:8] + x[8:]


def fetch(layer, w_ref, slope_ref, weights, slopes, sems):
    copies = [
        pltpu.make_async_copy(w_ref.at[layer], weights, sems.at[0]),
        pltpu.make_async_copy(slope_ref, slopes, sems.at[1]),
    ]
    for copy in copies:
        copy.start()
    return [slopes] + copies


def junction_kernel(meta, w_ref, slope_ref, tower_ref, halo_ref, table_ref, *refs, n_tp, n_seq, share, root):
    pieces, refs = refs[:n_seq], refs[n_seq:]
    up_ref, grad_ref, *refs = refs
    *out_refs, weights, taps, slopes, donors, rec_ref, tower, sems = refs
    ch, length = tower.shape
    width = length + 2 * EDGE
    count = share * n_seq
    tower_copy = pltpu.make_async_copy(tower_ref, tower, sems.at[2])
    tower_copy.start()
    seq_at = meta[n_tp + n_seq + 1]
    slopes = fetch(LAYERS - 1, w_ref, slope_ref, weights, slopes, sems)
    for m in range(n_seq):
        at = meta[n_tp + m]
        digits = pieces[m][ch:, :share].astype(F32)
        row = lax.broadcasted_iota(jnp.int32, (8, share), 0)
        first = (digits[0:1] * 256.0 + digits[1:2]) + (at * length).astype(F32)
        second = digits[2:3] * 256.0 + digits[3:4]
        third = digits[4:5] * 256.0 + digits[5:6]
        fourth = digits[6:7] + (digits[7:8] + digits[8:9])
        record = jnp.where(row == 0, first, jnp.where(row == 1, second, jnp.where(row == 2, third, fourth)))
        rec_ref[:, pl.ds(pl.multiple_of(at * share, 128), share)] = record
    table = table_ref[...]
    high = table.astype(BF16)
    rest = table - high.astype(F32)
    middle = rest.astype(BF16)
    last = (rest - middle.astype(F32)).astype(BF16)
    hit = lax.broadcasted_iota(jnp.int32, (table.shape[0], count), 0) == rec_ref[2:3, :].astype(jnp.int32)
    hit = jnp.where(hit, 1.0, 0.0).astype(BF16)
    rows = sum(
        lax.dot_general(part, hit, (((0,), (0,)), ((), ())), preferred_element_type=F32)
        for part in (last, middle, high)
    )
    donor = rec_ref[0:1, :].astype(jnp.int32)
    accept = rec_ref[1:2, :].astype(jnp.int32)
    weight = rec_ref[3:4, :] / root
    place = lax.broadcasted_iota(jnp.int32, (length, count), 0)
    accepts = jnp.zeros((ch, count), F32)
    for m in range(n_seq):
        at = meta[n_tp + m]
        cols = pl.ds(pl.multiple_of(at * share, 128), share)
        block = pieces[m][:ch, :]
        mine = rec_ref[0:1, cols].astype(jnp.int32) - at * length
        hit = lax.broadcasted_iota(jnp.int32, (length, share), 0) == mine
        donors[:, cols] = jnp.dot(block, jnp.where(hit, 1.0, 0.0).astype(BF16), preferred_element_type=F32)
        hit = place == accept - at * length
        accepts = accepts + jnp.dot(block, jnp.where(hit, 1.0, 0.0).astype(BF16), preferred_element_type=F32)
    product = donors[...] * accepts * rows
    scored = jnp.sum(product, axis=0, keepdims=True) / root
    score = jnp.zeros((1, share), F32)
    for m in range(n_seq):
        score = jnp.where(seq_at == m, scored[:, m * share : (m + 1) * share], score)
    scale = rows * weight
    tower_copy.wait()
    upstream = jnp.concatenate([tower[...], halo_ref[...]], axis=1)
    spot = position((width, count), 0, length) + seq_at * length
    for values, where in ((accepts * scale, donor), (donors[...] * scale, accept)):
        high = values.astype(BF16)
        low = (values - high.astype(F32)).astype(BF16)
        hit = jnp.where(spot == where, 1.0, 0.0).astype(BF16)
        both = lax.dot_general(
            jnp.concatenate([high, low], axis=0), hit, (((1,), (1,)), ((), ())), preferred_element_type=F32
        )
        upstream = upstream + (both[:ch] + both[ch:])
    up_ref[...] = upstream
    send_back(LAYERS - 1, upstream, meta, weights, slopes, taps, grad_ref, out_refs, score, n_tp, n_seq, length)


def pair_kernel(keep_ref, send_ref, got_ref, own_ref, *far_refs):
    count, ch, width = keep_ref.shape
    extra = join_rows(send_ref[count * ch :, :]) + join_rows(got_ref[count * ch :, :])
    split = split_rows(extra)
    for r in range(count):
        total = keep_ref[r].astype(F32) + got_ref[r * ch : (r + 1) * ch, :].astype(F32)
        if r == 0:
            own_ref[:ch, :] = total
            own_ref[ch:, :] = join_rows(split)
        else:
            far_refs[r - 1][:ch, :] = total.astype(BF16)
            far_refs[r - 1][ch:, :] = split


def backward_kernel(meta, *refs, layer, n_far, n_tp, n_seq, length):
    last = layer == 0
    if last:
        slopes = None
    else:
        w_ref, slope_ref, *refs = refs
        *refs, weights, taps, slopes, sems = refs
        slopes = fetch(layer - 1, w_ref, slope_ref, weights, slopes, sems)
    own_ref, refs = refs[0], refs[1:]
    far, refs = refs[:n_far], refs[n_far:]
    up_ref, state_ref, inverse_ref, gain_ref, *refs = refs
    out_ref, part_ref, *refs = refs
    if not last:
        grad_ref, *out_refs = refs
        if layer == LAYERS - 1:
            score_ref, *out_refs = out_refs
    ch, width = state_ref.shape
    channels = ch * n_tp
    sums = [own_ref[ch:, :]] + [join_rows(f[ch:, :]) for f in far]
    extra = (sums[0] + sums[1]) + (sums[2] + sums[3]) if n_far else sums[0]
    inner = extra[0:1, :]
    if layer == LAYERS - 1:
        score_ref[...] = extra
    inverse = inverse_ref[0:1, :width]
    gain = gain_ref[:, layer : layer + 1]
    back = own_ref[:ch, :]
    for f in far:
        back = back + f[:ch, :].astype(F32)
    x = state_ref[...].astype(F32)
    pre = x * gain * inverse
    sq = pre * pre
    th = jnp.tanh(pre * (K0 + K1 * sq))
    half = 0.5 + 0.5 * th
    back = back * (half + (pre * half) * (1.0 - th) * (K0 + (3.0 * K1) * sq))
    mine = back * x * inverse
    part = jnp.sum(mine[:, :length], axis=1, keepdims=True)
    part_ref[...] = jnp.broadcast_to(part, part_ref.shape)
    upstream = up_ref[:, :width] + (inverse * gain) * back - x * (inverse * inverse * inverse * inner / channels)
    out_ref[...] = upstream
    if not last:
        send_back(layer - 1, upstream, meta, weights, slopes, taps, grad_ref, out_refs, None, n_tp, n_seq, length)


def weight_kernel(meta, *refs, layer, path, n_tp, n_seq):
    pieces, refs = refs[:n_seq], refs[n_seq:]
    *sources, out_ref, whole, taps, held, done, in_sems, out_sems = refs
    ch, length = pieces[0].shape
    reach = reach_of(layer)
    total = n_seq * length
    parts = CHUNK // ch
    chunks = ch * n_tp // CHUNK
    me = meta[n_tp + n_seq]
    core = lax.rem(me, 2)

    def chunk_at(r):
        return r if path == "whole" else (me // 2) ^ r

    def lanes(m):
        return pl.ds(pl.multiple_of(meta[n_tp + m] * length, 128), length)

    def arrive(r):
        copies = []

        def add(source, side, where):
            copies.append(
                pltpu.make_async_copy(source, held.at[r, side, :, where], in_sems.at[r, len(copies)])
            )

        if path == "whole":
            for s in range(n_seq):
                for q in range(parts):
                    add(sources[0].at[s, r * parts + q], q, pl.ds(s * length, length))
        else:
            for s in range(n_seq):
                for q in range(2):
                    add(sources[q].at[s, chunk_at(r)], core if q == 0 else 1 - core, pl.ds(s * length, length))
        return copies

    def leave(r):
        cols = pl.ds(pl.multiple_of(chunk_at(r) * CHUNK, 128), CHUNK)
        return pltpu.make_async_copy(done.at[r % 2], out_ref.at[layer, :, :, cols], out_sems.at[r % 2])

    for r in range(chunks):
        for copy in arrive(r):
            copy.start()
    for m in range(n_seq):
        whole[:, lanes(m)] = pieces[m][...]
    grad = whole[...].astype(F32)
    lane = lax.broadcasted_iota(jnp.int32, (1, total), 1)
    taps[:ch, :] = jnp.where(lane < total - reach, roll(grad, -reach), 0.0).astype(BF16)
    taps[ch : 2 * ch, :] = whole[...]
    taps[2 * ch :, :] = jnp.where(lane >= reach, roll(grad, reach), 0.0).astype(BF16)
    for r in range(chunks):
        for copy in arrive(r):
            copy.wait()
        if r >= 2:
            leave(r - 2).wait()
        product = lax.dot_general(
            taps[...], held[r].reshape(CHUNK, total), (((1,), (1,)), ((), ())), preferred_element_type=F32
        )
        done[r % 2] = product.reshape(3, ch, CHUNK)
        leave(r).start()
    for r in range(max(0, chunks - 2), chunks):
        leave(r).wait()


def local(
    sequence_in,
    conv_weight,
    norm_gain,
    tissue_scale,
    donor_offset,
    acceptor_owner,
    acceptor_offset,
    tissue,
    tower_grad,
    score_grad,
):
    ch, length = sequence_in.shape
    n_tp, n_seq = size_of(TP), size_of("seq")
    channels, total = ch * n_tp, length * n_seq
    width = length + 2 * EDGE
    share = donor_offset.shape[0]
    count = share * n_seq
    paired = n_tp == 8
    n_far = 3 if paired else 0
    me = lax.axis_index(TP).astype(jnp.int32)
    seq_at = lax.axis_index("seq").astype(jnp.int32)
    meta = jnp.concatenate([tp_order(me), seq_order(seq_at), jnp.stack([me, seq_at])])
    sizes = dict(n_tp=n_tp, n_seq=n_seq)
    weights = conv_weight.transpose(0, 2, 1, 3).reshape(LAYERS, 3 * ch, channels)
    conv_flops = 6 * ch * channels * width

    def call(kernel, inputs, shapes, scratch=(), hbm_in=(), hbm_out=(), estimate=None, mib=24, **kw):
        inputs = [pltpu.with_memory_space_constraint(x, pltpu.HBM) if i in hbm_in else x for i, x in enumerate(inputs)]
        return pl.pallas_call(
            kernel,
            out_shape=[pltpu.HBM(x.shape, x.dtype) if i in hbm_out else x for i, x in enumerate(shapes)],
            in_specs=[SMEM] + [HBM if i in hbm_in else VMEM for i in range(len(inputs))],
            out_specs=[HBM if i in hbm_out else VMEM for i in range(len(shapes))],
            scratch_shapes=list(scratch),
            compiler_params=params(mib),
            cost_estimate=estimate,
            **kw,
        )(meta, *inputs)

    def array(shape, dtype=BF16):
        return jax.ShapeDtypeStruct(shape, dtype)

    edges = array((ch, 256))
    first, second = call(
        functools.partial(edge_kernel, **sizes),
        [sequence_in, tower_grad],
        [edges, edges],
        scratch=[pltpu.VMEM((2, ch, 128), BF16), pltpu.VMEM((2, ch, 128), F32), pltpu.SemaphoreType.DMA((4,))],
        hbm_in=(0, 1),
        name="edge",
    )
    pairs = [(i, i + 1) for i in range(1, n_seq - 1, 2)]
    first = lax.ppermute(first, "seq", [(i, i ^ 1) for i in range(n_seq)])
    second = lax.ppermute(second, "seq", pairs + [(j, i) for i, j in pairs])
    gain_cols = jnp.pad(norm_gain.T, ((0, 0), (0, 128 - LAYERS)))
    state, halo_grad = call(
        functools.partial(window_kernel, **sizes),
        [sequence_in, first, second, gain_cols],
        [array((ch, width)), array((ch, 128), F32)],
        scratch=[pltpu.VMEM((ch, length), BF16), pltpu.SemaphoreType.DMA],
        hbm_in=(0,),
        name="window",
    )

    record = pl.pallas_call(
        functools.partial(record_kernel, span=length),
        out_shape=array((16, length)),
        in_specs=[VMEM] * 5,
        out_specs=VMEM,
        compiler_params=params(),
        name="record",
    )(*(x.reshape(1, share) for x in (donor_offset, acceptor_owner, acceptor_offset, tissue, score_grad)))
    table = lax.dynamic_slice_in_dim(tissue_scale, me * ch, ch, 1)
    table = jnp.pad(table, ((0, -table.shape[0] % 128), (0, 0)))

    def forward(layer, own, extra):
        wide = length if layer == 0 else width
        final = layer == LAYERS - 1
        shapes = [
            array((ch + 16, length) if final else (ch, width)),
            array((n_tp, ch, wide)),
            array((8, width), F32),
            array((n_tp // 2, ch, length) if layer == 0 and paired else (ch, length)),
        ]
        if layer == 0:
            shapes.append(array((n_tp, ch, 128), F32))
        return call(
            functools.partial(forward_kernel, layer=layer, length=length, **sizes),
            [weights, own, *gather_tp(own), *extra],
            shapes,
            scratch=[
                pltpu.VMEM((n_tp, ch, width), BF16),
                pltpu.VMEM((n_tp, ch, wide), BF16),
                pltpu.VMEM((3 * ch, channels), BF16),
                pltpu.SemaphoreType.DMA((2,)),
            ],
            hbm_in=(0,),
            hbm_out=(1,),
            estimate=cost(conv_flops, 4 * channels * width, channels * width),
            name="forward",
        )

    state1, slope0, inverse0, hidden0, gains = forward(0, state, [])
    state2, slope1, inverse1, hidden1 = forward(1, state1, [gains])
    state3, slope2, inverse2, hidden2 = forward(2, state2, [gains, record])
    slopes = [slope0, slope1, slope2]
    stored = [(sequence_in, inverse0), (state1, inverse1), (state2, inverse2)]
    planned = paired and n_seq == 4

    if planned:
        pieces = gather_seq(state3)
        first = lax.all_gather(hidden0, "seq", axis=0)
        rest = jnp.concatenate([hidden1, hidden2], axis=0)
        rest = lax.all_gather(rest, ("seq", "pair"), axis=0).reshape(n_seq, n_tp // 2, 2, ch, length)
    else:
        pieces = gather_seq(state3)
        everything = [
            [lax.all_gather(h, ("seq",) + TP, axis=0).reshape(n_seq, n_tp, ch, length)]
            for h in (hidden0, hidden1, hidden2)
        ]

    def product_shapes(layer):
        wide = length if layer == 0 else width
        if paired:
            return [array((n_tp // 2, ch, wide)), array((n_tp // 2 * ch + 16, wide))]
        return [array((n_tp, ch, wide)), array((8, wide), F32)]

    def scratch(layer):
        wide = length if layer == 0 else width
        return [
            pltpu.VMEM((3 * ch, channels), BF16),
            pltpu.VMEM((3 * ch, wide), BF16),
            pltpu.VMEM((n_tp, ch, wide), BF16),
        ]

    def reduce_tp(products):
        if not paired:
            whole, extra = products
            own = lax.psum_scatter(whole.reshape(channels, -1), TP, scatter_dimension=0, tiled=True)
            return [jnp.concatenate([own.astype(F32), lax.psum(extra, TP)], axis=0)]
        keep, send = products
        wide = keep.shape[2]
        got = swap(send, TP, 1)
        far = array((ch + 16, wide))
        own, *far = pl.pallas_call(
            pair_kernel,
            out_shape=[array((ch + 8, wide), F32), far, far, far],
            in_specs=[VMEM] * 3,
            out_specs=[VMEM] * 4,
            compiler_params=params(),
            name="pair",
        )(keep, send, got)
        return [own] + [swap(v, TP, 2 * r + 2) for r, v in enumerate(far)]

    upstream, grad2, *products = call(
        functools.partial(junction_kernel, share=share, root=math.sqrt(channels), **sizes),
        [weights, slopes[2], tower_grad, halo_grad, table, *pieces],
        [array((ch, width), F32), array((ch, length))] + product_shapes(2),
        scratch=scratch(2)
        + [
            pltpu.VMEM((ch, count), F32),
            pltpu.VMEM((8, count), F32),
            pltpu.VMEM((ch, length), F32),
            pltpu.SemaphoreType.DMA((3,)),
        ],
        hbm_in=(0, 1, 2),
        estimate=cost(4 * conv_flops, 4 * channels * width),
        mib=32,
        name="junction",
    )

    def backward(layer, sums, upstream):
        state, inverse = stored[layer]
        wide = length if layer == 0 else width
        inputs = [*sums, upstream, state, inverse, gain_cols]
        shapes = [array((ch, wide), F32), array((ch, 128), F32)]
        extra, hbm = [], ()
        if layer > 0:
            inputs = [weights, slopes[layer - 1], *inputs]
            hbm = (0, 1)
            shapes.append(array((ch, length)))
            if layer == LAYERS - 1:
                shapes.append(array((8, width), F32))
            shapes += product_shapes(layer - 1)
            extra = scratch(layer - 1) + [pltpu.SemaphoreType.DMA((2,))]
        return call(
            functools.partial(backward_kernel, layer=layer, n_far=n_far, length=length, **sizes),
            inputs,
            shapes,
            scratch=extra,
            hbm_in=hbm,
            estimate=cost(conv_flops, 4 * channels * width),
            name="backward",
        )

    def weigh(layer, path, grads, sources, before):
        inputs = [*grads, *sources, *before]
        return call(
            functools.partial(weight_kernel, layer=layer, path=path, **sizes),
            inputs,
            [array((LAYERS, 3, ch, channels), F32)],
            scratch=[
                pltpu.VMEM((ch, total), BF16),
                pltpu.VMEM((3 * ch, total), BF16),
                pltpu.VMEM((channels // CHUNK, CHUNK // ch, ch, total), BF16),
                pltpu.VMEM((2, 3, ch, CHUNK), F32),
                pltpu.SemaphoreType.DMA((channels // CHUNK, n_seq * (CHUNK // ch))),
                pltpu.SemaphoreType.DMA((2,)),
            ],
            hbm_in=range(n_seq, len(inputs)),
            hbm_out=(0,),
            estimate=cost(6 * ch * channels * total, 2 * channels * total),
            mib=32,
            input_output_aliases={len(inputs): 0} if before else {},
            name="weight",
        )[0]

    sums = reduce_tp(products)
    upstream, part2, grad1, score_rows, *products = backward(2, sums, upstream)
    scores = score_rows[1, :share]

    grads2 = gather_seq(grad2)
    sums = reduce_tp(products)
    if planned:
        near = swap(first, TP, 1)
        sums, (first, near) = tie(sums, [first, near])
    upstream, part1, grad0, *products = backward(1, sums, upstream)

    grads1 = gather_seq(grad1)
    sums = reduce_tp(products)
    if planned:
        sums, grads2 = tie(sums, grads2)
    input_grad, part0 = backward(0, sums, upstream)

    columns = jnp.pad(jnp.stack([p[:, 0] for p in (part0, part1, part2)]), ((0, 8 - LAYERS), (0, 0)))
    pieces = gather_seq(columns)
    if len(pieces) == 4:
        gain_grad = (pieces[0] + pieces[1]) + (pieces[2] + pieces[3])
    else:
        gain_grad = sum(pieces)

    grads0 = gather_seq(grad0)
    if planned:
        weight_grad = weigh(0, "pair", grads0, [first, near], [])
        (rest,), got = tie([rest], [weight_grad, gain_grad, *grads1])
        weight_grad, gain_grad, grads1 = got[0], got[1], got[2:]
        for layer, grads in ((1, grads1), (2, grads2)):
            mine = rest[:, :, layer - 1]
            weight_grad = weigh(layer, "pair", grads, [mine, swap(mine, TP, 1)], [weight_grad])
    else:
        weight_grad = weigh(0, "whole", grads0, everything[0], [])
        weight_grad = weigh(1, "whole", grads1, everything[1], [weight_grad])
        weight_grad = weigh(2, "whole", grads2, everything[2], [weight_grad])
    return (scores, input_grad, weight_grad.transpose(0, 2, 1, 3), gain_grad[:LAYERS])


def solution(mesh):
    tp = mesh.shape["tp"]
    pairs = jax.sharding.Mesh(mesh.devices.reshape(mesh.shape["seq"], tp // 2, 2), ("seq",) + TP)
    return jax.shard_map(
        local,
        mesh=pairs,
        in_specs=(
            P(TP, "seq"),
            P(None, TP, None, None),
            P(None, TP),
            P(),
            P("seq"),
            P("seq", None),
            P("seq"),
            P("seq"),
            P(TP, "seq"),
            P("seq"),
        ),
        out_specs=(P("seq"), P(TP, "seq"), P(None, TP, None, None), P(None, TP)),
        check_vma=False,
    )
```

time: 411 us -> 289 us (0.70); the launches traced: 406 us -> 289 us
  Pallas kernels: 108 us -> 70.4 us
  starting transfers between devices: 80.9 us -> 47.7 us
  local copies, waits for them, and re-layouts: 48.8 us -> 15.7 us
  waiting for transfers between devices: 148 us -> 140 us
    pallas_call x15 -> x13, Pallas kernels: 108 us -> 69.7 us  [the longest x12 69.7 us: call(): pl.pallas_call(kernel, out_shape=[pltpu.HBM(x.shape, x.dtype) if i in hbm...]
    unnamed x136 -> x53, local copies, waits for them, and re-layouts: 45.1 us -> 9.59 us
    ppermute x66 -> x53, starting transfers between devices: 80.9 us -> 47.6 us  [the longest x51 43.8 us: swap(): return lax.ppermute(x, axis, [(i, i ^ mask) for i in range(size_of(axis))])]
    ppermute x66 -> x53, waiting for transfers between devices: 148 us -> 138 us  [the longest x51 137 us: swap(): return lax.ppermute(x, axis, [(i, i ^ mask) for i in range(size_of(axis))])]
  transfers between devices with their start and end apart: 67 -> 55, of which waited for: 25 -> 28; matrix products, arithmetic and copies ran while one was open for 2% -> 1% of each run, Pallas kernels for 23% -> 17%
where the time goes in v3:
time: 289 us
  waiting for transfers between devices  140 us (48%)
  Pallas kernels  70.4 us (24%)
  starting transfers between devices  47.7 us (17%)
  local copies, waits for them, and re-layouts  15.7 us (5%)
  between operations  14.6 us (5%)
    ppermute x51, waiting for transfers between devices, swap(): return lax.ppermute(x, axis, [(i, i ^ mask) for i in range(size_of(axis))])  137 us
    pallas_call x12, Pallas kernels, call(): pl.pallas_call(kernel, out_shape=[pltpu.HBM(x.shape, x.dtype) if i in hbm...  69.7 us
    ppermute x51, starting transfers between devices, swap(): return lax.ppermute(x, axis, [(i, i ^ mask) for i in range(size_of(axis))])  43.8 us
    unnamed x53, local copies, waits for them, and re-layouts  9.59 us
  transfers between devices with their start and end apart: 55, of which 28 were waited for; matrix products, arithmetic and copies ran while one was open for 1% of the time, Pallas kernels for 17%

profile of v3, /device:TPU:0, one launch (start us, length us, event | category | flops | bytes accessed | tf_op | source)
XLA Modules:
  0.0 288.8 jit_solution(17292550480409118874)
XLA Ops:
  7.3 1.8 edge.1
  9.1 3.1 %collective-permute-start = (bf16[192,256]{1,0:T(8,128)(2,1)S(1)}, bf16[192,256]{1,0:T(8,128)(2,1)S(1)}, u32[]{:S(2)}, u32[]{:S(2)}) collective-permute-start(bf16[192,256]{1,0:T(8,128)(2,1)S(1)} %get-tuple-element.71), channel_id=1, source_target_pairs={{0,8},{8,0},{16,24},{24,16},{1,9},{9,1},{17,25},{25,17},{2,10},{10... | collective-permute-start | bytes 294920 | tf_op jit(solution)/shard_map/ppermute | solution.py:553
  13.7 1.3 collective-permute-done.first_ref
  15.0 1.6 window.1
  17.3 2.7 collective-permute-start.7
  20.8 6.3 %collective-permute-done.7.refs_6_ = bf16[192,640]{1,0:T(8,128)(2,1)S(1)} collective-permute-done((bf16[192,640]{1,0:T(8,128)(2,1)S(1)}, bf16[192,640]{1,0:T(8,128)(2,1)S(1)}, u32[]{:S(2)}, u32[]{:S(2)}) %collective-permute-start.7) | collective-permute-done | bytes 245792 | tf_op jit(solution)/shard_map/ppermute | solution.py:51
  27.1 3.5 %collective-permute-done.5.refs_4_ = bf16[192,640]{1,0:T(8,128)(2,1)S(1)} collective-permute-done((bf16[192,640]{1,0:T(8,128)(2,1)S(1)}, bf16[192,640]{1,0:T(8,128)(2,1)S(1)}, u32[]{:S(2)}, u32[]{:S(2)}) %collective-permute-start.5) | collective-permute-done | bytes 245792 | tf_op jit(solution)/shard_map/ppermute | solution.py:51
  31.1 1.0 collective-permute-done.6.refs_5_
  32.5 7.6 %forward.3 = (bf16[192,640]{1,0:T(8,128)(2,1)S(1)}, bf16[8,192,512]{2,1,0:T(8,128)(2,1)}, f32[8,640]{1,0:T(8,128)S(1)}, bf16[4,192,512]{2,1,0:T(8,128)(2,1)S(1)}, f32[8,192,128]{2,1,0:T(8,128)S(1)}) custom-call(s32[14]{0:T(128)S(1)} %pad_add_fusion.meta, bf16[3,576,1536]{2,1,0:T(8,128)(2,1)} %bitcast.27, ...), custom_call_target="tpu_custom_call" | custom-call | flops 1132462080 | bytes 3932160 | tf_op jit(solution)/shard_map/forward/pallas_call | solution.py:529
  40.1 0.9 copy-done.4
  41.7 1.8 collective-permute-start.14
  43.5 0.8 collective-permute-start.12
  44.4 0.9 collective-permute-start.10
  45.3 6.2 %collective-permute-done.14.refs_6_ = bf16[192,640]{1,0:T(8,128)(2,1)S(1)} collective-permute-done((bf16[192,640]{1,0:T(8,128)(2,1)S(1)}, bf16[192,640]{1,0:T(8,128)(2,1)S(1)}, u32[]{:S(2)}, u32[]{:S(2)}) %collective-permute-start.14) | collective-permute-done | bytes 245792 | tf_op jit(solution)/shard_map/ppermute | solution.py:51
  51.5 4.4 %collective-permute-done.12.refs_4_ = bf16[192,640]{1,0:T(8,128)(2,1)S(1)} collective-permute-done((bf16[192,640]{1,0:T(8,128)(2,1)S(1)}, bf16[192,640]{1,0:T(8,128)(2,1)S(1)}, u32[]{:S(2)}, u32[]{:S(2)}) %collective-permute-start.12) | collective-permute-done | bytes 245792 | tf_op jit(solution)/shard_map/ppermute | solution.py:51
  56.5 1.0 collective-permute-done.13.refs_5_
  57.8 6.1 %forward.4 = (bf16[192,640]{1,0:T(8,128)(2,1)S(1)}, bf16[8,192,640]{2,1,0:T(8,128)(2,1)}, f32[8,640]{1,0:T(8,128)S(1)}, bf16[192,512]{1,0:T(8,128)(2,1)S(1)}) custom-call(s32[14]{0:T(128)S(1)} %pad_add_fusion.meta, bf16[3,576,1536]{2,1,0:T(8,128)(2,1)} %bitcast.28, bf16[192,640]{1,0:T(8,128)(2,1)S(1)} %get-tuple-element.74.own_ref.refs_0_.refs_7_, ...), custom_call_target="tpu_custom_call" | custom-call | flops 1132462080 | bytes 3932160 | tf_op jit(solution)/shard_map/forward/pallas_call | solution.py:529
  64.0 1.8 collective-permute-start.21
  65.8 0.9 collective-permute-start.19
  66.7 0.9 collective-permute-start.17
  67.6 6.2 %collective-permute-done.21.refs_6_ = bf16[192,640]{1,0:T(8,128)(2,1)S(1)} collective-permute-done((bf16[192,640]{1,0:T(8,128)(2,1)S(1)}, bf16[192,640]{1,0:T(8,128)(2,1)S(1)}, u32[]{:S(2)}, u32[]{:S(2)}) %collective-permute-start.21) | collective-permute-done | bytes 245792 | tf_op jit(solution)/shard_map/ppermute | solution.py:51
  73.8 4.4 %collective-permute-done.19.refs_4_ = bf16[192,640]{1,0:T(8,128)(2,1)S(1)} collective-permute-done((bf16[192,640]{1,0:T(8,128)(2,1)S(1)}, bf16[192,640]{1,0:T(8,128)(2,1)S(1)}, u32[]{:S(2)}, u32[]{:S(2)}) %collective-permute-start.19) | collective-permute-done | bytes 245792 | tf_op jit(solution)/shard_map/ppermute | solution.py:51
  78.8 0.9 collective-permute-done.20.refs_5_
  80.1 6.1 %forward.5 = (bf16[208,512]{1,0:T(8,128)(2,1)S(1)}, bf16[8,192,640]{2,1,0:T(8,128)(2,1)}, f32[8,640]{1,0:T(8,128)S(1)}, bf16[192,512]{1,0:T(8,128)(2,1)S(1)}) custom-call(s32[14]{0:T(128)S(1)} %pad_add_fusion.meta, bf16[3,576,1536]{2,1,0:T(8,128)(2,1)} %bitcast.29, bf16[192,640]{1,0:T(8,128)(2,1)S(1)} %get-tuple-element.77.own_ref.refs_0_.refs_7_, ...), custom_call_target="tpu_custom_call" | custom-call | flops 1132462080 | bytes 3932160 | tf_op jit(solution)/shard_map/forward/pallas_call | solution.py:529
  87.6 0.8 pad_maximum_fusion
  88.4 5.5 %collective-permute-start.24 = (bf16[208,512]{1,0:T(8,128)(2,1)}, bf16[208,512]{1,0:T(8,128)(2,1)S(1)}, u32[]{:S(2)}, u32[]{:S(2)}) collective-permute-start(bf16[208,512]{1,0:T(8,128)(2,1)} %copy-done.15), channel_id=1, source_target_pairs={{0,16},{8,24},{16,0},{24,8},{1,17},{9,25},{17,1},{25,9},{2,18},{10... | collective-permute-start | bytes 638984 | tf_op jit(solution)/shard_map/ppermute | solution.py:51
  93.9 21.2 %collective-permute-done.24.refs_2_ = bf16[208,512]{1,0:T(8,128)(2,1)S(1)} collective-permute-done((bf16[208,512]{1,0:T(8,128)(2,1)}, bf16[208,512]{1,0:T(8,128)(2,1)S(1)}, u32[]{:S(2)}, u32[]{:S(2)}) %collective-permute-start.24) | collective-permute-done | bytes 213024 | tf_op jit(solution)/shard_map/ppermute | solution.py:51
  115.1 1.7 all-gather.5.cloned.1.call-done
  117.0 5.3 %collective-permute-done.25.refs_3_ = bf16[208,512]{1,0:T(8,128)(2,1)} collective-permute-done((bf16[208,512]{1,0:T(8,128)(2,1)S(1)}, bf16[208,512]{1,0:T(8,128)(2,1)}, u32[]{:S(2)}, u32[]{:S(2)}) %collective-permute-start.25) | collective-permute-done | bytes 213024 | tf_op jit(solution)/shard_map/ppermute | solution.py:51
  122.3 0.9 copy-done.16
  123.2 0.9 copy-done.18
  124.1 7.4 %junction.1 = (f32[192,640]{1,0:T(8,128)S(1)}, bf16[192,512]{1,0:T(8,128)(2,1)S(1)}, bf16[4,192,640]{2,1,0:T(8,128)(2,1)S(1)}, bf16[784,640]{1,0:T(8,128)(2,1)S(1)}) custom-call(s32[14]{0:T(128)S(1)} %pad_add_fusion.meta, bf16[3,576,1536]{2,1,0:T(8,128)(2,1)} %bitcast.30, bf16[8,192,640]{2,1,0:T(8,128)(2,1)} %get-tuple-element.78.slope_ref, ...), custom_call_target="tpu_custom_call" | custom-call | flops 4529848320 | bytes 3932160 | tf_op jit(solution)/shard_map/junction/pallas_call | solution.py:529
  131.6 2.6 collective-permute-done.26.got_ref
  134.4 1.6 collective-permute-start.27
  136.1 1.8 collective-permute-start.29
  138.0 5.7 %collective-permute-done.27.refs_3_ = bf16[208,640]{1,0:T(8,128)(2,1)S(1)} collective-permute-done((bf16[208,640]{1,0:T(8,128)(2,1)S(1)}, bf16[208,640]{1,0:T(8,128)(2,1)S(1)}, u32[]{:S(2)}, u32[]{:S(2)}) %collective-permute-start.27) | collective-permute-done | bytes 266272 | tf_op jit(solution)/shard_map/ppermute | solution.py:51
  143.7 6.2 %collective-permute-done.28.refs_4_ = bf16[208,640]{1,0:T(8,128)(2,1)S(1)} collective-permute-done((bf16[208,640]{1,0:T(8,128)(2,1)S(1)}, bf16[208,640]{1,0:T(8,128)(2,1)S(1)}, u32[]{:S(2)}, u32[]{:S(2)}) %collective-permute-start.28) | collective-permute-done | bytes 266272 | tf_op jit(solution)/shard_map/ppermute | solution.py:51
  150.3 5.3 %backward.3 = (f32[192,640]{1,0:T(8,128)S(1)}, f32[192,128]{1,0:T(8,128)S(1)}, bf16[192,512]{1,0:T(8,128)(2,1)S(1)}, f32[8,640]{1,0:T(8,128)S(1)}, bf16[4,192,64...) custom-call(s32[14]{0:T(128)S(1)} %pad_add_fusion.meta, bf16[3,576,1536]{2,1,0:T(8,128)(2,1)} %bitcast.31, ...), custom_call_target="tpu_custom_call" | custom-call | flops 1132462080 | bytes 3932160 | tf_op jit(solution)/shard_map/backward/pallas_call | solution.py:529
  155.7 2.6 collective-permute-done.30.got_ref
  159.3 2.8 collective-permute-start.32
  162.1 5.7 %collective-permute-done.31.refs_3_ = bf16[208,640]{1,0:T(8,128)(2,1)S(1)} collective-permute-done((bf16[208,640]{1,0:T(8,128)(2,1)S(1)}, bf16[208,640]{1,0:T(8,128)(2,1)S(1)}, u32[]{:S(2)}, u32[]{:S(2)}) %collective-permute-start.31) | collective-permute-done | bytes 266272 | tf_op jit(solution)/shard_map/ppermute | solution.py:51
  167.8 6.4 %collective-permute-done.32.refs_4_ = bf16[208,640]{1,0:T(8,128)(2,1)S(1)} collective-permute-done((bf16[208,640]{1,0:T(8,128)(2,1)S(1)}, bf16[208,640]{1,0:T(8,128)(2,1)S(1)}, u32[]{:S(2)}, u32[]{:S(2)}) %collective-permute-start.32) | collective-permute-done | bytes 266272 | tf_op jit(solution)/shard_map/ppermute | solution.py:51
  174.3 4.9 %backward.4 = (f32[192,640]{1,0:T(8,128)S(1)}, f32[192,128]{1,0:T(8,128)S(1)}, bf16[192,512]{1,0:T(8,128)(2,1)S(1)}, bf16[4,192,512]{2,1,0:T(8,128)(2,1)S(1)}, bf16[784,512]{1,0:T(8,128)(2,1)S(1)}) custom-call(s32[14]{0:T(128)S(1)} %pad_add_fusion.meta, bf16[3,576,1536]{2,1,0:T(8,128)(2,1)} %bitcast.32, bf16[8,192,512]{2,1,0:T(8,128)(2,1)} %get-tuple-element.90.refs_1_, ...), custom_call_target="tpu_custom_call" | custom-call | flops 1132462080 | bytes 3932160 | tf_op jit(solution)/shard_map/backward/pallas_call | solution.py:529
  180.0 1.5 collective-permute-start.39
  181.5 18.5 %collective-permute-done.40.refs_2_ = bf16[192,512]{1,0:T(8,128)(2,1)S(1)} collective-permute-done((bf16[192,512]{1,0:T(8,128)(2,1)S(1)}, bf16[192,512]{1,0:T(8,128)(2,1)S(1)}, u32[]{:S(2)}, u32[]{:S(2)}) %collective-permute-start.40) | collective-permute-done | bytes 196640 | tf_op jit(solution)/shard_map/ppermute | solution.py:51
  200.0 2.6 collective-permute-start.43
  203.5 2.8 collective-permute-start.38
  206.5 13.5 %collective-permute-done.41.refs_3_ = bf16[192,512]{1,0:T(8,128)(2,1)S(1)} collective-permute-done((bf16[192,512]{1,0:T(8,128)(2,1)S(1)}, bf16[192,512]{1,0:T(8,128)(2,1)S(1)}, u32[]{:S(2)}, u32[]{:S(2)}) %collective-permute-start.41) | collective-permute-done | bytes 196640 | tf_op jit(solution)/shard_map/ppermute | solution.py:51
  220.1 1.8 collective-permute-done.43.refs_2_
  222.3 1.6 collective-permute-start.44
  223.9 1.8 backward.5
  225.8 1.2 collective-permute-start.46
  227.6 8.3 %collective-permute-done.49.refs_2_ = bf16[192,512]{1,0:T(8,128)(2,1)S(1)} collective-permute-done((bf16[192,512]{1,0:T(8,128)(2,1)S(1)}, bf16[192,512]{1,0:T(8,128)(2,1)S(1)}, u32[]{:S(2)}, u32[]{:S(2)}) %collective-permute-start.49) | collective-permute-done | bytes 196640 | tf_op jit(solution)/shard_map/ppermute | solution.py:51
  236.0 2.0 collective-permute-start.45
  238.0 4.1 %collective-permute-start.47 = (f32[8,192]{1,0:T(8,128)S(1)}, f32[8,192]{1,0:T(8,128)S(1)}, u32[]{:S(2)}, u32[]{:S(2)}) collective-permute-start(f32[8,192]{1,0:T(8,128)S(1)} %collective-permute-done.46), channel_id=1, source_target_pairs={{0,8},{8,0},{16,24},{24,16},{1,9},{9,1},{17,25},{25,17},{2,10},{10... | collective-permute-start | bytes 18440 | tf_op jit(solution)/shard_map/ppermute | solution.py:51
  242.1 9.0 %weight.3.refs_6_ = f32[3,3,192,1536]{3,2,1,0:T(8,128)} custom-call(s32[14]{0:T(128)S(1)} %pad_add_fusion.meta, bf16[192,512]{1,0:T(8,128)(2,1)S(1)} %get-tuple-element.124.refs_0_, bf16[192,512]{1,0:T(8,128)(2,1)S(1)} %collective-permute-done.42.refs_1_, bf16[192,512]{1,0:T(8,128)(2,1)S(1)} %collective-permute-done.43.refs_2_, ...), custom_call_target="tpu_custom_call" | custom-call | flops 3623878656 | bytes 6291456 | tf_op jit(solution)/shard_map/weight/pallas_call | solution.py:529
  251.2 3.5 %slice_bitcast_fusion = (bf16[4,4,192,512]{3,2,1,0:T(8,128)(2,1)S(1)}, bf16[4,4,192,512]{3,2,1,0:T(8,128)(2,1)S(1)}) fusion(bf16[4,4,2,192,512]{4,3,2,1,0:T(8,128)(2,1)} %bitcast.34), kind=kLoop, calls=%fused_computation | loop fusion | bytes 12582912 | tf_op jit(solution)/shard_map/squeeze | solution.py:748
  255.3 1.0 slice.21
  256.2 1.1 slice.27
  257.4 3.1 %collective-permute-done.52.refs_5_ = bf16[4,4,192,512]{3,2,1,0:T(8,128)(2,1)S(1)} collective-permute-done((bf16[4,4,192,512]{3,2,1,0:T(8,128)(2,1)S(1)}, bf16[4,4,192,512]{3,2,1,0:T(8,128)(2,1)S(1)}, u32[]{:S(2)}, u32[]{:S(2)}) %collective-permute-start.52) | collective-permute-done | bytes 3145760 | tf_op jit(solution)/shard_map/ppermute | solution.py:51
  260.4 1.8 copy-done.25
  262.2 9.0 %weight.4.refs_6_ = f32[3,3,192,1536]{3,2,1,0:T(8,128)} custom-call(s32[14]{0:T(128)S(1)} %pad_add_fusion.meta, bf16[192,512]{1,0:T(8,128)(2,1)S(1)} %get-tuple-element.132.refs_0_, bf16[192,512]{1,0:T(8,128)(2,1)S(1)} %collective-permute-done.48.refs_1_, bf16[192,512]{1,0:T(8,128)(2,1)S(1)} %collective-permute-done.49.refs_2_, ...), custom_call_target="tpu_custom_call", output_to_operand_aliasing={{}: (7, {})} | custom-call | flops 3623878656 | bytes 6291456 | tf_op jit(solution)/shard_map/weight/pallas_call | solution.py:529
  271.2 1.7 copy-done.24
  272.9 9.1 %weight.5 = f32[3,3,192,1536]{3,2,1,0:T(8,128)} custom-call(s32[14]{0:T(128)S(1)} %pad_add_fusion.meta, bf16[192,512]{1,0:T(8,128)(2,1)S(1)} %get-tuple-element.118.refs_0_, bf16[192,512]{1,0:T(8,128)(2,1)S(1)} %collective-permute-done.39.refs_1_, bf16[192,512]{1,0:T(8,128)(2,1)S(1)} %collective-permute-done.40.refs_2_, ...), custom_call_target="tpu_custom_call", output_to_operand_aliasing={{}: (7, {})} | custom-call | flops 3623878656 | bytes 6291456 | tf_op jit(solution)/shard_map/weight/pallas_call | solution.py:529
  (132 shorter events, 13.6 us)
Async XLA Ops:
  7.2 109.6 %copy-start = (f32[367,1536]{1,0:T(8,128)S(1)}, f32[367,1536]{1,0:T(8,128)}, u32[]{:S(2)}) copy-start(f32[367,1536]{1,0:T(8,128)} %param.13) | copy-start | bytes 6764548
  7.2 109.5 %all-gather.5.cloned.1.call-start = ((), (), s32[]{:S(2)}) async-start(), calls=%async_computation | async-start | bytes 3932160 | tf_op jit(solution)/shard_map/all_gather | solution.py:612
  9.1 5.9 %collective-permute-start = (bf16[192,256]{1,0:T(8,128)(2,1)S(1)}, bf16[192,256]{1,0:T(8,128)(2,1)S(1)}, u32[]{:S(2)}, u32[]{:S(2)}) collective-permute-start(bf16[192,256]{1,0:T(8,128)(2,1)S(1)} %get-tuple-element.71), channel_id=1, source_target_pairs={{0,8},{8,0},{16,24},{24,16},{1,9},{9,1},{17,25},{25,17},{2,10},{10... | collective-permute-start | bytes 294920 | tf_op jit(solution)/shard_map/ppermute | solution.py:553
  12.2 2.8 collective-permute-start.1
  17.3 9.8 %collective-permute-start.7 = (bf16[192,640]{1,0:T(8,128)(2,1)S(1)}, bf16[192,640]{1,0:T(8,128)(2,1)S(1)}, u32[]{:S(2)}, u32[]{:S(2)}) collective-permute-start(bf16[192,640]{1,0:T(8,128)(2,1)S(1)} %get-tuple-element.73.own_ref.refs_0_), channel_id=1, source_target_pairs={{0,6},{1,7},{2,4},{3,5},{4,2},{5,3},{6,0},{7,1},{8,14},{9,15},{10,... | collective-permute-start | bytes 737288 | tf_op jit(solution)/shard_map/ppermute | solution.py:51
  20.0 10.6 %collective-permute-start.5 = (bf16[192,640]{1,0:T(8,128)(2,1)S(1)}, bf16[192,640]{1,0:T(8,128)(2,1)S(1)}, u32[]{:S(2)}, u32[]{:S(2)}) collective-permute-start(bf16[192,640]{1,0:T(8,128)(2,1)S(1)} %get-tuple-element.73.own_ref.refs_0_), channel_id=1, source_target_pairs={{0,4},{1,5},{2,6},{3,7},{4,0},{5,1},{6,2},{7,3},{8,12},{9,13},{10,... | collective-permute-start | bytes 737288 | tf_op jit(solution)/shard_map/ppermute | solution.py:51
  20.5 10.1 %collective-permute-start.3 = (bf16[192,640]{1,0:T(8,128)(2,1)S(1)}, bf16[192,640]{1,0:T(8,128)(2,1)S(1)}, u32[]{:S(2)}, u32[]{:S(2)}) collective-permute-start(bf16[192,640]{1,0:T(8,128)(2,1)S(1)} %get-tuple-element.73.own_ref.refs_0_), channel_id=1, source_target_pairs={{0,2},{1,3},{2,0},{3,1},{4,6},{5,7},{6,4},{7,5},{8,10},{9,11},{10,... | collective-permute-start | bytes 737288 | tf_op jit(solution)/shard_map/ppermute | solution.py:51
  20.8 10.3 %collective-permute-start.2 = (bf16[192,640]{1,0:T(8,128)(2,1)S(1)}, bf16[192,640]{1,0:T(8,128)(2,1)S(1)}, u32[]{:S(2)}, u32[]{:S(2)}) collective-permute-start(bf16[192,640]{1,0:T(8,128)(2,1)S(1)} %get-tuple-element.73.own_ref.refs_0_), channel_id=1, source_target_pairs={{0,1},{1,0},{2,3},{3,2},{4,5},{5,4},{6,7},{7,6},{8,9},{9,8},{10,11... | collective-permute-start | bytes 737288 | tf_op jit(solution)/shard_map/ppermute | solution.py:51
  27.1 4.0 %collective-permute-start.8 = (bf16[192,640]{1,0:T(8,128)(2,1)S(1)}, bf16[192,640]{1,0:T(8,128)(2,1)S(1)}, u32[]{:S(2)}, u32[]{:S(2)}) collective-permute-start(bf16[192,640]{1,0:T(8,128)(2,1)S(1)} %collective-permute-done.7.refs_6_), channel_id=1, source_target_pairs={{0,1},{1,0},{2,3},{3,2},{4,5},{5,4},{6,7},{7,6},{8,9},{9,8},{10,11... | collective-permute-start | bytes 737288 | tf_op jit(solution)/shard_map/ppermute | solution.py:51
  30.6 1.5 collective-permute-start.6
  30.6 1.8 collective-permute-start.4
  41.7 209.5 %all-gather.7.cloned.1.call-start = ((), (), s32[]{:S(2)}) async-start(), calls=%async_computation.1 | async-start | bytes 6684672 | tf_op jit(solution)/shard_map/all_gather | solution.py:614
  41.7 9.8 %collective-permute-start.14 = (bf16[192,640]{1,0:T(8,128)(2,1)S(1)}, bf16[192,640]{1,0:T(8,128)(2,1)S(1)}, u32[]{:S(2)}, u32[]{:S(2)}) collective-permute-start(bf16[192,640]{1,0:T(8,128)(2,1)S(1)} %get-tuple-element.74.own_ref.refs_0_.refs_7_), channel_id=1, source_target_pairs={{0,6},{1,7},{2,4},{3,5},{4,2},{5,3},{6,0},{7,1},{8,14},{9,15},{10,... | collective-permute-start | bytes 737288 | tf_op jit(solution)/shard_map/ppermute | solution.py:51
  43.5 12.4 %collective-permute-start.12 = (bf16[192,640]{1,0:T(8,128)(2,1)S(1)}, bf16[192,640]{1,0:T(8,128)(2,1)S(1)}, u32[]{:S(2)}, u32[]{:S(2)}) collective-permute-start(bf16[192,640]{1,0:T(8,128)(2,1)S(1)} %get-tuple-element.74.own_ref.refs_0_.refs_7_), channel_id=1, source_target_pairs={{0,4},{1,5},{2,6},{3,7},{4,0},{5,1},{6,2},{7,3},{8,12},{9,13},{10,... | collective-permute-start | bytes 737288 | tf_op jit(solution)/shard_map/ppermute | solution.py:51
  44.4 11.7 %collective-permute-start.10 = (bf16[192,640]{1,0:T(8,128)(2,1)S(1)}, bf16[192,640]{1,0:T(8,128)(2,1)S(1)}, u32[]{:S(2)}, u32[]{:S(2)}) collective-permute-start(bf16[192,640]{1,0:T(8,128)(2,1)S(1)} %get-tuple-element.74.own_ref.refs_0_.refs_7_), channel_id=1, source_target_pairs={{0,2},{1,3},{2,0},{3,1},{4,6},{5,7},{6,4},{7,5},{8,10},{9,11},{10,... | collective-permute-start | bytes 737288 | tf_op jit(solution)/shard_map/ppermute | solution.py:51
  45.3 11.2 %collective-permute-start.9 = (bf16[192,640]{1,0:T(8,128)(2,1)S(1)}, bf16[192,640]{1,0:T(8,128)(2,1)S(1)}, u32[]{:S(2)}, u32[]{:S(2)}) collective-permute-start(bf16[192,640]{1,0:T(8,128)(2,1)S(1)} %get-tuple-element.74.own_ref.refs_0_.refs_7_), channel_id=1, source_target_pairs={{0,1},{1,0},{2,3},{3,2},{4,5},{5,4},{6,7},{7,6},{8,9},{9,8},{10,11... | collective-permute-start | bytes 737288 | tf_op jit(solution)/shard_map/ppermute | solution.py:51
  51.5 5.0 %collective-permute-start.15 = (bf16[192,640]{1,0:T(8,128)(2,1)S(1)}, bf16[192,640]{1,0:T(8,128)(2,1)S(1)}, u32[]{:S(2)}, u32[]{:S(2)}) collective-permute-start(bf16[192,640]{1,0:T(8,128)(2,1)S(1)} %collective-permute-done.14.refs_6_), channel_id=1, source_target_pairs={{0,1},{1,0},{2,3},{3,2},{4,5},{5,4},{6,7},{7,6},{8,9},{9,8},{10,11... | collective-permute-start | bytes 737288 | tf_op jit(solution)/shard_map/ppermute | solution.py:51
  56.0 1.5 collective-permute-start.13
  56.1 1.7 collective-permute-start.11
  57.8 20.9 %copy-start.13 = (s32[256]{0:T(256)S(1)}, s32[256]{0:T(256)}, u32[]{:S(2)}) copy-start(s32[256]{0:T(256)} %param.17) | copy-start | bytes 3076
  57.8 20.9 %copy-start.14 = (f32[256]{0:T(256)S(1)}, f32[256]{0:T(256)}, u32[]{:S(2)}) copy-start(f32[256]{0:T(256)} %param.19) | copy-start | bytes 3076
  64.0 22.3 %copy-start.6 = (f32[8,640]{1,0:T(8,128)}, f32[8,640]{1,0:T(8,128)S(1)}, u32[]{:S(2)}) copy-start(f32[8,640]{1,0:T(8,128)S(1)} %get-tuple-element.103.refs_8_) | copy-start | bytes 61444
  64.0 9.8 %collective-permute-start.21 = (bf16[192,640]{1,0:T(8,128)(2,1)S(1)}, bf16[192,640]{1,0:T(8,128)(2,1)S(1)}, u32[]{:S(2)}, u32[]{:S(2)}) collective-permute-start(bf16[192,640]{1,0:T(8,128)(2,1)S(1)} %get-tuple-element.77.own_ref.refs_0_.refs_7_), channel_id=1, source_target_pairs={{0,6},{1,7},{2,4},{3,5},{4,2},{5,3},{6,0},{7,1},{8,14},{9,15},{10,... | collective-permute-start | bytes 737288 | tf_op jit(solution)/shard_map/ppermute | solution.py:51
  65.8 12.4 %collective-permute-start.19 = (bf16[192,640]{1,0:T(8,128)(2,1)S(1)}, bf16[192,640]{1,0:T(8,128)(2,1)S(1)}, u32[]{:S(2)}, u32[]{:S(2)}) collective-permute-start(bf16[192,640]{1,0:T(8,128)(2,1)S(1)} %get-tuple-element.77.own_ref.refs_0_.refs_7_), channel_id=1, source_target_pairs={{0,4},{1,5},{2,6},{3,7},{4,0},{5,1},{6,2},{7,3},{8,12},{9,13},{10,... | collective-permute-start | bytes 737288 | tf_op jit(solution)/shard_map/ppermute | solution.py:51
  66.7 11.7 %collective-permute-start.17 = (bf16[192,640]{1,0:T(8,128)(2,1)S(1)}, bf16[192,640]{1,0:T(8,128)(2,1)S(1)}, u32[]{:S(2)}, u32[]{:S(2)}) collective-permute-start(bf16[192,640]{1,0:T(8,128)(2,1)S(1)} %get-tuple-element.77.own_ref.refs_0_.refs_7_), channel_id=1, source_target_pairs={{0,2},{1,3},{2,0},{3,1},{4,6},{5,7},{6,4},{7,5},{8,10},{9,11},{10,... | collective-permute-start | bytes 737288 | tf_op jit(solution)/shard_map/ppermute | solution.py:51
  67.6 11.3 %collective-permute-start.16 = (bf16[192,640]{1,0:T(8,128)(2,1)S(1)}, bf16[192,640]{1,0:T(8,128)(2,1)S(1)}, u32[]{:S(2)}, u32[]{:S(2)}) collective-permute-start(bf16[192,640]{1,0:T(8,128)(2,1)S(1)} %get-tuple-element.77.own_ref.refs_0_.refs_7_), channel_id=1, source_target_pairs={{0,1},{1,0},{2,3},{3,2},{4,5},{5,4},{6,7},{7,6},{8,9},{9,8},{10,11... | collective-permute-start | bytes 737288 | tf_op jit(solution)/shard_map/ppermute | solution.py:51
  73.8 5.0 %collective-permute-start.22 = (bf16[192,640]{1,0:T(8,128)(2,1)S(1)}, bf16[192,640]{1,0:T(8,128)(2,1)S(1)}, u32[]{:S(2)}, u32[]{:S(2)}) collective-permute-start(bf16[192,640]{1,0:T(8,128)(2,1)S(1)} %collective-permute-done.21.refs_6_), channel_id=1, source_target_pairs={{0,1},{1,0},{2,3},{3,2},{4,5},{5,4},{6,7},{7,6},{8,9},{9,8},{10,11... | collective-permute-start | bytes 737288 | tf_op jit(solution)/shard_map/ppermute | solution.py:51
  78.3 1.5 collective-permute-start.20
  78.4 1.7 collective-permute-start.18
  88.4 26.6 %collective-permute-start.24 = (bf16[208,512]{1,0:T(8,128)(2,1)}, bf16[208,512]{1,0:T(8,128)(2,1)S(1)}, u32[]{:S(2)}, u32[]{:S(2)}) collective-permute-start(bf16[208,512]{1,0:T(8,128)(2,1)} %copy-done.15), channel_id=1, source_target_pairs={{0,16},{8,24},{16,0},{24,8},{1,17},{9,25},{17,1},{25,9},{2,18},{10... | collective-permute-start | bytes 638984 | tf_op jit(solution)/shard_map/ppermute | solution.py:51
  93.9 23.1 %collective-permute-start.23 = (bf16[208,512]{1,0:T(8,128)(2,1)}, bf16[208,512]{1,0:T(8,128)(2,1)S(1)}, u32[]{:S(2)}, u32[]{:S(2)}) collective-permute-start(bf16[208,512]{1,0:T(8,128)(2,1)} %copy-done.15), channel_id=1, source_target_pairs={{0,8},{8,0},{16,24},{24,16},{1,9},{9,1},{17,25},{25,17},{2,10},{10... | collective-permute-start | bytes 638984 | tf_op jit(solution)/shard_map/ppermute | solution.py:51
  115.0 7.2 %collective-permute-start.25 = (bf16[208,512]{1,0:T(8,128)(2,1)S(1)}, bf16[208,512]{1,0:T(8,128)(2,1)}, u32[]{:S(2)}, u32[]{:S(2)}) collective-permute-start(bf16[208,512]{1,0:T(8,128)(2,1)S(1)} %collective-permute-done.24.refs_2_), channel_id=1, source_target_pairs={{0,8},{8,0},{16,24},{24,16},{1,9},{9,1},{17,25},{25,17},{2,10},{10... | collective-permute-start | bytes 638984 | tf_op jit(solution)/shard_map/ppermute | solution.py:51
  116.7 57.5 %collective-permute-start.34 = (bf16[4,4,192,512]{3,2,1,0:T(8,128)(2,1)}, bf16[4,4,192,512]{3,2,1,0:T(8,128)(2,1)S(1)}, u32[]{:S(2)}, u32[]{:S(2)}) collective-permute-start(bf16[4,4,192,512]{3,2,1,0:T(8,128)(2,1)} %bitcast.35), channel_id=1, source_target_pairs={{0,1},{1,0},{2,3},{3,2},{4,5},{5,4},{6,7},{7,6},{8,9},{9,8},{10,11... | collective-permute-start | bytes 9437192 | tf_op jit(solution)/shard_map/ppermute | solution.py:51
  124.1 26.2 %copy-start.3 = (f32[192,128]{1,0:T(8,128)S(1)}, f32[192,128]{1,0:T(8,128)}, u32[]{:S(2)}) copy-start(f32[192,128]{1,0:T(8,128)} %copy-done.2) | copy-start | bytes 294916
  124.1 26.2 %copy-start.9 = (f32[8,640]{1,0:T(8,128)S(1)}, f32[8,640]{1,0:T(8,128)}, u32[]{:S(2)}) copy-start(f32[8,640]{1,0:T(8,128)} %copy-done.8) | copy-start | bytes 61444
  131.5 2.7 collective-permute-start.26
  134.4 9.3 %collective-permute-start.27 = (bf16[208,640]{1,0:T(8,128)(2,1)S(1)}, bf16[208,640]{1,0:T(8,128)(2,1)S(1)}, u32[]{:S(2)}, u32[]{:S(2)}) collective-permute-start(bf16[208,640]{1,0:T(8,128)(2,1)S(1)} %get-tuple-element.84), channel_id=1, source_target_pairs={{0,2},{1,3},{2,0},{3,1},{4,6},{5,7},{6,4},{7,5},{8,10},{9,11},{10,... | collective-permute-start | bytes 798728 | tf_op jit(solution)/shard_map/ppermute | solution.py:51
  136.0 13.9 %collective-permute-start.28 = (bf16[208,640]{1,0:T(8,128)(2,1)S(1)}, bf16[208,640]{1,0:T(8,128)(2,1)S(1)}, u32[]{:S(2)}, u32[]{:S(2)}) collective-permute-start(bf16[208,640]{1,0:T(8,128)(2,1)S(1)} %get-tuple-element.85), channel_id=1, source_target_pairs={{0,4},{1,5},{2,6},{3,7},{4,0},{5,1},{6,2},{7,3},{8,12},{9,13},{10,... | collective-permute-start | bytes 798728 | tf_op jit(solution)/shard_map/ppermute | solution.py:51
  136.1 14.2 %collective-permute-start.29 = (bf16[208,640]{1,0:T(8,128)(2,1)S(1)}, bf16[208,640]{1,0:T(8,128)(2,1)S(1)}, u32[]{:S(2)}, u32[]{:S(2)}) collective-permute-start(bf16[208,640]{1,0:T(8,128)(2,1)S(1)} %get-tuple-element.86), channel_id=1, source_target_pairs={{0,6},{1,7},{2,4},{3,5},{4,2},{5,3},{6,0},{7,1},{8,14},{9,15},{10,... | collective-permute-start | bytes 798728 | tf_op jit(solution)/shard_map/ppermute | solution.py:51
  150.3 24.0 %copy-start.7 = (f32[8,640]{1,0:T(8,128)S(1)}, f32[8,640]{1,0:T(8,128)}, u32[]{:S(2)}) copy-start(f32[8,640]{1,0:T(8,128)} %copy-done.6) | copy-start | bytes 61444
  155.6 2.7 collective-permute-start.30
  158.5 9.3 %collective-permute-start.31 = (bf16[208,640]{1,0:T(8,128)(2,1)S(1)}, bf16[208,640]{1,0:T(8,128)(2,1)S(1)}, u32[]{:S(2)}, u32[]{:S(2)}) collective-permute-start(bf16[208,640]{1,0:T(8,128)(2,1)S(1)} %get-tuple-element.94), channel_id=1, source_target_pairs={{0,2},{1,3},{2,0},{3,1},{4,6},{5,7},{6,4},{7,5},{8,10},{9,11},{10,... | collective-permute-start | bytes 798728 | tf_op jit(solution)/shard_map/ppermute | solution.py:51
  159.3 15.0 %collective-permute-start.32 = (bf16[208,640]{1,0:T(8,128)(2,1)S(1)}, bf16[208,640]{1,0:T(8,128)(2,1)S(1)}, u32[]{:S(2)}, u32[]{:S(2)}) collective-permute-start(bf16[208,640]{1,0:T(8,128)(2,1)S(1)} %get-tuple-element.95), channel_id=1, source_target_pairs={{0,4},{1,5},{2,6},{3,7},{4,0},{5,1},{6,2},{7,3},{8,12},{9,13},{10,... | collective-permute-start | bytes 798728 | tf_op jit(solution)/shard_map/ppermute | solution.py:51
  162.1 12.1 %collective-permute-start.33 = (bf16[208,640]{1,0:T(8,128)(2,1)S(1)}, bf16[208,640]{1,0:T(8,128)(2,1)S(1)}, u32[]{:S(2)}, u32[]{:S(2)}) collective-permute-start(bf16[208,640]{1,0:T(8,128)(2,1)S(1)} %get-tuple-element.96), channel_id=1, source_target_pairs={{0,6},{1,7},{2,4},{3,5},{4,2},{5,3},{6,0},{7,1},{8,14},{9,15},{10,... | collective-permute-start | bytes 798728 | tf_op jit(solution)/shard_map/ppermute | solution.py:51
  174.3 49.7 %copy-start.5 = (bf16[192,512]{1,0:T(8,128)(2,1)S(1)}, bf16[192,512]{1,0:T(8,128)(2,1)}, u32[]{:S(2)}) copy-start(bf16[192,512]{1,0:T(8,128)(2,1)} %refs_5_.1) | copy-start | bytes 589828
  174.3 49.7 %copy-start.20 = (f32[8,640]{1,0:T(8,128)S(1)}, f32[8,640]{1,0:T(8,128)}, u32[]{:S(2)}) copy-start(f32[8,640]{1,0:T(8,128)} %copy-done.19) | copy-start | bytes 61444
  179.2 23.4 %collective-permute-start.35 = (bf16[784,512]{1,0:T(8,128)(2,1)S(1)}, bf16[784,512]{1,0:T(8,128)(2,1)S(1)}, u32[]{:S(2)}, u32[]{:S(2)}) collective-permute-start(bf16[784,512]{1,0:T(8,128)(2,1)S(1)} %get-tuple-element.105.send_ref), channel_id=1, source_target_pairs={{0,1},{1,0},{2,3},{3,2},{4,5},{5,4},{6,7},{7,6},{8,9},{9,8},{10,11... | collective-permute-start | bytes 2408456 | tf_op jit(solution)/shard_map/ppermute | solution.py:51
  179.3 20.7 %collective-permute-start.40 = (bf16[192,512]{1,0:T(8,128)(2,1)S(1)}, bf16[192,512]{1,0:T(8,128)(2,1)S(1)}, u32[]{:S(2)}, u32[]{:S(2)}) collective-permute-start(bf16[192,512]{1,0:T(8,128)(2,1)S(1)} %get-tuple-element.118.refs_0_), channel_id=1, source_target_pairs={{0,16},{8,24},{16,0},{24,8},{1,17},{9,25},{17,1},{25,9},{2,18},{10... | collective-permute-start | bytes 589832 | tf_op jit(solution)/shard_map/ppermute | solution.py:51
  180.0 23.5 %collective-permute-start.39 = (bf16[192,512]{1,0:T(8,128)(2,1)S(1)}, bf16[192,512]{1,0:T(8,128)(2,1)S(1)}, u32[]{:S(2)}, u32[]{:S(2)}) collective-permute-start(bf16[192,512]{1,0:T(8,128)(2,1)S(1)} %get-tuple-element.118.refs_0_), channel_id=1, source_target_pairs={{0,8},{8,0},{16,24},{24,16},{1,9},{9,1},{17,25},{25,17},{2,10},{10... | collective-permute-start | bytes 589832 | tf_op jit(solution)/shard_map/ppermute | solution.py:51
  200.0 20.1 %collective-permute-start.41 = (bf16[192,512]{1,0:T(8,128)(2,1)S(1)}, bf16[192,512]{1,0:T(8,128)(2,1)S(1)}, u32[]{:S(2)}, u32[]{:S(2)}) collective-permute-start(bf16[192,512]{1,0:T(8,128)(2,1)S(1)} %collective-permute-done.40.refs_2_), channel_id=1, source_target_pairs={{0,8},{8,0},{16,24},{24,16},{1,9},{9,1},{17,25},{25,17},{2,10},{10... | collective-permute-start | bytes 589832 | tf_op jit(solution)/shard_map/ppermute | solution.py:51
  200.0 21.9 %collective-permute-start.43 = (bf16[192,512]{1,0:T(8,128)(2,1)S(1)}, bf16[192,512]{1,0:T(8,128)(2,1)S(1)}, u32[]{:S(2)}, u32[]{:S(2)}) collective-permute-start(bf16[192,512]{1,0:T(8,128)(2,1)S(1)} %get-tuple-element.124.refs_0_), channel_id=1, source_target_pairs={{0,16},{8,24},{16,0},{24,8},{1,17},{9,25},{17,1},{25,9},{2,18},{10... | collective-permute-start | bytes 589832 | tf_op jit(solution)/shard_map/ppermute | solution.py:51
  202.8 19.5 %collective-permute-start.36 = (bf16[208,512]{1,0:T(8,128)(2,1)S(1)}, bf16[208,512]{1,0:T(8,128)(2,1)S(1)}, u32[]{:S(2)}, u32[]{:S(2)}) collective-permute-start(bf16[208,512]{1,0:T(8,128)(2,1)S(1)} %get-tuple-element.107), channel_id=1, source_target_pairs={{0,2},{1,3},{2,0},{3,1},{4,6},{5,7},{6,4},{7,5},{8,10},{9,11},{10,... | collective-permute-start | bytes 638984 | tf_op jit(solution)/shard_map/ppermute | solution.py:51
  203.2 20.7 %collective-permute-start.37 = (bf16[208,512]{1,0:T(8,128)(2,1)S(1)}, bf16[208,512]{1,0:T(8,128)(2,1)S(1)}, u32[]{:S(2)}, u32[]{:S(2)}) collective-permute-start(bf16[208,512]{1,0:T(8,128)(2,1)S(1)} %get-tuple-element.108), channel_id=1, source_target_pairs={{0,4},{1,5},{2,6},{3,7},{4,0},{5,1},{6,2},{7,3},{8,12},{9,13},{10,... | collective-permute-start | bytes 638984 | tf_op jit(solution)/shard_map/ppermute | solution.py:51
  203.5 20.5 %collective-permute-start.38 = (bf16[208,512]{1,0:T(8,128)(2,1)S(1)}, bf16[208,512]{1,0:T(8,128)(2,1)S(1)}, u32[]{:S(2)}, u32[]{:S(2)}) collective-permute-start(bf16[208,512]{1,0:T(8,128)(2,1)S(1)} %get-tuple-element.109), channel_id=1, source_target_pairs={{0,6},{1,7},{2,4},{3,5},{4,2},{5,3},{6,0},{7,1},{8,14},{9,15},{10,... | collective-permute-start | bytes 638984 | tf_op jit(solution)/shard_map/ppermute | solution.py:51
  220.1 15.9 %collective-permute-start.49 = (bf16[192,512]{1,0:T(8,128)(2,1)S(1)}, bf16[192,512]{1,0:T(8,128)(2,1)S(1)}, u32[]{:S(2)}, u32[]{:S(2)}) collective-permute-start(bf16[192,512]{1,0:T(8,128)(2,1)S(1)} %get-tuple-element.132.refs_0_), channel_id=1, source_target_pairs={{0,16},{8,24},{16,0},{24,8},{1,17},{9,25},{17,1},{25,9},{2,18},{10... | collective-permute-start | bytes 589832 | tf_op jit(solution)/shard_map/ppermute | solution.py:51
  221.9 14.1 %collective-permute-start.42 = (bf16[192,512]{1,0:T(8,128)(2,1)S(1)}, bf16[192,512]{1,0:T(8,128)(2,1)S(1)}, u32[]{:S(2)}, u32[]{:S(2)}) collective-permute-start(bf16[192,512]{1,0:T(8,128)(2,1)S(1)} %get-tuple-element.124.refs_0_), channel_id=1, source_target_pairs={{0,8},{8,0},{16,24},{24,16},{1,9},{9,1},{17,25},{25,17},{2,10},{10... | collective-permute-start | bytes 589832 | tf_op jit(solution)/shard_map/ppermute | solution.py:51
  222.3 19.8 %collective-permute-start.44 = (bf16[192,512]{1,0:T(8,128)(2,1)S(1)}, bf16[192,512]{1,0:T(8,128)(2,1)S(1)}, u32[]{:S(2)}, u32[]{:S(2)}) collective-permute-start(bf16[192,512]{1,0:T(8,128)(2,1)S(1)} %collective-permute-done.43.refs_2_), channel_id=1, source_target_pairs={{0,8},{8,0},{16,24},{24,16},{1,9},{9,1},{17,25},{25,17},{2,10},{10... | collective-permute-start | bytes 589832 | tf_op jit(solution)/shard_map/ppermute | solution.py:51
  225.8 12.1 %collective-permute-start.46 = (f32[8,192]{1,0:T(8,128)S(1)}, f32[8,192]{1,0:T(8,128)S(1)}, u32[]{:S(2)}, u32[]{:S(2)}) collective-permute-start(f32[8,192]{1,0:T(8,128)S(1)} %select_maximum_fusion), channel_id=1, source_target_pairs={{0,16},{8,24},{16,0},{24,8},{1,17},{9,25},{17,1},{25,9},{2,18},{10... | collective-permute-start | bytes 18440 | tf_op jit(solution)/shard_map/ppermute | solution.py:51
  227.0 24.1 %collective-permute-start.48 = (bf16[192,512]{1,0:T(8,128)(2,1)S(1)}, bf16[192,512]{1,0:T(8,128)(2,1)S(1)}, u32[]{:S(2)}, u32[]{:S(2)}) collective-permute-start(bf16[192,512]{1,0:T(8,128)(2,1)S(1)} %get-tuple-element.132.refs_0_), channel_id=1, source_target_pairs={{0,8},{8,0},{16,24},{24,16},{1,9},{9,1},{17,25},{25,17},{2,10},{10... | collective-permute-start | bytes 589832 | tf_op jit(solution)/shard_map/ppermute | solution.py:51
  235.9 15.2 %collective-permute-start.50 = (bf16[192,512]{1,0:T(8,128)(2,1)S(1)}, bf16[192,512]{1,0:T(8,128)(2,1)S(1)}, u32[]{:S(2)}, u32[]{:S(2)}) collective-permute-start(bf16[192,512]{1,0:T(8,128)(2,1)S(1)} %collective-permute-done.49.refs_2_), channel_id=1, source_target_pairs={{0,8},{8,0},{16,24},{24,16},{1,9},{9,1},{17,25},{25,17},{2,10},{10... | collective-permute-start | bytes 589832 | tf_op jit(solution)/shard_map/ppermute | solution.py:51
  236.0 15.1 %collective-permute-start.45 = (f32[8,192]{1,0:T(8,128)S(1)}, f32[8,192]{1,0:T(8,128)S(1)}, u32[]{:S(2)}, u32[]{:S(2)}) collective-permute-start(f32[8,192]{1,0:T(8,128)S(1)} %select_maximum_fusion), channel_id=1, source_target_pairs={{0,8},{8,0},{16,24},{24,16},{1,9},{9,1},{17,25},{25,17},{2,10},{10... | collective-permute-start | bytes 18440 | tf_op jit(solution)/shard_map/ppermute | solution.py:51
  238.0 13.1 %collective-permute-start.47 = (f32[8,192]{1,0:T(8,128)S(1)}, f32[8,192]{1,0:T(8,128)S(1)}, u32[]{:S(2)}, u32[]{:S(2)}) collective-permute-start(f32[8,192]{1,0:T(8,128)S(1)} %collective-permute-done.46), channel_id=1, source_target_pairs={{0,8},{8,0},{16,24},{24,16},{1,9},{9,1},{17,25},{25,17},{2,10},{10... | collective-permute-start | bytes 18440 | tf_op jit(solution)/shard_map/ppermute | solution.py:51
  254.7 5.7 %collective-permute-start.52 = (bf16[4,4,192,512]{3,2,1,0:T(8,128)(2,1)S(1)}, bf16[4,4,192,512]{3,2,1,0:T(8,128)(2,1)S(1)}, u32[]{:S(2)}, u32[]{:S(2)}) collective-permute-start(bf16[4,4,192,512]{3,2,1,0:T(8,128)(2,1)S(1)} %get-tuple-element.138.refs_4_), channel_id=1, source_target_pairs={{0,1},{1,0},{2,3},{3,2},{4,5},{5,4},{6,7},{7,6},{8,9},{9,8},{10,11... | collective-permute-start | bytes 9437192 | tf_op jit(solution)/shard_map/ppermute | solution.py:51
  254.8 16.4 %collective-permute-start.51 = (bf16[4,4,192,512]{3,2,1,0:T(8,128)(2,1)S(1)}, bf16[4,4,192,512]{3,2,1,0:T(8,128)(2,1)S(1)}, u32[]{:S(2)}, u32[]{:S(2)}) collective-permute-start(bf16[4,4,192,512]{3,2,1,0:T(8,128)(2,1)S(1)} %get-tuple-element.139.refs_4_), channel_id=1, source_target_pairs={{0,1},{1,0},{2,3},{3,2},{4,5},{5,4},{6,7},{7,6},{8,9},{9,8},{10,11... | collective-permute-start | bytes 9437192 | tf_op jit(solution)/shard_map/ppermute | solution.py:51
  (17 other events, 126.6 us)
Sparse Core Ops, SparseCore 0:
  41.8 74.8 all-gather.4
  119.5 114.9 all-gather.6
